TPU v7x, 32 devices: a whole 2x2x4 slice. The times are simulated.
32 devices in a mesh: ctx: 16 (over z, y, core), head: 2 (over x).
Axes of the slice: x: 2, y: 2, z: 4, core: 2. Of those that a mesh axis runs over, the one named last changes fastest.
Arguments:
- residual: bfloat16 [4096, 1024], P(('ctx', 'head')), may hold values from -6 to 6
- input_gain: float32 [2, 1024], replicated, may hold values from 0.25 to 1.75
- project_in: bfloat16 [2, 3, 1024, 1024], P(None, None, None, 'head'), may hold values from -0.1875 to 0.1875
- output_gain: float32 [2, 1024], P(None, 'head'), may hold values from 0.25 to 1.75
- project_out: bfloat16 [2, 1024, 1024], P(None, 'head'), may hold values from -0.1875 to 0.1875
Outputs:
- result_rows: bfloat16 [4096, 1024], P(('ctx', 'head'))
All inputs are finite; a program needn't handle non-finite values.
Results may differ from a plain program's by a relative error of at most 0.012.
Values may be sent and summed in bfloat16 or wider, within the bound.
No kernel may reach another device: no remote copies, remote signals or barrier semaphores. Data moves between devices by JAX's collectives and lax.ppermute only.
A program may use at most 192 MiB of HBM per device.

v0:
```python
import functools

import jax
import jax.numpy as jnp
from jax import lax
from jax.experimental import pallas as pl
from jax.experimental.pallas import tpu as pltpu
from jax.sharding import PartitionSpec as P

HD = 64
LAYERS = 2
EPSILON = 1e-06


def rms_scale(values, gain):
    mean_square = jnp.mean(values * values, axis=-1, keepdims=True)
    return values * lax.rsqrt(mean_square + EPSILON) * gain


def project_kernel(place, row_refs, gain_ref, weight_ref, out_ref, normed):
    rows = row_refs[0].shape[0]

    @pl.when(pl.program_id(0) == 0)
    def _():
        gain = gain_ref[...]
        for which, ref in enumerate(row_refs):
            scaled = rms_scale(ref[...].astype(jnp.float32), gain).astype(jnp.bfloat16)
            if len(row_refs) == 1:
                normed[...] = scaled
            else:
                start = place() if which == 0 else 1 - place()
                normed[pl.ds(pl.multiple_of(start * rows, rows), rows), :] = scaled

    field = jnp.dot(normed[...], weight_ref[...], preferred_element_type=jnp.float32)
    flipped = field.T.astype(jnp.bfloat16)
    for head in range(out_ref.shape[0]):
        out_ref[head] = flipped[head * HD : (head + 1) * HD]


def project(layer, rows, gain, project_in, place):
    width, columns = project_in.shape[2:]
    tokens = sum(r.shape[0] for r in rows)
    heads = columns // HD

    def kernel(*refs):
        project_kernel(place, refs[: len(rows)], *refs[len(rows) :])

    return pl.pallas_call(
        kernel,
        grid=(3,),
        in_specs=[pl.BlockSpec(r.shape, lambda m: (0, 0)) for r in rows]
        + [
            pl.BlockSpec((None, 1, width), lambda m: (layer, 0, 0)),
            pl.BlockSpec((None, None, width, columns), lambda m: (layer, m, 0, 0)),
        ],
        out_specs=pl.BlockSpec((heads, HD, tokens), lambda m: (0, m, 0)),
        out_shape=jax.ShapeDtypeStruct((heads, 3 * HD, tokens), jnp.bfloat16),
        scratch_shapes=[pltpu.VMEM((tokens, width), jnp.bfloat16)],
        compiler_params=pltpu.CompilerParams(vmem_limit_bytes=32 * 2**20),
        cost_estimate=pl.CostEstimate(
            flops=6 * tokens * width * columns, bytes_accessed=6 * width * columns, transcendentals=0
        ),
    )(*rows, gain, project_in)


def attention_kernel(shift_ref, own_ref, others_ref, gain_ref, out_ref, values):
    groups, _, tokens = own_ref.shape
    split = out_ref.shape[0]
    own_slot = others_ref.shape[0] if others_ref.shape[0] == 1 else None
    sources = others_ref.shape[0] + (own_slot is not None)

    def block(source, group, part):
        if source == own_slot:
            return own_ref[group, (1 + part) * HD : (2 + part) * HD, :]
        return others_ref[source, group, part * HD : (part + 1) * HD, :]

    for group in range(groups):
        for source in range(sources):
            values[group, source * tokens : (source + 1) * tokens, :] = block(source, group, 1).T
    offset = lax.broadcasted_iota(jnp.int32, (tokens, tokens), 1) - lax.broadcasted_iota(
        jnp.int32, (tokens, tokens), 0
    )
    gain = gain_ref[...]
    for group in range(groups):
        query = own_ref[group, :HD, :].T
        total = jnp.zeros((tokens, HD), jnp.float32)
        for past in range(group + 1):
            for source in range(sources):
                scores = jnp.dot(query, block(source, past, 0), preferred_element_type=jnp.float32)
                weights = scores * scores
                if past == group:
                    weights = jnp.where(offset <= shift_ref[source], weights, 0.0)
                total += jnp.dot(
                    weights.astype(jnp.bfloat16),
                    values[past, source * tokens : (source + 1) * tokens, :],
                    preferred_element_type=jnp.float32,
                )
        flipped = rms_scale(total, gain).T.astype(jnp.bfloat16)
        part = tokens // split
        for piece in range(split):
            out_ref[piece, group] = flipped[:, piece * part : (piece + 1) * part]


def attention(shift, own, others, gain, split):
    groups, _, tokens = own.shape
    sources = shift.shape[0]
    pairs = groups * (groups + 1) // 2 * sources * tokens * tokens
    return pl.pallas_call(
        attention_kernel,
        in_specs=[pl.BlockSpec(memory_space=pltpu.SMEM)] + [pl.BlockSpec(memory_space=pltpu.VMEM)] * 3,
        out_specs=pl.BlockSpec(memory_space=pltpu.VMEM),
        out_shape=jax.ShapeDtypeStruct((split, groups, HD, tokens // split), jnp.bfloat16),
        scratch_shapes=[pltpu.VMEM((groups, sources * tokens, HD), jnp.bfloat16)],
        compiler_params=pltpu.CompilerParams(vmem_limit_bytes=48 * 2**20),
        cost_estimate=pl.CostEstimate(flops=4 * pairs * HD, bytes_accessed=2**21, transcendentals=0),
    )(shift, own, others, gain)


def mix_kernel(place, mixed_ref, residual_ref, weight_refs, out_ref):
    depth = weight_refs[0].shape[0]
    total = residual_ref[...].astype(jnp.float32)
    for which, ref in enumerate(weight_refs):
        if len(weight_refs) == 1:
            mixed = mixed_ref[...]
        else:
            start = place() if which == 0 else 1 - place()
            mixed = mixed_ref[pl.ds(pl.multiple_of(start * depth, depth), depth), :]
        total += jnp.dot(mixed.T, ref[...], preferred_element_type=jnp.float32)
    out_ref[...] = total.astype(jnp.bfloat16)


def mix(mixed, residual, weights, place):
    depth, rows = mixed.shape
    width = residual.shape[1]
    steps = 4 if width % 1024 == 0 else 1

    def kernel(mixed_ref, residual_ref, *refs):
        mix_kernel(place, mixed_ref, residual_ref, refs[:-1], refs[-1])

    return pl.pallas_call(
        kernel,
        grid=(steps,),
        in_specs=[
            pl.BlockSpec((depth, rows), lambda n: (0, 0)),
            pl.BlockSpec((rows, width // steps), lambda n: (0, n)),
        ]
        + [pl.BlockSpec((w.shape[0], width // steps), lambda n: (0, n)) for w in weights],
        out_specs=pl.BlockSpec((rows, width // steps), lambda n: (0, n)),
        out_shape=jax.ShapeDtypeStruct(residual.shape, jnp.bfloat16),
        compiler_params=pltpu.CompilerParams(vmem_limit_bytes=32 * 2**20),
        cost_estimate=pl.CostEstimate(
            flops=2 * rows * width * depth, bytes_accessed=2 * width * depth, transcendentals=0
        ),
    )(mixed, residual, *weights)


def per_device(residual, input_gain, project_in, output_gain, project_out):
    shards, split = lax.axis_size("ctx"), lax.axis_size("head")
    local_heads = output_gain.shape[1] // HD
    replicas = shards // local_heads
    index = lax.axis_index("ctx")
    replica = index % replicas
    paired = split == 2
    swap = [(0, 1), (1, 0)]

    def place():
        return lax.axis_index("head")

    shard_groups = [[k * replicas + r for k in range(local_heads)] for r in range(replicas)]
    row_groups = [[c * split + x for x in range(split) for c in group] for group in shard_groups]
    head_groups = [[k * replicas + r for r in range(replicas)] for k in range(local_heads)]

    def other_half(weights):
        depth = weights.shape[0]
        near = index % 2
        half = lax.dynamic_slice_in_dim(weights, near * (depth // 2), depth // 2, axis=0)
        mine = lax.ppermute(half, "head", swap)
        theirs = lax.ppermute(mine, "ctx", [(c, c ^ 1) for c in range(shards)])
        return lax.cond(
            near == 0,
            lambda: jnp.concatenate([mine, theirs], axis=0),
            lambda: jnp.concatenate([theirs, mine], axis=0),
        )

    gains_in = input_gain[:, None, :]
    for layer in range(LAYERS):
        if paired:
            rows = [residual, lax.ppermute(residual, "head", swap)]
            held, _ = lax.optimization_barrier((project_out[layer], rows[1]))
            weights_out = [project_out[layer], other_half(held)]
        else:
            rows = [lax.all_gather(residual, "head", axis=0, tiled=True)]
            weights_out = [lax.all_gather(project_out[layer], "head", axis=0, tiled=True)]
        fields = project(layer, rows, gains_in, project_in, place)
        own = lax.all_to_all(fields, "ctx", 0, 0, axis_index_groups=shard_groups, tiled=True)
        tokens = own.shape[2]
        if replicas == 2:
            others = lax.ppermute(own[None, :, HD:], "ctx", [(c, c ^ 1) for c in range(shards)])
            shift = jnp.stack([2 * replica - 1, 0 * replica]) * tokens
        else:
            others = lax.all_gather(own[:, HD:], "ctx", axis=0, axis_index_groups=head_groups)
            shift = (replica - jnp.arange(replicas)) * tokens
        gain = lax.dynamic_slice_in_dim(output_gain[layer], index // replicas * HD, HD)[None]
        heads = attention(shift.astype(jnp.int32), own, others, gain, split)
        heads = heads.reshape(split * local_heads, HD, tokens // split)
        mixed = lax.all_to_all(heads, ("ctx", "head"), 0, 0, axis_index_groups=row_groups, tiled=True)
        mixed = mixed.reshape(split * local_heads * HD, tokens // split)
        residual = mix(mixed, residual, weights_out, place)
    return residual


def solution(mesh):
    return jax.shard_map(
        per_device,
        mesh=mesh,
        in_specs=(
            P(("ctx", "head"), None),
            P(),
            P(None, None, None, "head"),
            P(None, "head"),
            P(None, "head", None),
        ),
        out_specs=P(("ctx", "head"), None),
        check_vma=False,
    )
```

profile of v0, /device:TPU:0, one launch (start us, length us, event | category | flops | bytes accessed | tf_op | source)
XLA Modules:
  0.0 131.2 jit_solution(5072540100063814754)
XLA Ops:
  0.0 2.9 %collective-permute-start = (bf16[128,1024]{1,0:T(8,128)(2,1)}, bf16[128,1024]{1,0:T(8,128)(2,1)S(1)}, u32[]{:S(2)}, u32[]{:S(2)}) collective-permute-start(bf16[128,1024]{1,0:T(8,128)(2,1)} %residual_ref.1), channel_id=1, source_target_pairs={{0,1},{1,0},{2,3},{3,2},{4,5},{5,4},{6,7},{7,6},{8,9},{9,8},{10,11... | collective-permute-start | bytes 786440 | tf_op jit(solution)/shard_map/ppermute | solution.py:188
  3.6 5.8 %collective-permute-done.refs_1_ = bf16[128,1024]{1,0:T(8,128)(2,1)S(1)} collective-permute-done((bf16[128,1024]{1,0:T(8,128)(2,1)}, bf16[128,1024]{1,0:T(8,128)(2,1)S(1)}, u32[]{:S(2)}, u32[]{:S(2)}) %collective-permute-start) | collective-permute-done | bytes 262176 | tf_op jit(solution)/shard_map/ppermute | solution.py:188
  9.5 2.8 %copy-done = bf16[2,3,1024,512]{3,2,1,0:T(8,128)(2,1)S(1)} copy-done((bf16[2,3,1024,512]{3,2,1,0:T(8,128)(2,1)S(1)}, bf16[2,3,1024,512]{3,2,1,0:T(8,128)(2,1)}, u32[]{:S(2)}) %copy-start) | copy-done | bytes 6291480
  13.2 2.7 %shard_map.55 = bf16[8,192,256]{2,1,0:T(8,128)(2,1)} custom-call(bf16[128,1024]{1,0:T(8,128)(2,1)S(1)} %copy-done.2, bf16[128,1024]{1,0:T(8,128)(2,1)S(1)} %collective-permute-done.refs_1_, f32[2,1,1024]{2,1,0:T(1,128)S(1)} %broadcast_in_dim.11.refs_2_, bf16[2,3,1024,512]{3,2,1,0:T(8,128)(2,1)S(1)} %copy-done), custom_call_target="tpu_custom_call" | custom-call | flops 805306368 | bytes 3145728 | tf_op jit(solution)/shard_map/pallas_call | solution.py:48
  15.9 6.1 %all-to-all-start = ((bf16[8,192,256]{2,1,0:T(8,128)(2,1)}), bf16[8,192,256]{2,1,0:T(8,128)(2,1)S(1)}, u32[]{:S(2)}, u32[]{:S(2)}) async-start(bf16[8,192,256]{2,1,0:T(8,128)(2,1)} %shard_map.55), calls=%async_computation | async-start | bytes 1572864 | tf_op jit(solution)/shard_map/all_to_all | solution.py:195
  22.0 1.7 %slice_bitcast_fusion = (bf16[512,1024]{1,0:T(8,128)(2,1)S(1)}, bf16[512,1024]{1,0:T(8,128)(2,1)S(1)}) fusion(bf16[2,512,1024]{2,1,0:T(8,128)(2,1)} %param.13), kind=kLoop, calls=%fused_computation.4 | loop fusion | bytes 4194304 | tf_op jit(solution)/shard_map/squeeze | solution.py:190
  24.6 1.5 %collective-permute-start.2 = (bf16[256,1024]{1,0:T(8,128)(2,1)}, bf16[256,1024]{1,0:T(8,128)(2,1)}, u32[]{:S(2)}, u32[]{:S(2)}) collective-permute-start(bf16[256,1024]{1,0:T(8,128)(2,1)} %constant_dynamic-slice_fusion.2), channel_id=1, source_target_pairs={{0,1},{1,0},{2,3},{3,2},{4,5},{5,4},{6,7},{7,6},{8,9},{9,8},{10,11... | collective-permute-start | bytes 1572872 | tf_op jit(solution)/shard_map/ppermute | solution.py:177
  26.0 15.3 %all-to-all-done.own_ref = bf16[8,192,256]{2,1,0:T(8,128)(2,1)S(1)} async-done(((bf16[8,192,256]{2,1,0:T(8,128)(2,1)}), bf16[8,192,256]{2,1,0:T(8,128)(2,1)S(1)}, u32[]{:S(2)}, u32[]{:S(2)}) %all-to-all-start) | async-done | bytes 786464 | tf_op jit(solution)/shard_map/all_to_all | solution.py:195
  44.3 7.8 %shard_map.56 = bf16[2,8,64,128]{3,2,1,0:T(8,128)(2,1)} custom-call(s32[2]{0:T(128)S(1)} %add_multiply_fusion.shift_ref, bf16[8,192,256]{2,1,0:T(8,128)(2,1)S(1)} %all-to-all-done.own_ref, bf16[1,8,128,256]{3,2,1,0:T(8,128)(2,1)S(1)} %collective-permute-done.1.others_ref, f32[1,64]{1,0:T(1,128)S(1)} %constant_dynamic-slice_fusion.3.gain_ref), custom_call_target="tpu_custom_call" | custom-call | flops 1207959552 | bytes 2097152 | tf_op jit(solution)/shard_map/pallas_call | solution.py:108
  52.2 4.6 %all-to-all-start.1 = ((bf16[16,64,128]{2,1,0:T(8,128)(2,1)}), bf16[16,64,128]{2,1,0:T(8,128)(2,1)S(1)}, u32[]{:S(2)}, u32[]{:S(2)}) async-start(bf16[16,64,128]{2,1,0:T(8,128)(2,1)} %bitcast.2), calls=%async_computation.1 | async-start | bytes 524288 | tf_op jit(solution)/shard_map/all_to_all | solution.py:206
  56.8 2.3 %conditional.2 = (bf16[512,1024]{1,0:T(8,128)(2,1)}) conditional(s32[]{:T(128)} %convert_element_type.4, (bf16[256,1024]{1,0:T(8,128)(2,1)}, bf16[256,1024]{1,0:T(8,128)(2,1)}) %tuple.20, (bf16[256,1024]{1,0:T(8,128)(2,1)}, bf16[256,1024]{1,0:T(8,128)(2,1)}) %tuple.21), branch_computations={%region_0.1_spmd, %region_1.2_spmd} | conditional | flops 2097152 | bytes 2097160 | solution.py:179
  56.8 2.3 %pad_maximum_fusion.1 = bf16[512,1024]{1,0:T(8,128)(2,1)} fusion(bf16[256,1024]{1,0:T(8,128)(2,1)} %get-tuple-element.30, bf16[256,1024]{1,0:T(8,128)(2,1)} %get-tuple-element.29), kind=kLoop, calls=%fused_computation.1 | loop fusion | flops 2097152 | bytes 2097152 | tf_op jit(solution)/shard_map/cond/branch_1_fun/concatenate | solution.py:181
  59.1 7.8 %all-to-all-done.1 = bf16[16,64,128]{2,1,0:T(8,128)(2,1)S(1)} async-done(((bf16[16,64,128]{2,1,0:T(8,128)(2,1)}), bf16[16,64,128]{2,1,0:T(8,128)(2,1)S(1)}, u32[]{:S(2)}, u32[]{:S(2)}) %all-to-all-start.1) | async-done | bytes 262176 | tf_op jit(solution)/shard_map/all_to_all | solution.py:206
  66.9 3.0 %shard_map.57.refs_0_.residual_ref = bf16[128,1024]{1,0:T(8,128)(2,1)S(1)} custom-call(bf16[1024,128]{1,0:T(8,128)(2,1)S(1)} %bitcast.13, bf16[128,1024]{1,0:T(8,128)(2,1)S(1)} %copy-done.3, bf16[512,1024]{1,0:T(8,128)(2,1)S(1)} %get-tuple-element.37.refs_0_, bf16[512,1024]{1,0:T(8,128)(2,1)} %get-tuple-element.43.refs_1_), custom_call_target="tpu_custom_call" | custom-call | flops 268435456 | bytes 2097152 | tf_op jit(solution)/shard_map/pallas_call | solution.py:140
  71.1 5.3 %collective-permute-done.4.refs_1_ = bf16[128,1024]{1,0:T(8,128)(2,1)S(1)} collective-permute-done((bf16[128,1024]{1,0:T(8,128)(2,1)S(1)}, bf16[128,1024]{1,0:T(8,128)(2,1)S(1)}, u32[]{:S(2)}, u32[]{:S(2)}) %collective-permute-start.4) | collective-permute-done | bytes 262176 | tf_op jit(solution)/shard_map/ppermute | solution.py:188
  76.3 2.8 %copy-done.1 = bf16[2,3,1024,512]{3,2,1,0:T(8,128)(2,1)S(1)} copy-done((bf16[2,3,1024,512]{3,2,1,0:T(8,128)(2,1)S(1)}, bf16[2,3,1024,512]{3,2,1,0:T(8,128)(2,1)}, u32[]{:S(2)}) %copy-start.1) | copy-done | bytes 6291480
  79.1 2.7 %shard_map.58 = bf16[8,192,256]{2,1,0:T(8,128)(2,1)} custom-call(bf16[128,1024]{1,0:T(8,128)(2,1)S(1)} %shard_map.57.refs_0_.residual_ref, bf16[128,1024]{1,0:T(8,128)(2,1)S(1)} %collective-permute-done.4.refs_1_, f32[2,1,1024]{2,1,0:T(1,128)S(1)} %broadcast_in_dim.11.refs_2_, bf16[2,3,1024,512]{3,2,1,0:T(8,128)(2,1)S(1)} %copy-done.1), custom_call_target="tpu_custom_call" | custom-call | flops 805306368 | bytes 3145728 | tf_op jit(solution)/shard_map/pallas_call | solution.py:48
  81.8 4.4 %all-to-all-start.2 = ((bf16[8,192,256]{2,1,0:T(8,128)(2,1)}), bf16[8,192,256]{2,1,0:T(8,128)(2,1)S(1)}, u32[]{:S(2)}, u32[]{:S(2)}) async-start(bf16[8,192,256]{2,1,0:T(8,128)(2,1)} %shard_map.58), calls=%async_computation.2 | async-start | bytes 1572864 | tf_op jit(solution)/shard_map/all_to_all | solution.py:195
  87.7 17.3 %all-to-all-done.2.own_ref = bf16[8,192,256]{2,1,0:T(8,128)(2,1)S(1)} async-done(((bf16[8,192,256]{2,1,0:T(8,128)(2,1)}), bf16[8,192,256]{2,1,0:T(8,128)(2,1)S(1)}, u32[]{:S(2)}, u32[]{:S(2)}) %all-to-all-start.2) | async-done | bytes 786464 | tf_op jit(solution)/shard_map/all_to_all | solution.py:195
  107.0 7.8 %shard_map.59 = bf16[2,8,64,128]{3,2,1,0:T(8,128)(2,1)} custom-call(s32[2]{0:T(128)S(1)} %add_multiply_fusion.shift_ref, bf16[8,192,256]{2,1,0:T(8,128)(2,1)S(1)} %all-to-all-done.2.own_ref, bf16[1,8,128,256]{3,2,1,0:T(8,128)(2,1)S(1)} %collective-permute-done.5.others_ref, f32[1,64]{1,0:T(1,128)S(1)} %constant_dynamic-slice_fusion.1.gain_ref), custom_call_target="tpu_custom_call" | custom-call | flops 1207959552 | bytes 2097152 | tf_op jit(solution)/shard_map/pallas_call | solution.py:108
  114.8 3.7 %all-to-all-start.3 = ((bf16[16,64,128]{2,1,0:T(8,128)(2,1)}), bf16[16,64,128]{2,1,0:T(8,128)(2,1)S(1)}, u32[]{:S(2)}, u32[]{:S(2)}) async-start(bf16[16,64,128]{2,1,0:T(8,128)(2,1)} %bitcast.6), calls=%async_computation.3 | async-start | bytes 524288 | tf_op jit(solution)/shard_map/all_to_all | solution.py:206
  118.5 2.1 %conditional.3 = (bf16[512,1024]{1,0:T(8,128)(2,1)S(1)}) conditional(s32[]{:T(128)} %convert_element_type.4, (bf16[256,1024]{1,0:T(8,128)(2,1)}, bf16[256,1024]{1,0:T(8,128)(2,1)S(1)}) %tuple.23, (bf16[256,1024]{1,0:T(8,128)(2,1)S(1)}, bf16[256,1024]{1,0:T(8,128)(2,1)}) %tuple.24), branch_computations={%region_2.3_spmd, %region_3.4_spmd} | conditional | flops 2097152 | bytes 4194340 | solution.py:179
  120.6 8.2 %all-to-all-done.3 = bf16[16,64,128]{2,1,0:T(8,128)(2,1)S(1)} async-done(((bf16[16,64,128]{2,1,0:T(8,128)(2,1)}), bf16[16,64,128]{2,1,0:T(8,128)(2,1)S(1)}, u32[]{:S(2)}, u32[]{:S(2)}) %all-to-all-start.3) | async-done | bytes 262176 | tf_op jit(solution)/shard_map/all_to_all | solution.py:206
  128.8 2.4 %shard_map.60 = bf16[128,1024]{1,0:T(8,128)(2,1)} custom-call(bf16[1024,128]{1,0:T(8,128)(2,1)S(1)} %bitcast.14, bf16[128,1024]{1,0:T(8,128)(2,1)S(1)} %shard_map.57.refs_0_.residual_ref, bf16[512,1024]{1,0:T(8,128)(2,1)S(1)} %get-tuple-element.38.refs_0_, bf16[512,1024]{1,0:T(8,128)(2,1)S(1)} %get-tuple-element.44.refs_1_), custom_call_target="tpu_custom_call" | custom-call | flops 268435456 | bytes 2097152 | tf_op jit(solution)/shard_map/pallas_call | solution.py:140
  (32 shorter events, 12.1 us)
Async XLA Ops:
  0.0 9.5 %collective-permute-start = (bf16[128,1024]{1,0:T(8,128)(2,1)}, bf16[128,1024]{1,0:T(8,128)(2,1)S(1)}, u32[]{:S(2)}, u32[]{:S(2)}) collective-permute-start(bf16[128,1024]{1,0:T(8,128)(2,1)} %residual_ref.1), channel_id=1, source_target_pairs={{0,1},{1,0},{2,3},{3,2},{4,5},{5,4},{6,7},{7,6},{8,9},{9,8},{10,11... | collective-permute-start | bytes 786440 | tf_op jit(solution)/shard_map/ppermute | solution.py:188
  9.5 2.8 %copy-start = (bf16[2,3,1024,512]{3,2,1,0:T(8,128)(2,1)S(1)}, bf16[2,3,1024,512]{3,2,1,0:T(8,128)(2,1)}, u32[]{:S(2)}) copy-start(bf16[2,3,1024,512]{3,2,1,0:T(8,128)(2,1)} %refs_3_.3) | copy-start | bytes 18874372
  12.2 0.9 copy-start.2
  15.9 25.5 %all-to-all-start = ((bf16[8,192,256]{2,1,0:T(8,128)(2,1)}), bf16[8,192,256]{2,1,0:T(8,128)(2,1)S(1)}, u32[]{:S(2)}, u32[]{:S(2)}) async-start(bf16[8,192,256]{2,1,0:T(8,128)(2,1)} %shard_map.55), calls=%async_computation | async-start | bytes 1572864 | tf_op jit(solution)/shard_map/all_to_all | solution.py:195
  23.7 18.5 %copy-start.6 = (f32[2,512]{1,0:T(2,128)S(1)}, f32[2,512]{1,0:T(2,128)}, u32[]{:S(2)}) copy-start(f32[2,512]{1,0:T(2,128)} %param.12) | copy-start | bytes 12292
  24.6 17.8 %collective-permute-start.2 = (bf16[256,1024]{1,0:T(8,128)(2,1)}, bf16[256,1024]{1,0:T(8,128)(2,1)}, u32[]{:S(2)}, u32[]{:S(2)}) collective-permute-start(bf16[256,1024]{1,0:T(8,128)(2,1)} %constant_dynamic-slice_fusion.2), channel_id=1, source_target_pairs={{0,1},{1,0},{2,3},{3,2},{4,5},{5,4},{6,7},{7,6},{8,9},{9,8},{10,11... | collective-permute-start | bytes 1572872 | tf_op jit(solution)/shard_map/ppermute | solution.py:177
  42.2 2.1 %collective-permute-start.1 = (bf16[1,8,128,256]{3,2,1,0:T(8,128)(2,1)}, bf16[1,8,128,256]{3,2,1,0:T(8,128)(2,1)S(1)}, u32[]{:S(2)}, u32[]{:S(2)}) collective-permute-start(bf16[1,8,128,256]{3,2,1,0:T(8,128)(2,1)} %slice_bitcast_fusion.3), channel_id=1, source_target_pairs={{0,2},{2,0},{4,6},{6,4},{8,10},{10,8},{12,14},{14,12},{16,18},{18,... | collective-permute-start | bytes 1572872 | tf_op jit(solution)/shard_map/ppermute | solution.py:198
  42.4 14.4 %collective-permute-start.3 = (bf16[256,1024]{1,0:T(8,128)(2,1)}, bf16[256,1024]{1,0:T(8,128)(2,1)}, u32[]{:S(2)}, u32[]{:S(2)}) collective-permute-start(bf16[256,1024]{1,0:T(8,128)(2,1)} %collective-permute-done.2), channel_id=1, source_target_pairs={{0,2},{2,0},{4,6},{6,4},{8,10},{10,8},{12,14},{14,12},{16,18},{18,... | collective-permute-start | bytes 1572872 | tf_op jit(solution)/shard_map/ppermute | solution.py:178
  52.2 14.8 %all-to-all-start.1 = ((bf16[16,64,128]{2,1,0:T(8,128)(2,1)}), bf16[16,64,128]{2,1,0:T(8,128)(2,1)S(1)}, u32[]{:S(2)}, u32[]{:S(2)}) async-start(bf16[16,64,128]{2,1,0:T(8,128)(2,1)} %bitcast.2), calls=%async_computation.1 | async-start | bytes 524288 | tf_op jit(solution)/shard_map/all_to_all | solution.py:206
  56.8 10.2 %copy-start.3 = (bf16[128,1024]{1,0:T(8,128)(2,1)S(1)}, bf16[128,1024]{1,0:T(8,128)(2,1)}, u32[]{:S(2)}) copy-start(bf16[128,1024]{1,0:T(8,128)(2,1)} %residual_ref.1) | copy-start | bytes 786436
  69.9 6.4 %collective-permute-start.4 = (bf16[128,1024]{1,0:T(8,128)(2,1)S(1)}, bf16[128,1024]{1,0:T(8,128)(2,1)S(1)}, u32[]{:S(2)}, u32[]{:S(2)}) collective-permute-start(bf16[128,1024]{1,0:T(8,128)(2,1)S(1)} %shard_map.57.refs_0_.residual_ref), channel_id=1, source_target_pairs={{0,1},{1,0},{2,3},{3,2},{4,5},{5,4},{6,7},{7,6},{8,9},{9,8},{10,11... | collective-permute-start | bytes 786440 | tf_op jit(solution)/shard_map/ppermute | solution.py:188
  76.3 2.8 %copy-start.1 = (bf16[2,3,1024,512]{3,2,1,0:T(8,128)(2,1)S(1)}, bf16[2,3,1024,512]{3,2,1,0:T(8,128)(2,1)}, u32[]{:S(2)}) copy-start(bf16[2,3,1024,512]{3,2,1,0:T(8,128)(2,1)} %refs_3_.3) | copy-start | bytes 18874372
  81.8 23.1 %all-to-all-start.2 = ((bf16[8,192,256]{2,1,0:T(8,128)(2,1)}), bf16[8,192,256]{2,1,0:T(8,128)(2,1)S(1)}, u32[]{:S(2)}, u32[]{:S(2)}) async-start(bf16[8,192,256]{2,1,0:T(8,128)(2,1)} %shard_map.58), calls=%async_computation.2 | async-start | bytes 1572864 | tf_op jit(solution)/shard_map/all_to_all | solution.py:195
  87.1 18.1 %collective-permute-start.6 = (bf16[256,1024]{1,0:T(8,128)(2,1)}, bf16[256,1024]{1,0:T(8,128)(2,1)S(1)}, u32[]{:S(2)}, u32[]{:S(2)}) collective-permute-start(bf16[256,1024]{1,0:T(8,128)(2,1)} %constant_dynamic-slice_fusion), channel_id=1, source_target_pairs={{0,1},{1,0},{2,3},{3,2},{4,5},{5,4},{6,7},{7,6},{8,9},{9,8},{10,11... | collective-permute-start | bytes 1572872 | tf_op jit(solution)/shard_map/ppermute | solution.py:177
  105.0 2.0 %collective-permute-start.5 = (bf16[1,8,128,256]{3,2,1,0:T(8,128)(2,1)S(1)}, bf16[1,8,128,256]{3,2,1,0:T(8,128)(2,1)S(1)}, u32[]{:S(2)}, u32[]{:S(2)}) collective-permute-start(bf16[1,8,128,256]{3,2,1,0:T(8,128)(2,1)S(1)} %slice_bitcast_fusion.2), channel_id=1, source_target_pairs={{0,2},{2,0},{4,6},{6,4},{8,10},{10,8},{12,14},{14,12},{16,18},{18,... | collective-permute-start | bytes 1572872 | tf_op jit(solution)/shard_map/ppermute | solution.py:198
  105.2 13.3 %collective-permute-start.7 = (bf16[256,1024]{1,0:T(8,128)(2,1)S(1)}, bf16[256,1024]{1,0:T(8,128)(2,1)}, u32[]{:S(2)}, u32[]{:S(2)}) collective-permute-start(bf16[256,1024]{1,0:T(8,128)(2,1)S(1)} %collective-permute-done.6), channel_id=1, source_target_pairs={{0,2},{2,0},{4,6},{6,4},{8,10},{10,8},{12,14},{14,12},{16,18},{18,... | collective-permute-start | bytes 1572872 | tf_op jit(solution)/shard_map/ppermute | solution.py:178
  114.8 14.0 %all-to-all-start.3 = ((bf16[16,64,128]{2,1,0:T(8,128)(2,1)}), bf16[16,64,128]{2,1,0:T(8,128)(2,1)S(1)}, u32[]{:S(2)}, u32[]{:S(2)}) async-start(bf16[16,64,128]{2,1,0:T(8,128)(2,1)} %bitcast.6), calls=%async_computation.3 | async-start | bytes 524288 | tf_op jit(solution)/shard_map/all_to_all | solution.py:206
  118.5 0.8 copy-start.5
where the time goes:
time: 132 us; the launch traced here: 131 us
  waiting for transfers between devices  62.5 us (47%)
  Pallas kernels  26.4 us (20%)
  starting transfers between devices  25.9 us (20%)
  local copies, waits for them, and re-layouts  12.5 us (9%)
  other arithmetic  3.64 us (3%)
    all_to_all x2, waiting for transfers between devices, per_device(): lax.all_to_all(fields, 'ctx', 0, 0, axis_index_groups=shard_groups, tiled...  32.6 us
    all_to_all x2, waiting for transfers between devices, per_device(): lax.all_to_all(heads, ('ctx', 'head'), 0, 0, axis_index_groups=row_groups...  16 us
    pallas_call x2, Pallas kernels, attention(): pl.pallas_call(attention_kernel, in_specs=[pl.BlockSpec(memory_space=pltp...  15.7 us
    ppermute x2, waiting for transfers between devices, per_device(): rows = [residual, lax.ppermute(residual, 'head', swap)]  11.1 us
    all_to_all x2, starting transfers between devices, per_device(): lax.all_to_all(fields, 'ctx', 0, 0, axis_index_groups=shard_groups, tiled...  10.5 us
    all_to_all x2, starting transfers between devices, per_device(): lax.all_to_all(heads, ('ctx', 'head'), 0, 0, axis_index_groups=row_groups...  8.25 us
    unnamed x10, local copies, waits for them, and re-layouts  6.53 us
    pallas_call x2, Pallas kernels, project(): pl.pallas_call(kernel, grid=(3,), in_specs=[pl.BlockSpec(r.shape, lambda...  5.42 us
  transfers between devices with their start and end apart: 12, of which 8 were waited for; matrix products, arithmetic and copies ran while one was open for 7% of the time, Pallas kernels for 12%

commit v1 on v0

v1 whole, which is shorter than its diff:
```python
import functools

import jax
import jax.numpy as jnp
from jax import lax
from jax.experimental import pallas as pl
from jax.experimental.pallas import tpu as pltpu
from jax.sharding import PartitionSpec as P

HD = 64
LAYERS = 2
EPSILON = 1e-06
GRANT = 16 * 2**20
VMEM = pl.BlockSpec(memory_space=pltpu.VMEM)


def rms_scale(values, gain):
    mean_square = jnp.mean(values * values, axis=-1, keepdims=True)
    return values * lax.rsqrt(mean_square + EPSILON) * gain


def project_kernel(layer, row_ref, gain_ref, weight_ref, out_ref, normed):
    @pl.when(pl.program_id(0) == 0)
    def _():
        gain = gain_ref[layer : layer + 1, :]
        normed[...] = rms_scale(row_ref[...].astype(jnp.float32), gain).astype(jnp.bfloat16)

    field = jnp.dot(normed[...], weight_ref[...], preferred_element_type=jnp.float32)
    flipped = field.T.astype(jnp.bfloat16)
    for head in range(out_ref.shape[0]):
        out_ref[head] = flipped[head * HD : (head + 1) * HD]


def project(layer, rows, gain, project_in, weight=1):
    width, columns = project_in.shape[1:]
    tokens = rows.shape[0]
    heads = columns // HD
    return pl.pallas_call(
        functools.partial(project_kernel, layer),
        grid=(3,),
        in_specs=[
            pl.BlockSpec(rows.shape, lambda m: (0, 0)),
            pl.BlockSpec(gain.shape, lambda m: (0, 0)),
            pl.BlockSpec((None, width, columns), lambda m: (m, 0, 0)),
        ],
        out_specs=pl.BlockSpec((heads, HD, tokens), lambda m: (0, m, 0)),
        out_shape=jax.ShapeDtypeStruct((heads, 3 * HD, tokens), jnp.bfloat16),
        scratch_shapes=[pltpu.VMEM((tokens, width), jnp.bfloat16)],
        compiler_params=pltpu.CompilerParams(vmem_limit_bytes=GRANT),
        cost_estimate=pl.CostEstimate(
            flops=6 * tokens * width * columns * weight, bytes_accessed=6 * width * columns, transcendentals=0
        ),
    )(rows, gain, project_in)


def attention_kernel(layer, own_count, start, place, gain_ref, *refs):
    out_ref, keys, values = refs[-3:]
    own, others = refs[:own_count], refs[own_count:-3]
    sources, groups, _, tokens = keys.shape
    width = own[0].shape[-1]
    split, piece = out_ref.shape[0], out_ref.shape[-1]

    def part(source, chunk, group, which):
        rows = slice(which * HD, (which + 1) * HD)
        if sources > 2:
            return others[0][source, group, rows, :]
        return (others if source else own)[chunk][group, rows, :]

    for group in range(groups):
        for source in range(sources):
            for chunk in range(own_count):
                lanes = slice(chunk * width, (chunk + 1) * width)
                keys[source, group, :, lanes] = part(source, chunk, group, 1)
                values[source, group, lanes, :] = part(source, chunk, group, 2).T

    def shift(source):
        if sources == 2:
            return source * (2 * replica - 1)
        return replica - source

    def places(axis):
        place = lax.broadcasted_iota(jnp.int32, (tokens, tokens), axis) + start()
        return jnp.where(place >= tokens, place - tokens, place)

    ahead = places(1) - places(0)
    head, replica = place()
    gains = gain_ref[layer : layer + 1, :]
    gain = sum(
        jnp.where(head == index, gains[:, index * HD : (index + 1) * HD], 0.0) for index in range(gains.shape[1] // HD)
    )
    for group in range(groups):
        query = jnp.concatenate([ref[group, :HD, :] for ref in own], axis=1).T
        total = jnp.zeros((tokens, HD), jnp.float32)
        for past in range(group + 1):
            for source in range(sources):
                scores = jnp.dot(query, keys[source, past], preferred_element_type=jnp.float32)
                weights = scores * scores
                if past == group:
                    weights = jnp.where(ahead <= shift(source) * tokens, weights, 0.0)
                total += jnp.dot(
                    weights.astype(jnp.bfloat16), values[source, past], preferred_element_type=jnp.float32
                )
        flipped = rms_scale(total, gain).T.astype(jnp.bfloat16)
        for index in range(split):
            lanes = flipped[:, index * piece : (index + 1) * piece]
            if own_count == 1:
                out_ref[index, group] = lanes
            else:
                out_ref[start() // width if index == 0 else 1 - start() // width, group] = lanes


def attention(layer, sources, gain, own, others, start, place, split):
    groups = own[0].shape[0]
    tokens = sum(chunk.shape[2] for chunk in own)
    pairs = groups * (groups + 1) // 2 * sources * tokens * tokens

    def kernel(*refs):
        attention_kernel(layer, len(own), start, place, *refs)

    return pl.pallas_call(
        kernel,
        in_specs=[VMEM] * (1 + len(own) + len(others)),
        out_specs=VMEM,
        out_shape=jax.ShapeDtypeStruct((split, groups, HD, tokens // split), jnp.bfloat16),
        scratch_shapes=[
            pltpu.VMEM((sources, groups, HD, tokens), jnp.bfloat16),
            pltpu.VMEM((sources, groups, tokens, HD), jnp.bfloat16),
        ],
        compiler_params=pltpu.CompilerParams(vmem_limit_bytes=GRANT),
        cost_estimate=pl.CostEstimate(flops=4 * pairs * HD, bytes_accessed=2**21, transcendentals=0),
    )(gain, *own, *others)


def mix_kernel(starts, mixed_ref, residual_ref, *refs):
    weight_refs, out_ref, flipped = refs[:-2], refs[-2], refs[-1]

    @pl.when(pl.program_id(0) == 0)
    def _():
        first = 0
        for start, ref in zip(starts(), weight_refs):
            rows = ref.shape[0]
            at = start if isinstance(start, int) else pl.multiple_of(start, rows)
            flipped[:, first : first + rows] = mixed_ref[pl.ds(at, rows), :].T
            first += rows

    total, first = residual_ref[...].astype(jnp.float32), 0
    for ref in weight_refs:
        rows = ref.shape[0]
        total += jnp.dot(flipped[:, first : first + rows], ref[...], preferred_element_type=jnp.float32)
        first += rows
    out_ref[...] = total.astype(jnp.bfloat16)


def mix(mixed, residual, weights, starts):
    depth, rows = mixed.shape
    width = residual.shape[1]
    steps = 4 if width % 1024 == 0 else 1

    def kernel(*refs):
        mix_kernel(starts, *refs)

    return pl.pallas_call(
        kernel,
        grid=(steps,),
        in_specs=[
            pl.BlockSpec((depth, rows), lambda n: (0, 0)),
            pl.BlockSpec((rows, width // steps), lambda n: (0, n)),
        ]
        + [pl.BlockSpec((w.shape[0], width // steps), lambda n: (0, n)) for w in weights],
        out_specs=pl.BlockSpec((rows, width // steps), lambda n: (0, n)),
        out_shape=jax.ShapeDtypeStruct(residual.shape, jnp.bfloat16),
        scratch_shapes=[pltpu.VMEM((rows, depth), jnp.bfloat16)],
        compiler_params=pltpu.CompilerParams(vmem_limit_bytes=GRANT),
        cost_estimate=pl.CostEstimate(
            flops=2 * rows * width * depth, bytes_accessed=2 * width * depth, transcendentals=0
        ),
    )(mixed, residual, *weights)


def per_device(residual, input_gain, project_in, output_gain, project_out):
    shards, split = lax.axis_size("ctx"), lax.axis_size("head")
    depth = output_gain.shape[1]
    local_heads = depth // HD
    replicas = shards // local_heads
    paired = split == 2
    swap = [(0, 1), (1, 0)]
    neighbours = [(c, c ^ 1) for c in range(shards)]
    rows = residual.shape[0]

    shard_groups = [[k * replicas + r for k in range(local_heads)] for r in range(replicas)]
    row_groups = [[c * split + x for x in range(split) for c in group] for group in shard_groups]
    head_groups = [[k * replicas + r for r in range(replicas)] for k in range(local_heads)]

    def weight_starts():
        if not paired:
            return [0]
        mine = lax.axis_index("head")
        return [mine * depth, (1 - mine) * depth]

    def place():
        index = lax.axis_index("ctx")
        return index // replicas, index % replicas

    def first_place():
        return lax.axis_index("head") * rows if paired else 0

    before = None
    for layer in range(LAYERS):
        out, into = project_out[layer], project_in[layer]
        if paired:
            peer = lax.ppermute(residual, "head", swap)
            if before is None:
                out, _ = lax.optimization_barrier((out, peer))
            else:
                out, into, _ = lax.optimization_barrier((project_out, project_in, before))
                out, into = out[layer], into[layer]
            weights_out = [out, lax.ppermute(out, "head", swap)]
            chunks = [residual, peer]
        else:
            weights_out = [lax.all_gather(out, "head", axis=0, tiled=True)]
            chunks = [lax.all_gather(residual, "head", axis=0, tiled=True)]
        own = [
            lax.all_to_all(
                project(layer, chunk, input_gain, into, 1 + 20 * number),
                "ctx",
                0,
                0,
                axis_index_groups=shard_groups,
                tiled=True,
            )
            for number, chunk in enumerate(chunks)
        ]
        before = own[-1]
        tokens = rows * split
        if replicas == 1:
            others = []
        elif replicas == 2:
            others = [lax.ppermute(chunk, "ctx", neighbours) for chunk in own]
        else:
            own = [jnp.concatenate(own, axis=2)]
            others = [lax.all_gather(own[0], "ctx", axis=0, axis_index_groups=head_groups)]
        heads = attention(layer, replicas, output_gain, own, others, first_place, place, split)
        heads = heads.reshape(split * local_heads, HD, tokens // split)
        mixed = lax.all_to_all(heads, ("ctx", "head"), 0, 0, axis_index_groups=row_groups, tiled=True)
        mixed = mixed.reshape(split * local_heads * HD, tokens // split)
        residual = mix(mixed, residual, weights_out, weight_starts)
    return residual


def solution(mesh):
    return jax.shard_map(
        per_device,
        mesh=mesh,
        in_specs=(
            P(("ctx", "head"), None),
            P(),
            P(None, None, None, "head"),
            P(None, "head"),
            P(None, "head", None),
        ),
        out_specs=P(("ctx", "head"), None),
        check_vma=False,
    )
```

time: 132 us -> 127 us (0.962)
  waiting for transfers between devices: 62.5 us -> 55.2 us
  starting transfers between devices: 25.9 us -> 32.5 us
  other arithmetic: 3.64 us -> 0 us
  local copies, waits for them, and re-layouts: 12.5 us -> 9.02 us
  Pallas kernels: 26.4 us -> 28.9 us
    ppermute x8, waiting for transfers between devices: 13.9 us -> 3.91 us  [the longest x4 3.44 us: per_device(): others = [lax.ppermute(chunk, 'ctx', neighbours) for chunk in own]]
    all_to_all x2 -> x4, starting transfers between devices: 10.5 us -> 17.2 us  [per_device(): lax.all_to_all(project(layer, chunk, input_gain, into, 1 + 20 * number),...]
    squeeze x1 -> x4, local copies, waits for them, and re-layouts: 1.71 us -> 6.77 us  [the longest x2 3.39 us: per_device(): out, into = (out[layer], into[layer])]
    unnamed x10 -> x12, local copies, waits for them, and re-layouts: 6.53 us -> 2.25 us
    pallas_call x4 -> x6, Pallas kernels: 21.1 us -> 25 us  [the longest x2 16.6 us: attention(): pl.pallas_call(kernel, in_specs=[VMEM] * (1 + len(own) + len(others)), ou...]
    all_to_all x2, waiting for transfers between devices: 16 us -> 19.9 us  [per_device(): lax.all_to_all(heads, ('ctx', 'head'), 0, 0, axis_index_groups=row_groups...]
    concatenate x2 -> x0, other arithmetic: 3.56 us -> none  [other_half(): jnp.concatenate([mine, theirs], axis=0)]
    dynamic_slice x4 -> x0, local copies, waits for them, and re-layouts: 1.86 us -> none  [the longest x2 1.71 us: other_half(): lax.dynamic_slice_in_dim(weights, near * (depth // 2), depth // 2, axis=0)]
  transfers between devices with their start and end apart: 12 -> 14, of which waited for: 8 -> 9; matrix products, arithmetic and copies ran while one was open for 7% -> 5% of each run, Pallas kernels for 12% -> 20%
where the time goes in v1:
time: 127 us; the launch traced here: 126 us
  waiting for transfers between devices  55.2 us (43%)
  starting transfers between devices  32.5 us (26%)
  Pallas kernels  28.9 us (23%)
  local copies, waits for them, and re-layouts  9.02 us (7%)
    all_to_all x4, waiting for transfers between devices, per_device(): lax.all_to_all(project(layer, chunk, input_gain, into, 1 + 20 * number),...  31.5 us
    all_to_all x2, waiting for transfers between devices, per_device(): lax.all_to_all(heads, ('ctx', 'head'), 0, 0, axis_index_groups=row_groups...  19.9 us
    all_to_all x4, starting transfers between devices, per_device(): lax.all_to_all(project(layer, chunk, input_gain, into, 1 + 20 * number),...  17.2 us
    pallas_call x2, Pallas kernels, attention(): pl.pallas_call(kernel, in_specs=[VMEM] * (1 + len(own) + len(others)), ou...  16.6 us
    all_to_all x2, starting transfers between devices, per_device(): lax.all_to_all(heads, ('ctx', 'head'), 0, 0, axis_index_groups=row_groups...  9.02 us
    pallas_call x4, Pallas kernels, project(): pl.pallas_call(functools.partial(project_kernel, layer), grid=(3,), in_sp...  8.39 us
    ppermute x2, starting transfers between devices, per_device(): peer = lax.ppermute(residual, 'head', swap)  4.1 us
    pallas_call x2, Pallas kernels, mix(): pl.pallas_call(kernel, grid=(steps,), in_specs=[pl.BlockSpec((depth, rows...  3.9 us
  transfers between devices with their start and end apart: 14, of which 9 were waited for; matrix products, arithmetic and copies ran while one was open for 5% of the time, Pallas kernels for 20%

profile of v1, /device:TPU:0, one launch (start us, length us, event | category | flops | bytes accessed | tf_op | source)
XLA Modules:
  0.0 125.9 jit_solution(11830591509454536845)
XLA Ops:
  0.0 2.9 %collective-permute-start = (bf16[128,1024]{1,0:T(8,128)(2,1)}, bf16[128,1024]{1,0:T(8,128)(2,1)}, u32[]{:S(2)}, u32[]{:S(2)}) collective-permute-start(bf16[128,1024]{1,0:T(8,128)(2,1)} %refs_1_.1), channel_id=1, source_target_pairs={{0,1},{1,0},{2,3},{3,2},{4,5},{5,4},{6,7},{7,6},{8,9},{9,8},{10,11... | collective-permute-start | bytes 786440 | tf_op jit(solution)/shard_map/ppermute | solution.py:211
  2.9 2.1 %slice_bitcast_fusion.1.weight_ref = bf16[3,1024,512]{2,1,0:T(8,128)(2,1)S(1)} fusion(bf16[2,3,1024,512]{3,2,1,0:T(8,128)(2,1)} %param.7), kind=kLoop, calls=%fused_computation.1 | loop fusion | bytes 6291456 | tf_op jit(solution)/shard_map/squeeze | solution.py:209
  5.1 2.3 %shard_map.55 = bf16[8,192,128]{2,1,0:T(8,128)(2,1)} custom-call(bf16[128,1024]{1,0:T(8,128)(2,1)S(1)} %copy-done.1, f32[2,1024]{1,0:T(2,128)S(1)} %copy-done.4, bf16[3,1024,512]{2,1,0:T(8,128)(2,1)S(1)} %slice_bitcast_fusion.1.weight_ref), custom_call_target="tpu_custom_call" | custom-call | flops 402653184 | bytes 3145728 | tf_op jit(solution)/shard_map/pallas_call | solution.py:38
  7.3 5.8 %all-to-all-start = ((bf16[8,192,128]{2,1,0:T(8,128)(2,1)}), bf16[8,192,128]{2,1,0:T(8,128)(2,1)}, u32[]{:S(2)}, u32[]{:S(2)}) async-start(bf16[8,192,128]{2,1,0:T(8,128)(2,1)} %shard_map.55), calls=%async_computation | async-start | bytes 786432 | tf_op jit(solution)/shard_map/all_to_all | solution.py:223
  13.2 2.4 %shard_map.56 = bf16[8,192,128]{2,1,0:T(8,128)(2,1)S(1)} custom-call(bf16[128,1024]{1,0:T(8,128)(2,1)} %collective-permute-done.row_ref, f32[2,1024]{1,0:T(2,128)S(1)} %copy-done.4, bf16[3,1024,512]{2,1,0:T(8,128)(2,1)S(1)} %slice_bitcast_fusion.1.weight_ref), custom_call_target="tpu_custom_call" | custom-call | flops 8455716864 | bytes 3145728 | tf_op jit(solution)/shard_map/pallas_call | solution.py:38
  16.3 8.4 %all-to-all-done.refs_1_ = bf16[8,192,128]{2,1,0:T(8,128)(2,1)} async-done(((bf16[8,192,128]{2,1,0:T(8,128)(2,1)}), bf16[8,192,128]{2,1,0:T(8,128)(2,1)}, u32[]{:S(2)}, u32[]{:S(2)}) %all-to-all-start) | async-done | bytes 393248 | tf_op jit(solution)/shard_map/all_to_all | solution.py:223
  24.7 3.6 %all-to-all-start.1 = ((bf16[8,192,128]{2,1,0:T(8,128)(2,1)}), bf16[8,192,128]{2,1,0:T(8,128)(2,1)S(1)}, u32[]{:S(2)}, u32[]{:S(2)}) async-start(bf16[8,192,128]{2,1,0:T(8,128)(2,1)} %copy-done.2), calls=%async_computation.1 | async-start | bytes 786432 | tf_op jit(solution)/shard_map/all_to_all | solution.py:223
  30.3 9.2 %all-to-all-done.1.refs_2_ = bf16[8,192,128]{2,1,0:T(8,128)(2,1)S(1)} async-done(((bf16[8,192,128]{2,1,0:T(8,128)(2,1)}), bf16[8,192,128]{2,1,0:T(8,128)(2,1)S(1)}, u32[]{:S(2)}, u32[]{:S(2)}) %all-to-all-start.1) | async-done | bytes 393248 | tf_op jit(solution)/shard_map/all_to_all | solution.py:223
  39.5 1.7 %collective-permute-done.2.refs_4_ = bf16[8,192,128]{2,1,0:T(8,128)(2,1)S(1)} collective-permute-done((bf16[8,192,128]{2,1,0:T(8,128)(2,1)S(1)}, bf16[8,192,128]{2,1,0:T(8,128)(2,1)S(1)}, u32[]{:S(2)}, u32[]{:S(2)}) %collective-permute-start.2) | collective-permute-done | bytes 393248 | tf_op jit(solution)/shard_map/ppermute | solution.py:238
  41.2 8.3 %shard_map.57 = bf16[2,8,64,128]{3,2,1,0:T(8,128)(2,1)} custom-call(f32[2,512]{1,0:T(2,128)S(1)} %copy-done.5, bf16[8,192,128]{2,1,0:T(8,128)(2,1)} %all-to-all-done.refs_1_, bf16[8,192,128]{2,1,0:T(8,128)(2,1)S(1)} %all-to-all-done.1.refs_2_, bf16[8,192,128]{2,1,0:T(8,128)(2,1)S(1)} %collective-permute-done.1.refs_3_, ...), custom_call_target="tpu_custom_call" | custom-call | flops 1207959552 | bytes 2097152 | tf_op jit(solution)/shard_map/pallas_call | solution.py:120
  49.5 3.8 %all-to-all-start.2 = ((bf16[16,64,128]{2,1,0:T(8,128)(2,1)}), bf16[16,64,128]{2,1,0:T(8,128)(2,1)S(1)}, u32[]{:S(2)}, u32[]{:S(2)}) async-start(bf16[16,64,128]{2,1,0:T(8,128)(2,1)} %bitcast.1), calls=%async_computation.2 | async-start | bytes 524288 | tf_op jit(solution)/shard_map/all_to_all | solution.py:244
  53.8 9.7 %all-to-all-done.2 = bf16[16,64,128]{2,1,0:T(8,128)(2,1)S(1)} async-done(((bf16[16,64,128]{2,1,0:T(8,128)(2,1)}), bf16[16,64,128]{2,1,0:T(8,128)(2,1)S(1)}, u32[]{:S(2)}, u32[]{:S(2)}) %all-to-all-start.2) | async-done | bytes 262176 | tf_op jit(solution)/shard_map/all_to_all | solution.py:244
  66.1 2.1 %slice_bitcast_fusion.weight_ref = bf16[3,1024,512]{2,1,0:T(8,128)(2,1)S(1)} fusion(bf16[2,3,1024,512]{3,2,1,0:T(8,128)(2,1)} %param.7), kind=kLoop, calls=%fused_computation | loop fusion | bytes 6291456 | tf_op jit(solution)/shard_map/squeeze | solution.py:216
  70.4 4.1 %all-to-all-start.3 = ((bf16[8,192,128]{2,1,0:T(8,128)(2,1)}), bf16[8,192,128]{2,1,0:T(8,128)(2,1)}, u32[]{:S(2)}, u32[]{:S(2)}) async-start(bf16[8,192,128]{2,1,0:T(8,128)(2,1)} %copy-done), calls=%async_computation.3 | async-start | bytes 786432 | tf_op jit(solution)/shard_map/all_to_all | solution.py:223
  74.5 2.4 %shard_map.60 = bf16[8,192,128]{2,1,0:T(8,128)(2,1)S(1)} custom-call(bf16[128,1024]{1,0:T(8,128)(2,1)} %collective-permute-done.4.row_ref, f32[2,1024]{1,0:T(2,128)S(1)} %copy-done.4, bf16[3,1024,512]{2,1,0:T(8,128)(2,1)S(1)} %slice_bitcast_fusion.weight_ref), custom_call_target="tpu_custom_call" | custom-call | flops 8455716864 | bytes 3145728 | tf_op jit(solution)/shard_map/pallas_call | solution.py:38
  77.6 6.4 %all-to-all-done.3.refs_1_ = bf16[8,192,128]{2,1,0:T(8,128)(2,1)} async-done(((bf16[8,192,128]{2,1,0:T(8,128)(2,1)}), bf16[8,192,128]{2,1,0:T(8,128)(2,1)}, u32[]{:S(2)}, u32[]{:S(2)}) %all-to-all-start.3) | async-done | bytes 393248 | tf_op jit(solution)/shard_map/all_to_all | solution.py:223
  84.1 3.7 %all-to-all-start.4 = ((bf16[8,192,128]{2,1,0:T(8,128)(2,1)}), bf16[8,192,128]{2,1,0:T(8,128)(2,1)S(1)}, u32[]{:S(2)}, u32[]{:S(2)}) async-start(bf16[8,192,128]{2,1,0:T(8,128)(2,1)} %copy-done.3), calls=%async_computation.4 | async-start | bytes 786432 | tf_op jit(solution)/shard_map/all_to_all | solution.py:223
  89.0 1.5 %collective-permute-start.7 = (bf16[512,1024]{1,0:T(8,128)(2,1)S(1)}, bf16[512,1024]{1,0:T(8,128)(2,1)S(1)}, u32[]{:S(2)}, u32[]{:S(2)}) collective-permute-start(bf16[512,1024]{1,0:T(8,128)(2,1)S(1)} %slice_bitcast_fusion.2.refs_2_), channel_id=1, source_target_pairs={{0,1},{1,0},{2,3},{3,2},{4,5},{5,4},{6,7},{7,6},{8,9},{9,8},{10,11... | collective-permute-start | bytes 3145736 | tf_op jit(solution)/shard_map/ppermute | solution.py:217
  90.6 7.4 %all-to-all-done.4.refs_2_ = bf16[8,192,128]{2,1,0:T(8,128)(2,1)S(1)} async-done(((bf16[8,192,128]{2,1,0:T(8,128)(2,1)}), bf16[8,192,128]{2,1,0:T(8,128)(2,1)S(1)}, u32[]{:S(2)}, u32[]{:S(2)}) %all-to-all-start.4) | async-done | bytes 393248 | tf_op jit(solution)/shard_map/all_to_all | solution.py:223
  98.0 1.7 %collective-permute-done.6.refs_4_ = bf16[8,192,128]{2,1,0:T(8,128)(2,1)S(1)} collective-permute-done((bf16[8,192,128]{2,1,0:T(8,128)(2,1)S(1)}, bf16[8,192,128]{2,1,0:T(8,128)(2,1)S(1)}, u32[]{:S(2)}, u32[]{:S(2)}) %collective-permute-start.6) | collective-permute-done | bytes 393248 | tf_op jit(solution)/shard_map/ppermute | solution.py:238
  99.7 8.3 %shard_map.61 = bf16[2,8,64,128]{3,2,1,0:T(8,128)(2,1)} custom-call(f32[2,512]{1,0:T(2,128)S(1)} %copy-done.5, bf16[8,192,128]{2,1,0:T(8,128)(2,1)} %all-to-all-done.3.refs_1_, bf16[8,192,128]{2,1,0:T(8,128)(2,1)S(1)} %all-to-all-done.4.refs_2_, bf16[8,192,128]{2,1,0:T(8,128)(2,1)S(1)} %collective-permute-done.5.refs_3_, ...), custom_call_target="tpu_custom_call" | custom-call | flops 1207959552 | bytes 2097152 | tf_op jit(solution)/shard_map/pallas_call | solution.py:120
  108.0 5.2 %all-to-all-start.5 = ((bf16[16,64,128]{2,1,0:T(8,128)(2,1)}), bf16[16,64,128]{2,1,0:T(8,128)(2,1)S(1)}, u32[]{:S(2)}, u32[]{:S(2)}) async-start(bf16[16,64,128]{2,1,0:T(8,128)(2,1)} %bitcast.5), calls=%async_computation.5 | async-start | bytes 524288 | tf_op jit(solution)/shard_map/all_to_all | solution.py:244
  113.3 10.2 %all-to-all-done.5 = bf16[16,64,128]{2,1,0:T(8,128)(2,1)S(1)} async-done(((bf16[16,64,128]{2,1,0:T(8,128)(2,1)}), bf16[16,64,128]{2,1,0:T(8,128)(2,1)S(1)}, u32[]{:S(2)}, u32[]{:S(2)}) %all-to-all-start.5) | async-done | bytes 262176 | tf_op jit(solution)/shard_map/all_to_all | solution.py:244
  123.5 2.4 %shard_map.62 = bf16[128,1024]{1,0:T(8,128)(2,1)} custom-call(bf16[1024,128]{1,0:T(8,128)(2,1)S(1)} %bitcast.12, bf16[128,1024]{1,0:T(8,128)(2,1)S(1)} %shard_map.58.row_ref.refs_1_, bf16[512,1024]{1,0:T(8,128)(2,1)S(1)} %slice_bitcast_fusion.2.refs_2_, bf16[512,1024]{1,0:T(8,128)(2,1)S(1)} %collective-permute-done.7.refs_3_), custom_call_target="tpu_custom_call" | custom-call | flops 268435456 | bytes 2097152 | tf_op jit(solution)/shard_map/pallas_call | solution.py:162
  (28 shorter events, 10.0 us)
Async XLA Ops:
  0.0 5.0 %copy-start.1 = (bf16[128,1024]{1,0:T(8,128)(2,1)S(1)}, bf16[128,1024]{1,0:T(8,128)(2,1)}, u32[]{:S(2)}) copy-start(bf16[128,1024]{1,0:T(8,128)(2,1)} %refs_1_.1) | copy-start | bytes 786436
  0.0 5.0 %copy-start.4 = (f32[2,1024]{1,0:T(2,128)S(1)}, f32[2,1024]{1,0:T(2,128)}, u32[]{:S(2)}) copy-start(f32[2,1024]{1,0:T(2,128)} %gain_ref.7) | copy-start | bytes 24580
  0.0 13.2 %collective-permute-start = (bf16[128,1024]{1,0:T(8,128)(2,1)}, bf16[128,1024]{1,0:T(8,128)(2,1)}, u32[]{:S(2)}, u32[]{:S(2)}) collective-permute-start(bf16[128,1024]{1,0:T(8,128)(2,1)} %refs_1_.1), channel_id=1, source_target_pairs={{0,1},{1,0},{2,3},{3,2},{4,5},{5,4},{6,7},{7,6},{8,9},{9,8},{10,11... | collective-permute-start | bytes 786440 | tf_op jit(solution)/shard_map/ppermute | solution.py:211
  7.3 17.4 %all-to-all-start = ((bf16[8,192,128]{2,1,0:T(8,128)(2,1)}), bf16[8,192,128]{2,1,0:T(8,128)(2,1)}, u32[]{:S(2)}, u32[]{:S(2)}) async-start(bf16[8,192,128]{2,1,0:T(8,128)(2,1)} %shard_map.55), calls=%async_computation | async-start | bytes 786432 | tf_op jit(solution)/shard_map/all_to_all | solution.py:223
  13.2 28.0 %copy-start.5 = (f32[2,512]{1,0:T(2,128)S(1)}, f32[2,512]{1,0:T(2,128)}, u32[]{:S(2)}) copy-start(f32[2,512]{1,0:T(2,128)} %refs_0_.3) | copy-start | bytes 12292
  15.5 0.8 copy-start.2
  24.7 14.7 %all-to-all-start.1 = ((bf16[8,192,128]{2,1,0:T(8,128)(2,1)}), bf16[8,192,128]{2,1,0:T(8,128)(2,1)S(1)}, u32[]{:S(2)}, u32[]{:S(2)}) async-start(bf16[8,192,128]{2,1,0:T(8,128)(2,1)} %copy-done.2), calls=%async_computation.1 | async-start | bytes 786432 | tf_op jit(solution)/shard_map/all_to_all | solution.py:223
  29.6 24.1 %collective-permute-start.3 = (bf16[512,1024]{1,0:T(8,128)(2,1)S(1)}, bf16[512,1024]{1,0:T(8,128)(2,1)S(1)}, u32[]{:S(2)}, u32[]{:S(2)}) collective-permute-start(bf16[512,1024]{1,0:T(8,128)(2,1)S(1)} %slice_bitcast_fusion.3.refs_2_), channel_id=1, source_target_pairs={{0,1},{1,0},{2,3},{3,2},{4,5},{5,4},{6,7},{7,6},{8,9},{9,8},{10,11... | collective-permute-start | bytes 3145736 | tf_op jit(solution)/shard_map/ppermute | solution.py:217
  30.3 9.2 %collective-permute-start.1 = (bf16[8,192,128]{2,1,0:T(8,128)(2,1)}, bf16[8,192,128]{2,1,0:T(8,128)(2,1)S(1)}, u32[]{:S(2)}, u32[]{:S(2)}) collective-permute-start(bf16[8,192,128]{2,1,0:T(8,128)(2,1)} %all-to-all-done.refs_1_), channel_id=1, source_target_pairs={{0,2},{2,0},{4,6},{6,4},{8,10},{10,8},{12,14},{14,12},{16,18},{18,... | collective-permute-start | bytes 1179656 | tf_op jit(solution)/shard_map/ppermute | solution.py:238
  39.5 1.7 %collective-permute-start.2 = (bf16[8,192,128]{2,1,0:T(8,128)(2,1)S(1)}, bf16[8,192,128]{2,1,0:T(8,128)(2,1)S(1)}, u32[]{:S(2)}, u32[]{:S(2)}) collective-permute-start(bf16[8,192,128]{2,1,0:T(8,128)(2,1)S(1)} %all-to-all-done.1.refs_2_), channel_id=1, source_target_pairs={{0,2},{2,0},{4,6},{6,4},{8,10},{10,8},{12,14},{14,12},{16,18},{18,... | collective-permute-start | bytes 1179656 | tf_op jit(solution)/shard_map/ppermute | solution.py:238
  49.5 14.0 %all-to-all-start.2 = ((bf16[16,64,128]{2,1,0:T(8,128)(2,1)}), bf16[16,64,128]{2,1,0:T(8,128)(2,1)S(1)}, u32[]{:S(2)}, u32[]{:S(2)}) async-start(bf16[16,64,128]{2,1,0:T(8,128)(2,1)} %bitcast.1), calls=%async_computation.2 | async-start | bytes 524288 | tf_op jit(solution)/shard_map/all_to_all | solution.py:244
  65.0 9.5 %collective-permute-start.4 = (bf16[128,1024]{1,0:T(8,128)(2,1)S(1)}, bf16[128,1024]{1,0:T(8,128)(2,1)}, u32[]{:S(2)}, u32[]{:S(2)}) collective-permute-start(bf16[128,1024]{1,0:T(8,128)(2,1)S(1)} %shard_map.58.row_ref.refs_1_), channel_id=1, source_target_pairs={{0,1},{1,0},{2,3},{3,2},{4,5},{5,4},{6,7},{7,6},{8,9},{9,8},{10,11... | collective-permute-start | bytes 786440 | tf_op jit(solution)/shard_map/ppermute | solution.py:211
  69.7 0.7 copy-start
  70.4 13.7 %all-to-all-start.3 = ((bf16[8,192,128]{2,1,0:T(8,128)(2,1)}), bf16[8,192,128]{2,1,0:T(8,128)(2,1)}, u32[]{:S(2)}, u32[]{:S(2)}) async-start(bf16[8,192,128]{2,1,0:T(8,128)(2,1)} %copy-done), calls=%async_computation.3 | async-start | bytes 786432 | tf_op jit(solution)/shard_map/all_to_all | solution.py:223
  76.9 0.8 copy-start.3
  84.1 13.9 %all-to-all-start.4 = ((bf16[8,192,128]{2,1,0:T(8,128)(2,1)}), bf16[8,192,128]{2,1,0:T(8,128)(2,1)S(1)}, u32[]{:S(2)}, u32[]{:S(2)}) async-start(bf16[8,192,128]{2,1,0:T(8,128)(2,1)} %copy-done.3), calls=%async_computation.4 | async-start | bytes 786432 | tf_op jit(solution)/shard_map/all_to_all | solution.py:223
  89.0 24.2 %collective-permute-start.7 = (bf16[512,1024]{1,0:T(8,128)(2,1)S(1)}, bf16[512,1024]{1,0:T(8,128)(2,1)S(1)}, u32[]{:S(2)}, u32[]{:S(2)}) collective-permute-start(bf16[512,1024]{1,0:T(8,128)(2,1)S(1)} %slice_bitcast_fusion.2.refs_2_), channel_id=1, source_target_pairs={{0,1},{1,0},{2,3},{3,2},{4,5},{5,4},{6,7},{7,6},{8,9},{9,8},{10,11... | collective-permute-start | bytes 3145736 | tf_op jit(solution)/shard_map/ppermute | solution.py:217
  90.6 7.4 %collective-permute-start.5 = (bf16[8,192,128]{2,1,0:T(8,128)(2,1)}, bf16[8,192,128]{2,1,0:T(8,128)(2,1)S(1)}, u32[]{:S(2)}, u32[]{:S(2)}) collective-permute-start(bf16[8,192,128]{2,1,0:T(8,128)(2,1)} %all-to-all-done.3.refs_1_), channel_id=1, source_target_pairs={{0,2},{2,0},{4,6},{6,4},{8,10},{10,8},{12,14},{14,12},{16,18},{18,... | collective-permute-start | bytes 1179656 | tf_op jit(solution)/shard_map/ppermute | solution.py:238
  98.0 1.7 %collective-permute-start.6 = (bf16[8,192,128]{2,1,0:T(8,128)(2,1)S(1)}, bf16[8,192,128]{2,1,0:T(8,128)(2,1)S(1)}, u32[]{:S(2)}, u32[]{:S(2)}) collective-permute-start(bf16[8,192,128]{2,1,0:T(8,128)(2,1)S(1)} %all-to-all-done.4.refs_2_), channel_id=1, source_target_pairs={{0,2},{2,0},{4,6},{6,4},{8,10},{10,8},{12,14},{14,12},{16,18},{18,... | collective-permute-start | bytes 1179656 | tf_op jit(solution)/shard_map/ppermute | solution.py:238
  108.0 15.4 %all-to-all-start.5 = ((bf16[16,64,128]{2,1,0:T(8,128)(2,1)}), bf16[16,64,128]{2,1,0:T(8,128)(2,1)S(1)}, u32[]{:S(2)}, u32[]{:S(2)}) async-start(bf16[16,64,128]{2,1,0:T(8,128)(2,1)} %bitcast.5), calls=%async_computation.5 | async-start | bytes 524288 | tf_op jit(solution)/shard_map/all_to_all | solution.py:244

commit v2 on v1

v2 whole, which is shorter than its diff:
```python
import functools

import jax
import jax.numpy as jnp
from jax import lax
from jax.experimental import pallas as pl
from jax.experimental.pallas import tpu as pltpu
from jax.sharding import PartitionSpec as P

HD = 64
LAYERS = 2
EPSILON = 1e-06
VMEM = pl.BlockSpec(memory_space=pltpu.VMEM)
HBM = pl.BlockSpec(memory_space=pltpu.HBM)


def params(mebibytes):
    return pltpu.CompilerParams(vmem_limit_bytes=mebibytes * 2**20)


def rms_scale(values, gain):
    mean_square = jnp.mean(values * values, axis=-1, keepdims=True)
    return values * lax.rsqrt(mean_square + EPSILON) * gain


def fetch(pairs, semaphores):
    copies = [pltpu.make_async_copy(*pair, semaphores.at[index]) for index, pair in enumerate(pairs)]
    for copy in copies:
        copy.start()
    return copies


def project_rows(rows, gain, weights, flat, place, outs):
    normed = rms_scale(rows, gain).astype(jnp.bfloat16)
    for which in range(3):
        field = jnp.dot(normed, weights(which), preferred_element_type=jnp.float32)
        flipped = field.T.astype(jnp.bfloat16)
        part = slice(which * HD, (which + 1) * HD)
        if len(outs) == 1:
            for head in range(outs[0].shape[0]):
                outs[0][head, part, :] = flipped[head * HD : (head + 1) * HD]
        else:
            flat[...] = flipped
            for slot, out in enumerate(outs):
                start = (place()[0] ^ slot) * HD
                out[part, :] = flat[pl.ds(pl.multiple_of(start, HD), HD), :]


def project(rows, gain, weights, layer, place):
    width, columns = weights.shape[1:]
    tokens = rows.shape[0]

    def kernel(row_ref, gain_ref, weight_ref, out_ref):
        values = row_ref[...].astype(jnp.float32)
        project_rows(values, gain_ref[layer : layer + 1, :], lambda which: weight_ref[which], None, place, [out_ref])

    return pl.pallas_call(
        kernel,
        in_specs=[VMEM] * 3,
        out_specs=VMEM,
        out_shape=jax.ShapeDtypeStruct((columns // HD, 3 * HD, tokens), jnp.bfloat16),
        compiler_params=params(16),
        cost_estimate=pl.CostEstimate(
            flops=6 * tokens * width * columns, bytes_accessed=6 * width * columns, transcendentals=0
        ),
    )(rows, gain, weights)


def mix_rows(starts, mixed, residual, weights):
    total = residual.astype(jnp.float32)
    for start, weight in zip(starts, weights):
        rows = weight.shape[0]
        at = start if isinstance(start, int) else pl.multiple_of(start, rows)
        total += jnp.dot(mixed[pl.ds(at, rows), :].T, weight[...], preferred_element_type=jnp.float32)
    return total.astype(jnp.bfloat16)


def rows_step(residual, mixed=(), onward=(), place=None, slots=False, weight=1):
    rows, width = residual.shape
    operands, views, shapes, outs = [residual], [None], [(residual.shape, jnp.bfloat16)], []
    flops, itself = 0, False
    if mixed:
        entries, index, parts, starts = mixed
        operands += [entries] + list(parts)
        views += [None] + [index if len(part.shape) == 3 else None for part in parts]
        shapes += [(entries.shape, jnp.bfloat16)] + [(part.shape[-2:], jnp.bfloat16) for part in parts]
        outs.append(jax.ShapeDtypeStruct(residual.shape, jnp.bfloat16))
        flops += 2 * rows * width * entries.shape[0]
    if onward:
        layer, gain, project_in = onward
        columns = project_in.shape[-1]
        itself = len(project_in.shape) == 4
        operands += [gain] + [project_in] * (3 if itself else 1)
        views += [None] + [(layer, which) for which in range(3)]
        shapes += [(gain.shape, jnp.float32)] + [(project_in.shape[2:], jnp.bfloat16)] * 3
        shape, heads = (3 * HD, rows), columns // HD
        outs += [jax.ShapeDtypeStruct(shape if slots else (heads, *shape), jnp.bfloat16)] * (heads if slots else 1)
        flops += 6 * rows * width * columns
    count = len(operands)
    scratch = [pltpu.VMEM(*shape) for shape in shapes] + [pltpu.SemaphoreType.DMA((count,))] if itself else []
    if onward and slots:
        scratch.append(pltpu.VMEM((columns, rows), jnp.bfloat16))

    def kernel(*refs):
        sources, results, held = refs[:count], list(refs[count : count + len(outs)]), refs[count + len(outs) :]
        flat = refs[-1] if slots else None
        if itself:
            pairs = [(ref if view is None else ref.at[view], to) for ref, view, to in zip(sources, views, held)]
            copies = fetch(pairs, held[count])
        else:
            held = sources

        def arrived(index):
            if itself:
                copies[index].wait()
            return held[index]

        current, used = arrived(0)[...], 1
        if mixed:
            used = 2 + len(parts)
            current = mix_rows(starts(), arrived(1), current, [arrived(index) for index in range(2, used)])
            results.pop(0)[...] = current
        if onward:
            scale = arrived(used)[layer : layer + 1, :]

            def weights(which):
                return arrived(used + 1 + which)[...] if itself else held[used + 1][which]

            project_rows(current.astype(jnp.float32), scale, weights, flat, place, results)

    return pl.pallas_call(
        kernel,
        in_specs=[HBM if itself else VMEM] * count,
        out_specs=[VMEM] * len(outs),
        out_shape=outs,
        scratch_shapes=scratch,
        compiler_params=params(59 if itself else 16),
        cost_estimate=pl.CostEstimate(flops=flops * weight, bytes_accessed=flops // rows, transcendentals=0),
    )(*operands)


def assemble(slots, place):
    def kernel(*refs):
        for slot, ref in enumerate(refs[:-1]):
            refs[-1][place()[0] ^ slot] = ref[...]

    return pl.pallas_call(
        kernel,
        in_specs=[VMEM] * len(slots),
        out_specs=VMEM,
        out_shape=jax.ShapeDtypeStruct((len(slots), *slots[0].shape), slots[0].dtype),
        compiler_params=params(8),
        cost_estimate=pl.CostEstimate(flops=0, bytes_accessed=4 * len(slots) * slots[0].size, transcendentals=0),
    )(*slots)


def attention_kernel(layer, own_count, start, place, gain_ref, *refs):
    out_ref, keys, values = refs[-3:]
    own, others = refs[:own_count], refs[own_count:-3]
    groups, split, piece = out_ref.shape[1], out_ref.shape[0], out_ref.shape[-1]
    tokens = split * piece
    span = values.shape[1] // groups
    sources = span // tokens
    width = own[0].shape[-1]
    head, replica = place()

    def part(source, chunk, group, which):
        rows = slice(which * HD, (which + 1) * HD)
        if sources > 2:
            return others[0][source, group, rows, :]
        return (others if source else own)[chunk][group, rows, :]

    for group in range(groups):
        for source in range(sources):
            for chunk in range(own_count):
                first = group * span + source * tokens + chunk * width
                keys[first : first + width, :] = part(source, chunk, group, 1).T
                values[:, first : first + width] = part(source, chunk, group, 2)

    def shift(source):
        if sources == 2:
            return source * (2 * replica - 1)
        return replica - source

    def places(axis):
        place = lax.broadcasted_iota(jnp.int32, (tokens, tokens), axis) + start()
        return jnp.where(place >= tokens, place - tokens, place)

    ahead = places(0) - places(1)
    visible = [ahead <= shift(source) * tokens for source in range(sources)]
    gains = gain_ref[layer : layer + 1, :]
    gain = sum(
        jnp.where(head == index, gains[:, index * HD : (index + 1) * HD], 0.0) for index in range(gains.shape[1] // HD)
    ).T
    step = min(span, 512)
    for group in range(groups):
        query = jnp.concatenate([ref[group, :HD, :] for ref in own], axis=1)
        total = jnp.zeros((HD, tokens), jnp.float32)
        for first in range(0, (group + 1) * span, step):
            scores = jnp.dot(keys[first : first + step, :], query, preferred_element_type=jnp.float32)
            weights = scores * scores
            if first >= group * span:
                source = (first - group * span) // tokens
                mask = jnp.concatenate(visible[source : source + step // tokens], axis=0)
                weights = jnp.where(mask, weights, 0.0)
            total += jnp.dot(
                values[:, first : first + step], weights.astype(jnp.bfloat16), preferred_element_type=jnp.float32
            )
        mean_square = jnp.mean(total * total, axis=0, keepdims=True)
        scaled = (total * lax.rsqrt(mean_square + EPSILON) * gain).astype(jnp.bfloat16)
        for index in range(split):
            lanes = scaled[:, index * piece : (index + 1) * piece]
            if own_count == 1:
                out_ref[index, group] = lanes
            else:
                out_ref[start() // width if index == 0 else 1 - start() // width, group] = lanes


def attention(layer, sources, gain, own, others, start, place, split):
    groups = own[0].shape[0]
    tokens = sum(chunk.shape[2] for chunk in own)
    pairs = groups * (groups + 1) // 2 * sources * tokens * tokens

    def kernel(*refs):
        attention_kernel(layer, len(own), start, place, *refs)

    return pl.pallas_call(
        kernel,
        in_specs=[VMEM] * (1 + len(own) + len(others)),
        out_specs=VMEM,
        out_shape=jax.ShapeDtypeStruct((split, groups, HD, tokens // split), jnp.bfloat16),
        scratch_shapes=[
            pltpu.VMEM((groups * sources * tokens, HD), jnp.bfloat16),
            pltpu.VMEM((HD, groups * sources * tokens), jnp.bfloat16),
        ],
        compiler_params=params(16),
        cost_estimate=pl.CostEstimate(flops=4 * pairs * HD, bytes_accessed=2**21, transcendentals=0),
    )(gain, *own, *others)


def per_device(residual, input_gain, project_in, output_gain, project_out):
    shards, split = lax.axis_size("ctx"), lax.axis_size("head")
    depth = output_gain.shape[1]
    local_heads = depth // HD
    replicas = shards // local_heads
    paired = split == 2 and replicas == 2 and local_heads & (local_heads - 1) == 0
    swap = [(0, 1), (1, 0)]
    neighbours = [(c, c ^ 1) for c in range(shards)]
    rows = residual.shape[0]
    tokens = rows * split

    shard_groups = [[k * replicas + r for k in range(local_heads)] for r in range(replicas)]
    row_groups = [[c * split + x for x in range(split) for c in group] for group in shard_groups]
    head_groups = [[k * replicas + r for r in range(replicas)] for k in range(local_heads)]

    def weight_starts():
        if not paired:
            return [0]
        mine = lax.axis_index("head")
        return [mine * depth, (1 - mine) * depth]

    def place():
        index = lax.axis_index("ctx")
        return index // replicas, index % replicas

    def first_place():
        return lax.axis_index("head") * rows if paired else 0

    def to_heads(fields):
        return lax.all_to_all(fields, "ctx", 0, 0, axis_index_groups=shard_groups, tiled=True)

    if paired:
        (fields,) = rows_step(residual, onward=(0, input_gain, project_in), place=place)
    before, into = None, project_in
    for layer in range(LAYERS):
        out = project_out[layer]
        if paired:
            peer = lax.ppermute(residual, "head", swap)
            out, _ = lax.optimization_barrier((out, peer if before is None else before))
            weights_out = [out, lax.ppermute(out, "head", swap)]
            slots = rows_step(peer, (), (layer, input_gain, into), place, True, 20)
            received = [slots[0]]
            for slot in range(1, local_heads):
                partners = [(c, c ^ (replicas * slot)) for c in range(shards)]
                received.append(lax.ppermute(slots[slot], "ctx", partners))
            own = [to_heads(fields), assemble(received, place)]
            others = [lax.ppermute(chunk, "ctx", neighbours) for chunk in own]
            before = own[1]
        else:
            weights_out = [lax.all_gather(out, "head", axis=0, tiled=True)]
            gathered = lax.all_gather(residual, "head", axis=0, tiled=True)
            own = [to_heads(project(gathered, input_gain, project_in[layer], layer, place))]
            others = []
            if replicas > 1:
                others = [lax.all_gather(own[0], "ctx", axis=0, axis_index_groups=head_groups)]
                if replicas == 2:
                    others = [lax.ppermute(own[0], "ctx", neighbours)]
        heads = attention(layer, replicas, output_gain, own, others, first_place, place, split)
        if paired:
            into, _ = lax.optimization_barrier((project_in, heads))
            into = into[(layer + 1) % LAYERS]
        heads = heads.reshape(split * local_heads, HD, tokens // split)
        mixed = lax.all_to_all(heads, ("ctx", "head"), 0, 0, axis_index_groups=row_groups, tiled=True)
        mixed = (mixed.reshape(split * depth, tokens // split), layer, weights_out, weight_starts)
        if paired and layer + 1 < LAYERS:
            residual, fields = rows_step(residual, mixed, (layer + 1, input_gain, into), place)
        else:
            (residual,) = rows_step(residual, mixed)
    return residual


def solution(mesh):
    return jax.shard_map(
        per_device,
        mesh=mesh,
        in_specs=(
            P(("ctx", "head"), None),
            P(),
            P(None, None, None, "head"),
            P(None, "head"),
            P(None, "head", None),
        ),
        out_specs=P(("ctx", "head"), None),
        check_vma=False,
    )
```

time: 127 us -> 114 us (0.90)
  waiting for transfers between devices: 55.2 us -> 35.5 us
  starting transfers between devices: 32.5 us -> 47 us
  local copies, waits for them, and re-layouts: 9.02 us -> 5.14 us
  Pallas kernels: 28.9 us -> 25.3 us
    all_to_all x4 -> x2, waiting for transfers between devices: 31.5 us -> 0.01 us  [to_heads(): lax.all_to_all(fields, 'ctx', 0, 0, axis_index_groups=shard_groups, tiled...]
    ppermute x0 -> x14, starting transfers between devices: none -> 22.7 us  [per_device(): received.append(lax.ppermute(slots[slot], 'ctx', partners))]
    ppermute x0 -> x14, waiting for transfers between devices: none -> 11.1 us  [per_device(): received.append(lax.ppermute(slots[slot], 'ctx', partners))]
    all_to_all x4 -> x2, starting transfers between devices: 17.2 us -> 9.47 us  [to_heads(): lax.all_to_all(fields, 'ctx', 0, 0, axis_index_groups=shard_groups, tiled...]
    pallas_call x2, Pallas kernels: 16.6 us -> 11.6 us  [attention(): pl.pallas_call(kernel, in_specs=[VMEM] * (1 + len(own) + len(others)), ou...]
    squeeze x4 -> x2, local copies, waits for them, and re-layouts: 6.77 us -> 3.66 us  [the longest x1 2.13 us: per_device(): into = into[(layer + 1) % LAYERS]]
    ppermute x2, waiting for transfers between devices: 0.01 us -> 2.42 us  [per_device(): peer = lax.ppermute(residual, 'head', swap)]
    all_to_all x2, waiting for transfers between devices: 19.9 us -> 18.4 us  [per_device(): lax.all_to_all(heads, ('ctx', 'head'), 0, 0, axis_index_groups=row_groups...]
  transfers between devices with their start and end apart: 14 -> 26, of which waited for: 9 -> 13; matrix products, arithmetic and copies ran while one was open for 5% -> 3% of each run, Pallas kernels for 20% -> 18%
where the time goes in v2:
time: 114 us; the launch traced here: 113 us
  starting transfers between devices  47 us (41%)
  waiting for transfers between devices  35.5 us (31%)
  Pallas kernels  25.3 us (22%)
  local copies, waits for them, and re-layouts  5.14 us (5%)
    ppermute x14, starting transfers between devices, per_device(): received.append(lax.ppermute(slots[slot], 'ctx', partners))  22.7 us
    all_to_all x2, waiting for transfers between devices, per_device(): lax.all_to_all(heads, ('ctx', 'head'), 0, 0, axis_index_groups=row_groups...  18.4 us
    pallas_call x5, Pallas kernels, rows_step(): pl.pallas_call(kernel, in_specs=[HBM if itself else VMEM] * count, out_sp...  13.6 us
    pallas_call x2, Pallas kernels, attention(): pl.pallas_call(kernel, in_specs=[VMEM] * (1 + len(own) + len(others)), ou...  11.6 us
    ppermute x14, waiting for transfers between devices, per_device(): received.append(lax.ppermute(slots[slot], 'ctx', partners))  11.1 us
    all_to_all x2, starting transfers between devices, to_heads(): lax.all_to_all(fields, 'ctx', 0, 0, axis_index_groups=shard_groups, tiled...  9.47 us
    all_to_all x2, starting transfers between devices, per_device(): lax.all_to_all(heads, ('ctx', 'head'), 0, 0, axis_index_groups=row_groups...  8.59 us
    ppermute x2, starting transfers between devices, per_device(): peer = lax.ppermute(residual, 'head', swap)  4.02 us
  transfers between devices with their start and end apart: 26, of which 13 were waited for; matrix products, arithmetic and copies ran while one was open for 3% of the time, Pallas kernels for 18%

profile of v2, /device:TPU:0, one launch (start us, length us, event | category | flops | bytes accessed | tf_op | source)
XLA Modules:
  0.0 113.3 jit_solution(673352516640715383)
XLA Ops:
  0.0 2.9 %collective-permute-start = (bf16[128,1024]{1,0:T(8,128)(2,1)}, bf16[128,1024]{1,0:T(8,128)(2,1)S(1)}, u32[]{:S(2)}, u32[]{:S(2)}) collective-permute-start(bf16[128,1024]{1,0:T(8,128)(2,1)} %refs_0_.6), channel_id=1, source_target_pairs={{0,1},{1,0},{2,3},{3,2},{4,5},{5,4},{6,7},{7,6},{8,9},{9,8},{10,11... | collective-permute-start | bytes 786440 | tf_op jit(solution)/shard_map/ppermute | solution.py:278
  2.9 3.2 %shard_map.55 = bf16[8,192,128]{2,1,0:T(8,128)(2,1)} custom-call(bf16[128,1024]{1,0:T(8,128)(2,1)} %refs_0_.6, f32[2,1024]{1,0:T(2,128)} %refs_1_.5, bf16[2,3,1024,512]{3,2,1,0:T(8,128)(2,1)} %refs_4_.4, bf16[2,3,1024,512]{3,2,1,0:T(8,128)(2,1)} %refs_4_.4, bf16[2,3,1024,512]{3,2,1,0:T(8,128)(2,1)} %refs_4_.4), custom_call_target="tpu_custom_call" | custom-call | flops 402653184 | bytes 3145728 | tf_op jit(solution)/shard_map/pallas_call | solution.py:131
  6.2 5.8 %all-to-all-start = ((bf16[8,192,128]{2,1,0:T(8,128)(2,1)}), bf16[8,192,128]{2,1,0:T(8,128)(2,1)S(1)}, u32[]{:S(2)}, u32[]{:S(2)}) async-start(bf16[8,192,128]{2,1,0:T(8,128)(2,1)} %shard_map.55), calls=%async_computation | async-start | bytes 786432 | tf_op jit(solution)/shard_map/all_to_all | solution.py:270
  12.8 3.3 %shard_map.56 = (bf16[192,128]{1,0:T(8,128)(2,1)}, bf16[192,128]{1,0:T(8,128)(2,1)}, bf16[192,128]{1,0:T(8,128)(2,1)}, bf16[192,128]{1,0:T(8,128)(2,1)}, bf16[19...) custom-call(bf16[128,1024]{1,0:T(8,128)(2,1)} %copy-done.6, ...), custom_call_target="tpu_custom_call" | custom-call | flops 8053063680 | bytes 3145728 | tf_op jit(solution)/shard_map/pallas_call | solution.py:131
  16.2 2.1 %collective-permute-start.1 = (bf16[192,128]{1,0:T(8,128)(2,1)}, bf16[192,128]{1,0:T(8,128)(2,1)S(1)}, u32[]{:S(2)}, u32[]{:S(2)}) collective-permute-start(bf16[192,128]{1,0:T(8,128)(2,1)} %get-tuple-element.27), channel_id=1, source_target_pairs={{0,4},{2,6},{4,0},{6,2},{8,12},{10,14},{12,8},{14,10},{16,20},{18,... | collective-permute-start | bytes 147464 | tf_op jit(solution)/shard_map/ppermute | solution.py:285
  21.9 2.9 %collective-permute-start.4 = (bf16[192,128]{1,0:T(8,128)(2,1)S(1)}, bf16[192,128]{1,0:T(8,128)(2,1)S(1)}, u32[]{:S(2)}, u32[]{:S(2)}) collective-permute-start(bf16[192,128]{1,0:T(8,128)(2,1)S(1)} %copy-done.10), channel_id=1, source_target_pairs={{0,16},{2,18},{4,20},{6,22},{8,24},{10,26},{12,28},{14,30},{16,0},... | collective-permute-start | bytes 147464 | tf_op jit(solution)/shard_map/ppermute | solution.py:285
  26.2 3.3 %collective-permute-start.6 = (bf16[192,128]{1,0:T(8,128)(2,1)S(1)}, bf16[192,128]{1,0:T(8,128)(2,1)S(1)}, u32[]{:S(2)}, u32[]{:S(2)}) collective-permute-start(bf16[192,128]{1,0:T(8,128)(2,1)S(1)} %copy-done.8), channel_id=1, source_target_pairs={{0,24},{2,26},{4,28},{6,30},{8,16},{10,18},{12,20},{14,22},{16,8},... | collective-permute-start | bytes 147464 | tf_op jit(solution)/shard_map/ppermute | solution.py:285
  32.6 3.7 %collective-permute-done.7.refs_7_ = bf16[192,128]{1,0:T(8,128)(2,1)S(1)} collective-permute-done((bf16[192,128]{1,0:T(8,128)(2,1)S(1)}, bf16[192,128]{1,0:T(8,128)(2,1)S(1)}, u32[]{:S(2)}, u32[]{:S(2)}) %collective-permute-start.7) | collective-permute-done | bytes 49184 | tf_op jit(solution)/shard_map/ppermute | solution.py:285
  38.6 5.8 %shard_map.58 = bf16[2,8,64,128]{3,2,1,0:T(8,128)(2,1)} custom-call(f32[2,512]{1,0:T(2,128)S(1)} %copy-done.4, bf16[8,192,128]{2,1,0:T(8,128)(2,1)S(1)} %all-to-all-done.refs_1_, bf16[8,192,128]{2,1,0:T(8,128)(2,1)S(1)} %shard_map.57.refs_2_, bf16[8,192,128]{2,1,0:T(8,128)(2,1)S(1)} %collective-permute-done.8.refs_3_, ...), custom_call_target="tpu_custom_call" | custom-call | flops 1207959552 | bytes 2097152 | tf_op jit(solution)/shard_map/pallas_call | solution.py:227
  44.4 4.2 %all-to-all-start.1 = ((bf16[16,64,128]{2,1,0:T(8,128)(2,1)}), bf16[16,64,128]{2,1,0:T(8,128)(2,1)}, u32[]{:S(2)}, u32[]{:S(2)}) async-start(bf16[16,64,128]{2,1,0:T(8,128)(2,1)} %bitcast), calls=%async_computation.1 | async-start | bytes 524288 | tf_op jit(solution)/shard_map/all_to_all | solution.py:303
  48.7 2.1 %slice_bitcast_fusion.refs_5_.refs_2_ = bf16[3,1024,512]{2,1,0:T(8,128)(2,1)S(1)} fusion(bf16[2,3,1024,512]{3,2,1,0:T(8,128)(2,1)} %refs_4_.4), kind=kLoop, calls=%fused_computation | loop fusion | bytes 6291456 | tf_op jit(solution)/shard_map/squeeze | solution.py:301
  50.8 8.3 %all-to-all-done.1 = bf16[16,64,128]{2,1,0:T(8,128)(2,1)} async-done(((bf16[16,64,128]{2,1,0:T(8,128)(2,1)}), bf16[16,64,128]{2,1,0:T(8,128)(2,1)}, u32[]{:S(2)}, u32[]{:S(2)}) %all-to-all-start.1) | async-done | bytes 262176 | tf_op jit(solution)/shard_map/all_to_all | solution.py:303
  59.1 2.8 %shard_map.59 = (bf16[128,1024]{1,0:T(8,128)(2,1)}, bf16[8,192,128]{2,1,0:T(8,128)(2,1)S(1)}) custom-call(bf16[128,1024]{1,0:T(8,128)(2,1)S(1)} %copy-done, bf16[1024,128]{1,0:T(8,128)(2,1)} %bitcast.1.refs_1_, bf16[512,1024]{1,0:T(8,128)(2,1)} %get-tuple-element.34.refs_2_, bf16[512,1024]{1,0:T(8,128)(2,1)} %collective-permute-done.10.refs_3_, ...), custom_call_target="tpu_custom_call" | custom-call | flops 671088640 | bytes 5242880 | tf_op jit(solution)/shard_map/pallas_call | solution.py:131
  63.8 3.6 %all-to-all-start.2 = ((bf16[8,192,128]{2,1,0:T(8,128)(2,1)}), bf16[8,192,128]{2,1,0:T(8,128)(2,1)S(1)}, u32[]{:S(2)}, u32[]{:S(2)}) async-start(bf16[8,192,128]{2,1,0:T(8,128)(2,1)} %copy-done.1), calls=%async_computation.2 | async-start | bytes 786432 | tf_op jit(solution)/shard_map/all_to_all | solution.py:270
  67.4 2.4 %collective-permute-done.11.refs_0_ = bf16[128,1024]{1,0:T(8,128)(2,1)} collective-permute-done((bf16[128,1024]{1,0:T(8,128)(2,1)}, bf16[128,1024]{1,0:T(8,128)(2,1)}, u32[]{:S(2)}, u32[]{:S(2)}) %collective-permute-start.11) | collective-permute-done | bytes 262176 | tf_op jit(solution)/shard_map/ppermute | solution.py:278
  72.8 2.3 %collective-permute-start.14 = (bf16[192,128]{1,0:T(8,128)(2,1)S(1)}, bf16[192,128]{1,0:T(8,128)(2,1)S(1)}, u32[]{:S(2)}, u32[]{:S(2)}) collective-permute-start(bf16[192,128]{1,0:T(8,128)(2,1)S(1)} %get-tuple-element.41), channel_id=1, source_target_pairs={{0,12},{2,14},{4,8},{6,10},{8,4},{10,6},{12,0},{14,2},{16,28},{18,... | collective-permute-start | bytes 147464 | tf_op jit(solution)/shard_map/ppermute | solution.py:285
  77.3 1.8 %collective-permute-start.16 = (bf16[192,128]{1,0:T(8,128)(2,1)S(1)}, bf16[192,128]{1,0:T(8,128)(2,1)S(1)}, u32[]{:S(2)}, u32[]{:S(2)}) collective-permute-start(bf16[192,128]{1,0:T(8,128)(2,1)S(1)} %get-tuple-element.43), channel_id=1, source_target_pairs={{0,20},{2,22},{4,16},{6,18},{8,28},{10,30},{12,24},{14,26},{16,4},... | collective-permute-start | bytes 147464 | tf_op jit(solution)/shard_map/ppermute | solution.py:285
  79.1 2.0 %collective-permute-start.17 = (bf16[192,128]{1,0:T(8,128)(2,1)S(1)}, bf16[192,128]{1,0:T(8,128)(2,1)S(1)}, u32[]{:S(2)}, u32[]{:S(2)}) collective-permute-start(bf16[192,128]{1,0:T(8,128)(2,1)S(1)} %get-tuple-element.44), channel_id=1, source_target_pairs={{0,24},{2,26},{4,28},{6,30},{8,16},{10,18},{12,20},{14,22},{16,8},... | collective-permute-start | bytes 147464 | tf_op jit(solution)/shard_map/ppermute | solution.py:285
  81.2 2.4 %collective-permute-start.18 = (bf16[192,128]{1,0:T(8,128)(2,1)S(1)}, bf16[192,128]{1,0:T(8,128)(2,1)S(1)}, u32[]{:S(2)}, u32[]{:S(2)}) collective-permute-start(bf16[192,128]{1,0:T(8,128)(2,1)S(1)} %get-tuple-element.45), channel_id=1, source_target_pairs={{0,28},{2,30},{4,24},{6,26},{8,20},{10,22},{12,16},{14,18},{16,12}... | collective-permute-start | bytes 147464 | tf_op jit(solution)/shard_map/ppermute | solution.py:285
  85.1 2.9 %collective-permute-done.18.refs_7_ = bf16[192,128]{1,0:T(8,128)(2,1)S(1)} collective-permute-done((bf16[192,128]{1,0:T(8,128)(2,1)S(1)}, bf16[192,128]{1,0:T(8,128)(2,1)S(1)}, u32[]{:S(2)}, u32[]{:S(2)}) %collective-permute-start.18) | collective-permute-done | bytes 49184 | tf_op jit(solution)/shard_map/ppermute | solution.py:285
  90.4 5.8 %shard_map.62 = bf16[2,8,64,128]{3,2,1,0:T(8,128)(2,1)} custom-call(f32[2,512]{1,0:T(2,128)S(1)} %copy-done.4, bf16[8,192,128]{2,1,0:T(8,128)(2,1)S(1)} %all-to-all-done.2.refs_1_, bf16[8,192,128]{2,1,0:T(8,128)(2,1)S(1)} %shard_map.61.refs_2_, bf16[8,192,128]{2,1,0:T(8,128)(2,1)S(1)} %collective-permute-done.19.refs_3_, ...), custom_call_target="tpu_custom_call" | custom-call | flops 1207959552 | bytes 2097152 | tf_op jit(solution)/shard_map/pallas_call | solution.py:227
  96.2 4.4 %all-to-all-start.3 = ((bf16[16,64,128]{2,1,0:T(8,128)(2,1)}), bf16[16,64,128]{2,1,0:T(8,128)(2,1)S(1)}, u32[]{:S(2)}, u32[]{:S(2)}) async-start(bf16[16,64,128]{2,1,0:T(8,128)(2,1)} %bitcast.4), calls=%async_computation.3 | async-start | bytes 524288 | tf_op jit(solution)/shard_map/all_to_all | solution.py:303
  100.6 10.2 %all-to-all-done.3 = bf16[16,64,128]{2,1,0:T(8,128)(2,1)S(1)} async-done(((bf16[16,64,128]{2,1,0:T(8,128)(2,1)}), bf16[16,64,128]{2,1,0:T(8,128)(2,1)S(1)}, u32[]{:S(2)}, u32[]{:S(2)}) %all-to-all-start.3) | async-done | bytes 262176 | tf_op jit(solution)/shard_map/all_to_all | solution.py:303
  110.8 2.5 %shard_map.63 = bf16[128,1024]{1,0:T(8,128)(2,1)} custom-call(bf16[128,1024]{1,0:T(8,128)(2,1)} %get-tuple-element.36.refs_0_, bf16[1024,128]{1,0:T(8,128)(2,1)S(1)} %bitcast.10, bf16[512,1024]{1,0:T(8,128)(2,1)} %get-tuple-element.46.refs_2_, bf16[512,1024]{1,0:T(8,128)(2,1)S(1)} %collective-permute-done.21.refs_3_), custom_call_target="tpu_custom_call" | custom-call | flops 268435456 | bytes 2097152 | tf_op jit(solution)/shard_map/pallas_call | solution.py:131
  (61 shorter events, 22.2 us)
Async XLA Ops:
  0.0 12.0 %collective-permute-start = (bf16[128,1024]{1,0:T(8,128)(2,1)}, bf16[128,1024]{1,0:T(8,128)(2,1)S(1)}, u32[]{:S(2)}, u32[]{:S(2)}) collective-permute-start(bf16[128,1024]{1,0:T(8,128)(2,1)} %refs_0_.6), channel_id=1, source_target_pairs={{0,1},{1,0},{2,3},{3,2},{4,5},{5,4},{6,7},{7,6},{8,9},{9,8},{10,11... | collective-permute-start | bytes 786440 | tf_op jit(solution)/shard_map/ppermute | solution.py:278
  6.2 30.2 %all-to-all-start = ((bf16[8,192,128]{2,1,0:T(8,128)(2,1)}), bf16[8,192,128]{2,1,0:T(8,128)(2,1)S(1)}, u32[]{:S(2)}, u32[]{:S(2)}) async-start(bf16[8,192,128]{2,1,0:T(8,128)(2,1)} %shard_map.55), calls=%async_computation | async-start | bytes 786432 | tf_op jit(solution)/shard_map/all_to_all | solution.py:270
  16.2 8.6 %collective-permute-start.1 = (bf16[192,128]{1,0:T(8,128)(2,1)}, bf16[192,128]{1,0:T(8,128)(2,1)S(1)}, u32[]{:S(2)}, u32[]{:S(2)}) collective-permute-start(bf16[192,128]{1,0:T(8,128)(2,1)} %get-tuple-element.27), channel_id=1, source_target_pairs={{0,4},{2,6},{4,0},{6,2},{8,12},{10,14},{12,8},{14,10},{16,20},{18,... | collective-permute-start | bytes 147464 | tf_op jit(solution)/shard_map/ppermute | solution.py:285
  18.2 7.9 %collective-permute-start.2 = (bf16[192,128]{1,0:T(8,128)(2,1)}, bf16[192,128]{1,0:T(8,128)(2,1)S(1)}, u32[]{:S(2)}, u32[]{:S(2)}) collective-permute-start(bf16[192,128]{1,0:T(8,128)(2,1)} %get-tuple-element.28), channel_id=1, source_target_pairs={{0,8},{2,10},{4,12},{6,14},{8,0},{10,2},{12,4},{14,6},{16,24},{18,... | collective-permute-start | bytes 147464 | tf_op jit(solution)/shard_map/ppermute | solution.py:285
  19.7 9.7 %collective-permute-start.3 = (bf16[192,128]{1,0:T(8,128)(2,1)}, bf16[192,128]{1,0:T(8,128)(2,1)S(1)}, u32[]{:S(2)}, u32[]{:S(2)}) collective-permute-start(bf16[192,128]{1,0:T(8,128)(2,1)} %get-tuple-element.29), channel_id=1, source_target_pairs={{0,12},{2,14},{4,8},{6,10},{8,4},{10,6},{12,0},{14,2},{16,28},{18,... | collective-permute-start | bytes 147464 | tf_op jit(solution)/shard_map/ppermute | solution.py:285
  21.3 29.5 %collective-permute-start.10 = (bf16[512,1024]{1,0:T(8,128)(2,1)}, bf16[512,1024]{1,0:T(8,128)(2,1)}, u32[]{:S(2)}, u32[]{:S(2)}) collective-permute-start(bf16[512,1024]{1,0:T(8,128)(2,1)} %get-tuple-element.34.refs_2_), channel_id=1, source_target_pairs={{0,1},{1,0},{2,3},{3,2},{4,5},{5,4},{6,7},{7,6},{8,9},{9,8},{10,11... | collective-permute-start | bytes 3145736 | tf_op jit(solution)/shard_map/ppermute | solution.py:280
  21.9 7.7 %collective-permute-start.4 = (bf16[192,128]{1,0:T(8,128)(2,1)S(1)}, bf16[192,128]{1,0:T(8,128)(2,1)S(1)}, u32[]{:S(2)}, u32[]{:S(2)}) collective-permute-start(bf16[192,128]{1,0:T(8,128)(2,1)S(1)} %copy-done.10), channel_id=1, source_target_pairs={{0,16},{2,18},{4,20},{6,22},{8,24},{10,26},{12,28},{14,30},{16,0},... | collective-permute-start | bytes 147464 | tf_op jit(solution)/shard_map/ppermute | solution.py:285
  24.7 6.2 %collective-permute-start.5 = (bf16[192,128]{1,0:T(8,128)(2,1)S(1)}, bf16[192,128]{1,0:T(8,128)(2,1)S(1)}, u32[]{:S(2)}, u32[]{:S(2)}) collective-permute-start(bf16[192,128]{1,0:T(8,128)(2,1)S(1)} %copy-done.9), channel_id=1, source_target_pairs={{0,20},{2,22},{4,16},{6,18},{8,28},{10,30},{12,24},{14,26},{16,4},... | collective-permute-start | bytes 147464 | tf_op jit(solution)/shard_map/ppermute | solution.py:285
  26.2 6.4 %collective-permute-start.6 = (bf16[192,128]{1,0:T(8,128)(2,1)S(1)}, bf16[192,128]{1,0:T(8,128)(2,1)S(1)}, u32[]{:S(2)}, u32[]{:S(2)}) collective-permute-start(bf16[192,128]{1,0:T(8,128)(2,1)S(1)} %copy-done.8), channel_id=1, source_target_pairs={{0,24},{2,26},{4,28},{6,30},{8,16},{10,18},{12,20},{14,22},{16,8},... | collective-permute-start | bytes 147464 | tf_op jit(solution)/shard_map/ppermute | solution.py:285
  29.5 6.8 %collective-permute-start.7 = (bf16[192,128]{1,0:T(8,128)(2,1)S(1)}, bf16[192,128]{1,0:T(8,128)(2,1)S(1)}, u32[]{:S(2)}, u32[]{:S(2)}) collective-permute-start(bf16[192,128]{1,0:T(8,128)(2,1)S(1)} %copy-done.7), channel_id=1, source_target_pairs={{0,28},{2,30},{4,24},{6,26},{8,20},{10,22},{12,16},{14,18},{16,12}... | collective-permute-start | bytes 147464 | tf_op jit(solution)/shard_map/ppermute | solution.py:285
  36.4 2.3 %collective-permute-start.8 = (bf16[8,192,128]{2,1,0:T(8,128)(2,1)S(1)}, bf16[8,192,128]{2,1,0:T(8,128)(2,1)S(1)}, u32[]{:S(2)}, u32[]{:S(2)}) collective-permute-start(bf16[8,192,128]{2,1,0:T(8,128)(2,1)S(1)} %all-to-all-done.refs_1_), channel_id=1, source_target_pairs={{0,2},{2,0},{4,6},{6,4},{8,10},{10,8},{12,14},{14,12},{16,18},{18,... | collective-permute-start | bytes 1179656 | tf_op jit(solution)/shard_map/ppermute | solution.py:287
  44.4 14.6 %all-to-all-start.1 = ((bf16[16,64,128]{2,1,0:T(8,128)(2,1)}), bf16[16,64,128]{2,1,0:T(8,128)(2,1)}, u32[]{:S(2)}, u32[]{:S(2)}) async-start(bf16[16,64,128]{2,1,0:T(8,128)(2,1)} %bitcast), calls=%async_computation.1 | async-start | bytes 524288 | tf_op jit(solution)/shard_map/all_to_all | solution.py:303
  62.7 7.1 %collective-permute-start.11 = (bf16[128,1024]{1,0:T(8,128)(2,1)}, bf16[128,1024]{1,0:T(8,128)(2,1)}, u32[]{:S(2)}, u32[]{:S(2)}) collective-permute-start(bf16[128,1024]{1,0:T(8,128)(2,1)} %get-tuple-element.36.refs_0_), channel_id=1, source_target_pairs={{0,1},{1,0},{2,3},{3,2},{4,5},{5,4},{6,7},{7,6},{8,9},{9,8},{10,11... | collective-permute-start | bytes 786440 | tf_op jit(solution)/shard_map/ppermute | solution.py:278
  63.8 24.3 %all-to-all-start.2 = ((bf16[8,192,128]{2,1,0:T(8,128)(2,1)}), bf16[8,192,128]{2,1,0:T(8,128)(2,1)S(1)}, u32[]{:S(2)}, u32[]{:S(2)}) async-start(bf16[8,192,128]{2,1,0:T(8,128)(2,1)} %copy-done.1), calls=%async_computation.2 | async-start | bytes 786432 | tf_op jit(solution)/shard_map/all_to_all | solution.py:270
  71.5 5.8 %collective-permute-start.12 = (bf16[192,128]{1,0:T(8,128)(2,1)S(1)}, bf16[192,128]{1,0:T(8,128)(2,1)S(1)}, u32[]{:S(2)}, u32[]{:S(2)}) collective-permute-start(bf16[192,128]{1,0:T(8,128)(2,1)S(1)} %get-tuple-element.39), channel_id=1, source_target_pairs={{0,4},{2,6},{4,0},{6,2},{8,12},{10,14},{12,8},{14,10},{16,20},{18,... | collective-permute-start | bytes 147464 | tf_op jit(solution)/shard_map/ppermute | solution.py:285
  72.8 6.4 %collective-permute-start.13 = (bf16[192,128]{1,0:T(8,128)(2,1)S(1)}, bf16[192,128]{1,0:T(8,128)(2,1)S(1)}, u32[]{:S(2)}, u32[]{:S(2)}) collective-permute-start(bf16[192,128]{1,0:T(8,128)(2,1)S(1)} %get-tuple-element.40), channel_id=1, source_target_pairs={{0,8},{2,10},{4,12},{6,14},{8,0},{10,2},{12,4},{14,6},{16,24},{18,... | collective-permute-start | bytes 147464 | tf_op jit(solution)/shard_map/ppermute | solution.py:285
  72.8 8.4 %collective-permute-start.14 = (bf16[192,128]{1,0:T(8,128)(2,1)S(1)}, bf16[192,128]{1,0:T(8,128)(2,1)S(1)}, u32[]{:S(2)}, u32[]{:S(2)}) collective-permute-start(bf16[192,128]{1,0:T(8,128)(2,1)S(1)} %get-tuple-element.41), channel_id=1, source_target_pairs={{0,12},{2,14},{4,8},{6,10},{8,4},{10,6},{12,0},{14,2},{16,28},{18,... | collective-permute-start | bytes 147464 | tf_op jit(solution)/shard_map/ppermute | solution.py:285
  75.1 25.5 %collective-permute-start.21 = (bf16[512,1024]{1,0:T(8,128)(2,1)}, bf16[512,1024]{1,0:T(8,128)(2,1)S(1)}, u32[]{:S(2)}, u32[]{:S(2)}) collective-permute-start(bf16[512,1024]{1,0:T(8,128)(2,1)} %get-tuple-element.46.refs_2_), channel_id=1, source_target_pairs={{0,1},{1,0},{2,3},{3,2},{4,5},{5,4},{6,7},{7,6},{8,9},{9,8},{10,11... | collective-permute-start | bytes 3145736 | tf_op jit(solution)/shard_map/ppermute | solution.py:280
  75.7 7.8 %collective-permute-start.15 = (bf16[192,128]{1,0:T(8,128)(2,1)S(1)}, bf16[192,128]{1,0:T(8,128)(2,1)S(1)}, u32[]{:S(2)}, u32[]{:S(2)}) collective-permute-start(bf16[192,128]{1,0:T(8,128)(2,1)S(1)} %get-tuple-element.42), channel_id=1, source_target_pairs={{0,16},{2,18},{4,20},{6,22},{8,24},{10,26},{12,28},{14,30},{16,0},... | collective-permute-start | bytes 147464 | tf_op jit(solution)/shard_map/ppermute | solution.py:285
  77.3 7.4 %collective-permute-start.16 = (bf16[192,128]{1,0:T(8,128)(2,1)S(1)}, bf16[192,128]{1,0:T(8,128)(2,1)S(1)}, u32[]{:S(2)}, u32[]{:S(2)}) collective-permute-start(bf16[192,128]{1,0:T(8,128)(2,1)S(1)} %get-tuple-element.43), channel_id=1, source_target_pairs={{0,20},{2,22},{4,16},{6,18},{8,28},{10,30},{12,24},{14,26},{16,4},... | collective-permute-start | bytes 147464 | tf_op jit(solution)/shard_map/ppermute | solution.py:285
  79.1 6.0 %collective-permute-start.17 = (bf16[192,128]{1,0:T(8,128)(2,1)S(1)}, bf16[192,128]{1,0:T(8,128)(2,1)S(1)}, u32[]{:S(2)}, u32[]{:S(2)}) collective-permute-start(bf16[192,128]{1,0:T(8,128)(2,1)S(1)} %get-tuple-element.44), channel_id=1, source_target_pairs={{0,24},{2,26},{4,28},{6,30},{8,16},{10,18},{12,20},{14,22},{16,8},... | collective-permute-start | bytes 147464 | tf_op jit(solution)/shard_map/ppermute | solution.py:285
  81.2 6.8 %collective-permute-start.18 = (bf16[192,128]{1,0:T(8,128)(2,1)S(1)}, bf16[192,128]{1,0:T(8,128)(2,1)S(1)}, u32[]{:S(2)}, u32[]{:S(2)}) collective-permute-start(bf16[192,128]{1,0:T(8,128)(2,1)S(1)} %get-tuple-element.45), channel_id=1, source_target_pairs={{0,28},{2,30},{4,24},{6,26},{8,20},{10,22},{12,16},{14,18},{16,12}... | collective-permute-start | bytes 147464 | tf_op jit(solution)/shard_map/ppermute | solution.py:285
  88.1 2.3 %collective-permute-start.19 = (bf16[8,192,128]{2,1,0:T(8,128)(2,1)S(1)}, bf16[8,192,128]{2,1,0:T(8,128)(2,1)S(1)}, u32[]{:S(2)}, u32[]{:S(2)}) collective-permute-start(bf16[8,192,128]{2,1,0:T(8,128)(2,1)S(1)} %all-to-all-done.2.refs_1_), channel_id=1, source_target_pairs={{0,2},{2,0},{4,6},{6,4},{8,10},{10,8},{12,14},{14,12},{16,18},{18,... | collective-permute-start | bytes 1179656 | tf_op jit(solution)/shard_map/ppermute | solution.py:287
  96.2 14.6 %all-to-all-start.3 = ((bf16[16,64,128]{2,1,0:T(8,128)(2,1)}), bf16[16,64,128]{2,1,0:T(8,128)(2,1)S(1)}, u32[]{:S(2)}, u32[]{:S(2)}) async-start(bf16[16,64,128]{2,1,0:T(8,128)(2,1)} %bitcast.4), calls=%async_computation.3 | async-start | bytes 524288 | tf_op jit(solution)/shard_map/all_to_all | solution.py:303
  (13 other events, 114.0 us)

commit v3 on v2

--- a/solution.py
+++ b/solution.py
@@ -75,7 +75,7 @@
     return total.astype(jnp.bfloat16)
 
 
-def rows_step(residual, mixed=(), onward=(), place=None, slots=False, weight=1):
+def rows_step(residual, mixed=(), onward=(), place=None, slots=False, weight=1, keep=False):
     rows, width = residual.shape
     operands, views, shapes, outs = [residual], [None], [(residual.shape, jnp.bfloat16)], []
     flops, itself = 0, False
@@ -84,7 +84,7 @@
         operands += [entries] + list(parts)
         views += [None] + [index if len(part.shape) == 3 else None for part in parts]
         shapes += [(entries.shape, jnp.bfloat16)] + [(part.shape[-2:], jnp.bfloat16) for part in parts]
-        outs.append(jax.ShapeDtypeStruct(residual.shape, jnp.bfloat16))
+        outs.append((pltpu.VMEM if onward else jax.ShapeDtypeStruct)(residual.shape, jnp.bfloat16))
         flops += 2 * rows * width * entries.shape[0]
     if onward:
         layer, gain, project_in = onward
@@ -92,9 +92,11 @@
         itself = len(project_in.shape) == 4
         operands += [gain] + [project_in] * (3 if itself else 1)
         views += [None] + [(layer, which) for which in range(3)]
-        shapes += [(gain.shape, jnp.float32)] + [(project_in.shape[2:], jnp.bfloat16)] * 3
+        shapes += [(gain.shape, jnp.float32)] + [(project_in.shape[2:], jnp.bfloat16)] * (0 if keep else 3)
         shape, heads = (3 * HD, rows), columns // HD
-        outs += [jax.ShapeDtypeStruct(shape if slots else (heads, *shape), jnp.bfloat16)] * (heads if slots else 1)
+        outs += [pltpu.VMEM(shape if slots else (heads, *shape), jnp.bfloat16)] * (heads if slots else 1)
+        if keep:
+            outs.append(pltpu.VMEM(project_in.shape[1:], jnp.bfloat16))
         flops += 6 * rows * width * columns
     count = len(operands)
     scratch = [pltpu.VMEM(*shape) for shape in shapes] + [pltpu.SemaphoreType.DMA((count,))] if itself else []
@@ -104,6 +106,9 @@
     def kernel(*refs):
         sources, results, held = refs[:count], list(refs[count : count + len(outs)]), refs[count + len(outs) :]
         flat = refs[-1] if slots else None
+        if keep:
+            kept = results.pop()
+            held = (*held[: count - 3], *(kept.at[which] for which in range(3)), *held[count - 3 :])
         if itself:
             pairs = [(ref if view is None else ref.at[view], to) for ref, view, to in zip(sources, views, held)]
             copies = fetch(pairs, held[count])
@@ -128,13 +133,15 @@
 
             project_rows(current.astype(jnp.float32), scale, weights, flat, place, results)
 
+    if itself:
+        operands = [pltpu.with_memory_space_constraint(operand, pltpu.HBM) for operand in operands]
     return pl.pallas_call(
         kernel,
         in_specs=[HBM if itself else VMEM] * count,
         out_specs=[VMEM] * len(outs),
         out_shape=outs,
         scratch_shapes=scratch,
-        compiler_params=params(59 if itself else 16),
+        compiler_params=params(16),
         cost_estimate=pl.CostEstimate(flops=flops * weight, bytes_accessed=flops // rows, transcendentals=0),
     )(*operands)
 
@@ -148,7 +155,7 @@
         kernel,
         in_specs=[VMEM] * len(slots),
         out_specs=VMEM,
-        out_shape=jax.ShapeDtypeStruct((len(slots), *slots[0].shape), slots[0].dtype),
+        out_shape=pltpu.VMEM((len(slots), *slots[0].shape), slots[0].dtype),
         compiler_params=params(8),
         cost_estimate=pl.CostEstimate(flops=0, bytes_accessed=4 * len(slots) * slots[0].size, transcendentals=0),
     )(*slots)
@@ -270,13 +277,12 @@
         return lax.all_to_all(fields, "ctx", 0, 0, axis_index_groups=shard_groups, tiled=True)
 
     if paired:
-        (fields,) = rows_step(residual, onward=(0, input_gain, project_in), place=place)
-    before, into = None, project_in
+        fields, into = rows_step(residual, onward=(0, input_gain, project_in), place=place, keep=True)
     for layer in range(LAYERS):
-        out = project_out[layer]
         if paired:
             peer = lax.ppermute(residual, "head", swap)
-            out, _ = lax.optimization_barrier((out, peer if before is None else before))
+            before = peer if layer == 0 else before
+            out, _ = lax.optimization_barrier((project_out[layer], before))
             weights_out = [out, lax.ppermute(out, "head", swap)]
             slots = rows_step(peer, (), (layer, input_gain, into), place, True, 20)
             received = [slots[0]]
@@ -284,10 +290,10 @@
                 partners = [(c, c ^ (replicas * slot)) for c in range(shards)]
                 received.append(lax.ppermute(slots[slot], "ctx", partners))
             own = [to_heads(fields), assemble(received, place)]
+            before = own[1]
             others = [lax.ppermute(chunk, "ctx", neighbours) for chunk in own]
-            before = own[1]
         else:
-            weights_out = [lax.all_gather(out, "head", axis=0, tiled=True)]
+            weights_out = [lax.all_gather(project_out[layer], "head", axis=0, tiled=True)]
             gathered = lax.all_gather(residual, "head", axis=0, tiled=True)
             own = [to_heads(project(gathered, input_gain, project_in[layer], layer, place))]
             others = []

time: 114 us -> 112 us (0.982)
  Pallas kernels: 25.3 us -> 23.8 us
    pallas_call x5, Pallas kernels: 13.6 us -> 12.1 us  [rows_step(): pl.pallas_call(kernel, in_specs=[HBM if itself else VMEM] * count, out_sp...]
  transfers between devices with their start and end apart: 26 -> 26, of which waited for: 13 -> 12; matrix products, arithmetic and copies ran while one was open for 3% -> 3% of each run, Pallas kernels for 18% -> 17%
where the time goes in v3:
time: 112 us; the launch traced here: 111 us
  starting transfers between devices  47.1 us (42%)
  waiting for transfers between devices  35.5 us (32%)
  Pallas kernels  23.8 us (21%)
  local copies, waits for them, and re-layouts  4.44 us (4%)
    ppermute x14, starting transfers between devices, per_device(): received.append(lax.ppermute(slots[slot], 'ctx', partners))  22.6 us
    all_to_all x2, waiting for transfers between devices, per_device(): lax.all_to_all(heads, ('ctx', 'head'), 0, 0, axis_index_groups=row_groups...  18.4 us
    pallas_call x5, Pallas kernels, rows_step(): pl.pallas_call(kernel, in_specs=[HBM if itself else VMEM] * count, out_sp...  12.1 us
    pallas_call x2, Pallas kernels, attention(): pl.pallas_call(kernel, in_specs=[VMEM] * (1 + len(own) + len(others)), ou...  11.6 us
    ppermute x14, waiting for transfers between devices, per_device(): received.append(lax.ppermute(slots[slot], 'ctx', partners))  11.1 us
    all_to_all x2, starting transfers between devices, to_heads(): lax.all_to_all(fields, 'ctx', 0, 0, axis_index_groups=shard_groups, tiled...  9.48 us
    all_to_all x2, starting transfers between devices, per_device(): lax.all_to_all(heads, ('ctx', 'head'), 0, 0, axis_index_groups=row_groups...  8.6 us
    ppermute x2, starting transfers between devices, per_device(): peer = lax.ppermute(residual, 'head', swap)  4.04 us
  transfers between devices with their start and end apart: 26, of which 12 were waited for; matrix products, arithmetic and copies ran while one was open for 3% of the time, Pallas kernels for 17%

profile of v3, /device:TPU:0, one launch (start us, length us, event | category | flops | bytes accessed | tf_op | source)
XLA Modules:
  0.0 111.0 jit_solution(5672747538322948940)
XLA Ops:
  0.0 2.9 %collective-permute-start = (bf16[128,1024]{1,0:T(8,128)(2,1)}, bf16[128,1024]{1,0:T(8,128)(2,1)}, u32[]{:S(2)}, u32[]{:S(2)}) collective-permute-start(bf16[128,1024]{1,0:T(8,128)(2,1)} %refs_0_.6), channel_id=1, source_target_pairs={{0,1},{1,0},{2,3},{3,2},{4,5},{5,4},{6,7},{7,6},{8,9},{9,8},{10,11... | collective-permute-start | bytes 786440 | tf_op jit(solution)/shard_map/ppermute | solution.py:283
  2.9 3.3 %shard_map.55 = (bf16[8,192,128]{2,1,0:T(8,128)(2,1)}, bf16[3,1024,512]{2,1,0:T(8,128)(2,1)S(1)}) custom-call(bf16[128,1024]{1,0:T(8,128)(2,1)} %refs_0_.6, f32[2,1024]{1,0:T(2,128)} %refs_1_.5, bf16[2,3,1024,512]{3,2,1,0:T(8,128)(2,1)} %refs_4_.2, bf16[2,3,1024,512]{3,2,1,0:T(8,128)(2,1)} %refs_4_.2, bf16[2,3,1024,512]{3,2,1,0:T(8,128)(2,1)} %refs_4_.2), custom_call_target="tpu_custom_call" | custom-call | flops 402653184 | bytes 3145728 | tf_op jit(solution)/shard_map/pallas_call | solution.py:138
  6.2 5.8 %all-to-all-start = ((bf16[8,192,128]{2,1,0:T(8,128)(2,1)}), bf16[8,192,128]{2,1,0:T(8,128)(2,1)S(1)}, u32[]{:S(2)}, u32[]{:S(2)}) async-start(bf16[8,192,128]{2,1,0:T(8,128)(2,1)} %get-tuple-element.28), calls=%async_computation | async-start | bytes 786432 | tf_op jit(solution)/shard_map/all_to_all | solution.py:277
  12.1 1.9 %shard_map.56 = (bf16[192,128]{1,0:T(8,128)(2,1)S(1)}, bf16[192,128]{1,0:T(8,128)(2,1)S(1)}, bf16[192,128]{1,0:T(8,128)(2,1)S(1)}, bf16[192,128]{1,0:T(8,128)(2,...) custom-call(bf16[128,1024]{1,0:T(8,128)(2,1)} %collective-permute-do, ...), custom_call_target="tpu_custom_call" | custom-call | flops 8053063680 | bytes 3145728 | tf_op jit(solution)/shard_map/pallas_call | solution.py:138
  14.0 2.1 %collective-permute-start.1 = (bf16[192,128]{1,0:T(8,128)(2,1)S(1)}, bf16[192,128]{1,0:T(8,128)(2,1)S(1)}, u32[]{:S(2)}, u32[]{:S(2)}) collective-permute-start(bf16[192,128]{1,0:T(8,128)(2,1)S(1)} %get-tuple-element.31), channel_id=1, source_target_pairs={{0,4},{2,6},{4,0},{6,2},{8,12},{10,14},{12,8},{14,10},{16,20},{18,... | collective-permute-start | bytes 147464 | tf_op jit(solution)/shard_map/ppermute | solution.py:291
  19.7 2.8 %collective-permute-start.4 = (bf16[192,128]{1,0:T(8,128)(2,1)S(1)}, bf16[192,128]{1,0:T(8,128)(2,1)S(1)}, u32[]{:S(2)}, u32[]{:S(2)}) collective-permute-start(bf16[192,128]{1,0:T(8,128)(2,1)S(1)} %get-tuple-element.34), channel_id=1, source_target_pairs={{0,16},{2,18},{4,20},{6,22},{8,24},{10,26},{12,28},{14,30},{16,0},... | collective-permute-start | bytes 147464 | tf_op jit(solution)/shard_map/ppermute | solution.py:291
  24.0 3.3 %collective-permute-start.6 = (bf16[192,128]{1,0:T(8,128)(2,1)S(1)}, bf16[192,128]{1,0:T(8,128)(2,1)S(1)}, u32[]{:S(2)}, u32[]{:S(2)}) collective-permute-start(bf16[192,128]{1,0:T(8,128)(2,1)S(1)} %get-tuple-element.36), channel_id=1, source_target_pairs={{0,24},{2,26},{4,28},{6,30},{8,16},{10,18},{12,20},{14,22},{16,8},... | collective-permute-start | bytes 147464 | tf_op jit(solution)/shard_map/ppermute | solution.py:291
  27.3 3.7 %collective-permute-done.5.refs_5_ = bf16[192,128]{1,0:T(8,128)(2,1)S(1)} collective-permute-done((bf16[192,128]{1,0:T(8,128)(2,1)S(1)}, bf16[192,128]{1,0:T(8,128)(2,1)S(1)}, u32[]{:S(2)}, u32[]{:S(2)}) %collective-permute-start.5) | collective-permute-done | bytes 49184 | tf_op jit(solution)/shard_map/ppermute | solution.py:291
  31.0 3.0 %collective-permute-done.7.refs_7_ = bf16[192,128]{1,0:T(8,128)(2,1)S(1)} collective-permute-done((bf16[192,128]{1,0:T(8,128)(2,1)S(1)}, bf16[192,128]{1,0:T(8,128)(2,1)S(1)}, u32[]{:S(2)}, u32[]{:S(2)}) %collective-permute-start.7) | collective-permute-done | bytes 49184 | tf_op jit(solution)/shard_map/ppermute | solution.py:291
  36.4 5.8 %shard_map.58 = bf16[2,8,64,128]{3,2,1,0:T(8,128)(2,1)} custom-call(f32[2,512]{1,0:T(2,128)S(1)} %copy-done.3, bf16[8,192,128]{2,1,0:T(8,128)(2,1)S(1)} %all-to-all-done.refs_1_, bf16[8,192,128]{2,1,0:T(8,128)(2,1)S(1)} %shard_map.57.refs_2_, bf16[8,192,128]{2,1,0:T(8,128)(2,1)S(1)} %collective-permute-done.8.refs_3_, ...), custom_call_target="tpu_custom_call" | custom-call | flops 1207959552 | bytes 2097152 | tf_op jit(solution)/shard_map/pallas_call | solution.py:234
  42.2 4.2 %all-to-all-start.1 = ((bf16[16,64,128]{2,1,0:T(8,128)(2,1)}), bf16[16,64,128]{2,1,0:T(8,128)(2,1)}, u32[]{:S(2)}, u32[]{:S(2)}) async-start(bf16[16,64,128]{2,1,0:T(8,128)(2,1)} %bitcast), calls=%async_computation.1 | async-start | bytes 524288 | tf_op jit(solution)/shard_map/all_to_all | solution.py:309
  46.4 2.1 %slice_bitcast_fusion.refs_5_.refs_2_ = bf16[3,1024,512]{2,1,0:T(8,128)(2,1)S(1)} fusion(bf16[2,3,1024,512]{3,2,1,0:T(8,128)(2,1)} %refs_4_.2), kind=kLoop, calls=%fused_computation | loop fusion | bytes 6291456 | tf_op jit(solution)/shard_map/squeeze | solution.py:307
  48.6 8.3 %all-to-all-done.1 = bf16[16,64,128]{2,1,0:T(8,128)(2,1)} async-done(((bf16[16,64,128]{2,1,0:T(8,128)(2,1)}), bf16[16,64,128]{2,1,0:T(8,128)(2,1)}, u32[]{:S(2)}, u32[]{:S(2)}) %all-to-all-start.1) | async-done | bytes 262176 | tf_op jit(solution)/shard_map/all_to_all | solution.py:309
  56.9 2.8 %shard_map.59 = (bf16[128,1024]{1,0:T(8,128)(2,1)}, bf16[8,192,128]{2,1,0:T(8,128)(2,1)S(1)}) custom-call(bf16[128,1024]{1,0:T(8,128)(2,1)S(1)} %copy-done, bf16[1024,128]{1,0:T(8,128)(2,1)} %bitcast.1.refs_1_, bf16[512,1024]{1,0:T(8,128)(2,1)} %get-tuple-element.38.refs_2_, bf16[512,1024]{1,0:T(8,128)(2,1)} %collective-permute-done.10.refs_3_, ...), custom_call_target="tpu_custom_call" | custom-call | flops 671088640 | bytes 5242880 | tf_op jit(solution)/shard_map/pallas_call | solution.py:138
  61.6 3.6 %all-to-all-start.2 = ((bf16[8,192,128]{2,1,0:T(8,128)(2,1)}), bf16[8,192,128]{2,1,0:T(8,128)(2,1)S(1)}, u32[]{:S(2)}, u32[]{:S(2)}) async-start(bf16[8,192,128]{2,1,0:T(8,128)(2,1)} %copy-done.1), calls=%async_computation.2 | async-start | bytes 786432 | tf_op jit(solution)/shard_map/all_to_all | solution.py:277
  65.2 2.4 %collective-permute-done.11.refs_0_ = bf16[128,1024]{1,0:T(8,128)(2,1)} collective-permute-done((bf16[128,1024]{1,0:T(8,128)(2,1)}, bf16[128,1024]{1,0:T(8,128)(2,1)}, u32[]{:S(2)}, u32[]{:S(2)}) %collective-permute-start.11) | collective-permute-done | bytes 262176 | tf_op jit(solution)/shard_map/ppermute | solution.py:283
  70.6 2.3 %collective-permute-start.14 = (bf16[192,128]{1,0:T(8,128)(2,1)S(1)}, bf16[192,128]{1,0:T(8,128)(2,1)S(1)}, u32[]{:S(2)}, u32[]{:S(2)}) collective-permute-start(bf16[192,128]{1,0:T(8,128)(2,1)S(1)} %get-tuple-element.45), channel_id=1, source_target_pairs={{0,12},{2,14},{4,8},{6,10},{8,4},{10,6},{12,0},{14,2},{16,28},{18,... | collective-permute-start | bytes 147464 | tf_op jit(solution)/shard_map/ppermute | solution.py:291
  76.9 2.0 %collective-permute-start.17 = (bf16[192,128]{1,0:T(8,128)(2,1)S(1)}, bf16[192,128]{1,0:T(8,128)(2,1)S(1)}, u32[]{:S(2)}, u32[]{:S(2)}) collective-permute-start(bf16[192,128]{1,0:T(8,128)(2,1)S(1)} %get-tuple-element.48), channel_id=1, source_target_pairs={{0,24},{2,26},{4,28},{6,30},{8,16},{10,18},{12,20},{14,22},{16,8},... | collective-permute-start | bytes 147464 | tf_op jit(solution)/shard_map/ppermute | solution.py:291
  79.0 2.4 %collective-permute-start.18 = (bf16[192,128]{1,0:T(8,128)(2,1)S(1)}, bf16[192,128]{1,0:T(8,128)(2,1)S(1)}, u32[]{:S(2)}, u32[]{:S(2)}) collective-permute-start(bf16[192,128]{1,0:T(8,128)(2,1)S(1)} %get-tuple-element.49), channel_id=1, source_target_pairs={{0,28},{2,30},{4,24},{6,26},{8,20},{10,22},{12,16},{14,18},{16,12}... | collective-permute-start | bytes 147464 | tf_op jit(solution)/shard_map/ppermute | solution.py:291
  82.9 2.8 %collective-permute-done.18.refs_7_ = bf16[192,128]{1,0:T(8,128)(2,1)S(1)} collective-permute-done((bf16[192,128]{1,0:T(8,128)(2,1)S(1)}, bf16[192,128]{1,0:T(8,128)(2,1)S(1)}, u32[]{:S(2)}, u32[]{:S(2)}) %collective-permute-start.18) | collective-permute-done | bytes 49184 | tf_op jit(solution)/shard_map/ppermute | solution.py:291
  88.1 5.8 %shard_map.62 = bf16[2,8,64,128]{3,2,1,0:T(8,128)(2,1)} custom-call(f32[2,512]{1,0:T(2,128)S(1)} %copy-done.3, bf16[8,192,128]{2,1,0:T(8,128)(2,1)S(1)} %all-to-all-done.2.refs_1_, bf16[8,192,128]{2,1,0:T(8,128)(2,1)S(1)} %shard_map.61.refs_2_, bf16[8,192,128]{2,1,0:T(8,128)(2,1)S(1)} %collective-permute-done.19.refs_3_, ...), custom_call_target="tpu_custom_call" | custom-call | flops 1207959552 | bytes 2097152 | tf_op jit(solution)/shard_map/pallas_call | solution.py:234
  93.9 4.4 %all-to-all-start.3 = ((bf16[16,64,128]{2,1,0:T(8,128)(2,1)}), bf16[16,64,128]{2,1,0:T(8,128)(2,1)S(1)}, u32[]{:S(2)}, u32[]{:S(2)}) async-start(bf16[16,64,128]{2,1,0:T(8,128)(2,1)} %bitcast.4), calls=%async_computation.3 | async-start | bytes 524288 | tf_op jit(solution)/shard_map/all_to_all | solution.py:309
  98.4 10.2 %all-to-all-done.3 = bf16[16,64,128]{2,1,0:T(8,128)(2,1)S(1)} async-done(((bf16[16,64,128]{2,1,0:T(8,128)(2,1)}), bf16[16,64,128]{2,1,0:T(8,128)(2,1)S(1)}, u32[]{:S(2)}, u32[]{:S(2)}) %all-to-all-start.3) | async-done | bytes 262176 | tf_op jit(solution)/shard_map/all_to_all | solution.py:309
  108.5 2.5 %shard_map.63 = bf16[128,1024]{1,0:T(8,128)(2,1)} custom-call(bf16[128,1024]{1,0:T(8,128)(2,1)} %get-tuple-element.40.refs_0_, bf16[1024,128]{1,0:T(8,128)(2,1)S(1)} %bitcast.10, bf16[512,1024]{1,0:T(8,128)(2,1)} %get-tuple-element.50.refs_2_, bf16[512,1024]{1,0:T(8,128)(2,1)S(1)} %collective-permute-done.21.refs_3_), custom_call_target="tpu_custom_call" | custom-call | flops 268435456 | bytes 2097152 | tf_op jit(solution)/shard_map/pallas_call | solution.py:138
  (49 shorter events, 20.4 us)
Async XLA Ops:
  0.0 12.1 %collective-permute-start = (bf16[128,1024]{1,0:T(8,128)(2,1)}, bf16[128,1024]{1,0:T(8,128)(2,1)}, u32[]{:S(2)}, u32[]{:S(2)}) collective-permute-start(bf16[128,1024]{1,0:T(8,128)(2,1)} %refs_0_.6), channel_id=1, source_target_pairs={{0,1},{1,0},{2,3},{3,2},{4,5},{5,4},{6,7},{7,6},{8,9},{9,8},{10,11... | collective-permute-start | bytes 786440 | tf_op jit(solution)/shard_map/ppermute | solution.py:283
  6.2 27.9 %all-to-all-start = ((bf16[8,192,128]{2,1,0:T(8,128)(2,1)}), bf16[8,192,128]{2,1,0:T(8,128)(2,1)S(1)}, u32[]{:S(2)}, u32[]{:S(2)}) async-start(bf16[8,192,128]{2,1,0:T(8,128)(2,1)} %get-tuple-element.28), calls=%async_computation | async-start | bytes 786432 | tf_op jit(solution)/shard_map/all_to_all | solution.py:277
  14.0 8.6 %collective-permute-start.1 = (bf16[192,128]{1,0:T(8,128)(2,1)S(1)}, bf16[192,128]{1,0:T(8,128)(2,1)S(1)}, u32[]{:S(2)}, u32[]{:S(2)}) collective-permute-start(bf16[192,128]{1,0:T(8,128)(2,1)S(1)} %get-tuple-element.31), channel_id=1, source_target_pairs={{0,4},{2,6},{4,0},{6,2},{8,12},{10,14},{12,8},{14,10},{16,20},{18,... | collective-permute-start | bytes 147464 | tf_op jit(solution)/shard_map/ppermute | solution.py:291
  16.0 7.9 %collective-permute-start.2 = (bf16[192,128]{1,0:T(8,128)(2,1)S(1)}, bf16[192,128]{1,0:T(8,128)(2,1)S(1)}, u32[]{:S(2)}, u32[]{:S(2)}) collective-permute-start(bf16[192,128]{1,0:T(8,128)(2,1)S(1)} %get-tuple-element.32), channel_id=1, source_target_pairs={{0,8},{2,10},{4,12},{6,14},{8,0},{10,2},{12,4},{14,6},{16,24},{18,... | collective-permute-start | bytes 147464 | tf_op jit(solution)/shard_map/ppermute | solution.py:291
  17.5 9.7 %collective-permute-start.3 = (bf16[192,128]{1,0:T(8,128)(2,1)S(1)}, bf16[192,128]{1,0:T(8,128)(2,1)S(1)}, u32[]{:S(2)}, u32[]{:S(2)}) collective-permute-start(bf16[192,128]{1,0:T(8,128)(2,1)S(1)} %get-tuple-element.33), channel_id=1, source_target_pairs={{0,12},{2,14},{4,8},{6,10},{8,4},{10,6},{12,0},{14,2},{16,28},{18,... | collective-permute-start | bytes 147464 | tf_op jit(solution)/shard_map/ppermute | solution.py:291
  19.1 29.5 %collective-permute-start.10 = (bf16[512,1024]{1,0:T(8,128)(2,1)}, bf16[512,1024]{1,0:T(8,128)(2,1)}, u32[]{:S(2)}, u32[]{:S(2)}) collective-permute-start(bf16[512,1024]{1,0:T(8,128)(2,1)} %get-tuple-element.38.refs_2_), channel_id=1, source_target_pairs={{0,1},{1,0},{2,3},{3,2},{4,5},{5,4},{6,7},{7,6},{8,9},{9,8},{10,11... | collective-permute-start | bytes 3145736 | tf_op jit(solution)/shard_map/ppermute | solution.py:286
  19.7 7.7 %collective-permute-start.4 = (bf16[192,128]{1,0:T(8,128)(2,1)S(1)}, bf16[192,128]{1,0:T(8,128)(2,1)S(1)}, u32[]{:S(2)}, u32[]{:S(2)}) collective-permute-start(bf16[192,128]{1,0:T(8,128)(2,1)S(1)} %get-tuple-element.34), channel_id=1, source_target_pairs={{0,16},{2,18},{4,20},{6,22},{8,24},{10,26},{12,28},{14,30},{16,0},... | collective-permute-start | bytes 147464 | tf_op jit(solution)/shard_map/ppermute | solution.py:291
  22.5 8.5 %collective-permute-start.5 = (bf16[192,128]{1,0:T(8,128)(2,1)S(1)}, bf16[192,128]{1,0:T(8,128)(2,1)S(1)}, u32[]{:S(2)}, u32[]{:S(2)}) collective-permute-start(bf16[192,128]{1,0:T(8,128)(2,1)S(1)} %get-tuple-element.35), channel_id=1, source_target_pairs={{0,20},{2,22},{4,16},{6,18},{8,28},{10,30},{12,24},{14,26},{16,4},... | collective-permute-start | bytes 147464 | tf_op jit(solution)/shard_map/ppermute | solution.py:291
  24.0 7.0 %collective-permute-start.6 = (bf16[192,128]{1,0:T(8,128)(2,1)S(1)}, bf16[192,128]{1,0:T(8,128)(2,1)S(1)}, u32[]{:S(2)}, u32[]{:S(2)}) collective-permute-start(bf16[192,128]{1,0:T(8,128)(2,1)S(1)} %get-tuple-element.36), channel_id=1, source_target_pairs={{0,24},{2,26},{4,28},{6,30},{8,16},{10,18},{12,20},{14,22},{16,8},... | collective-permute-start | bytes 147464 | tf_op jit(solution)/shard_map/ppermute | solution.py:291
  27.3 6.8 %collective-permute-start.7 = (bf16[192,128]{1,0:T(8,128)(2,1)S(1)}, bf16[192,128]{1,0:T(8,128)(2,1)S(1)}, u32[]{:S(2)}, u32[]{:S(2)}) collective-permute-start(bf16[192,128]{1,0:T(8,128)(2,1)S(1)} %get-tuple-element.37), channel_id=1, source_target_pairs={{0,28},{2,30},{4,24},{6,26},{8,20},{10,22},{12,16},{14,18},{16,12}... | collective-permute-start | bytes 147464 | tf_op jit(solution)/shard_map/ppermute | solution.py:291
  34.2 2.3 %collective-permute-start.8 = (bf16[8,192,128]{2,1,0:T(8,128)(2,1)S(1)}, bf16[8,192,128]{2,1,0:T(8,128)(2,1)S(1)}, u32[]{:S(2)}, u32[]{:S(2)}) collective-permute-start(bf16[8,192,128]{2,1,0:T(8,128)(2,1)S(1)} %all-to-all-done.refs_1_), channel_id=1, source_target_pairs={{0,2},{2,0},{4,6},{6,4},{8,10},{10,8},{12,14},{14,12},{16,18},{18,... | collective-permute-start | bytes 1179656 | tf_op jit(solution)/shard_map/ppermute | solution.py:294
  42.2 14.6 %all-to-all-start.1 = ((bf16[16,64,128]{2,1,0:T(8,128)(2,1)}), bf16[16,64,128]{2,1,0:T(8,128)(2,1)}, u32[]{:S(2)}, u32[]{:S(2)}) async-start(bf16[16,64,128]{2,1,0:T(8,128)(2,1)} %bitcast), calls=%async_computation.1 | async-start | bytes 524288 | tf_op jit(solution)/shard_map/all_to_all | solution.py:309
  60.5 7.1 %collective-permute-start.11 = (bf16[128,1024]{1,0:T(8,128)(2,1)}, bf16[128,1024]{1,0:T(8,128)(2,1)}, u32[]{:S(2)}, u32[]{:S(2)}) collective-permute-start(bf16[128,1024]{1,0:T(8,128)(2,1)} %get-tuple-element.40.refs_0_), channel_id=1, source_target_pairs={{0,1},{1,0},{2,3},{3,2},{4,5},{5,4},{6,7},{7,6},{8,9},{9,8},{10,11... | collective-permute-start | bytes 786440 | tf_op jit(solution)/shard_map/ppermute | solution.py:283
  61.6 24.3 %all-to-all-start.2 = ((bf16[8,192,128]{2,1,0:T(8,128)(2,1)}), bf16[8,192,128]{2,1,0:T(8,128)(2,1)S(1)}, u32[]{:S(2)}, u32[]{:S(2)}) async-start(bf16[8,192,128]{2,1,0:T(8,128)(2,1)} %copy-done.1), calls=%async_computation.2 | async-start | bytes 786432 | tf_op jit(solution)/shard_map/all_to_all | solution.py:277
  69.3 5.8 %collective-permute-start.12 = (bf16[192,128]{1,0:T(8,128)(2,1)S(1)}, bf16[192,128]{1,0:T(8,128)(2,1)S(1)}, u32[]{:S(2)}, u32[]{:S(2)}) collective-permute-start(bf16[192,128]{1,0:T(8,128)(2,1)S(1)} %get-tuple-element.43), channel_id=1, source_target_pairs={{0,4},{2,6},{4,0},{6,2},{8,12},{10,14},{12,8},{14,10},{16,20},{18,... | collective-permute-start | bytes 147464 | tf_op jit(solution)/shard_map/ppermute | solution.py:291
  70.6 6.4 %collective-permute-start.13 = (bf16[192,128]{1,0:T(8,128)(2,1)S(1)}, bf16[192,128]{1,0:T(8,128)(2,1)S(1)}, u32[]{:S(2)}, u32[]{:S(2)}) collective-permute-start(bf16[192,128]{1,0:T(8,128)(2,1)S(1)} %get-tuple-element.44), channel_id=1, source_target_pairs={{0,8},{2,10},{4,12},{6,14},{8,0},{10,2},{12,4},{14,6},{16,24},{18,... | collective-permute-start | bytes 147464 | tf_op jit(solution)/shard_map/ppermute | solution.py:291
  70.6 8.4 %collective-permute-start.14 = (bf16[192,128]{1,0:T(8,128)(2,1)S(1)}, bf16[192,128]{1,0:T(8,128)(2,1)S(1)}, u32[]{:S(2)}, u32[]{:S(2)}) collective-permute-start(bf16[192,128]{1,0:T(8,128)(2,1)S(1)} %get-tuple-element.45), channel_id=1, source_target_pairs={{0,12},{2,14},{4,8},{6,10},{8,4},{10,6},{12,0},{14,2},{16,28},{18,... | collective-permute-start | bytes 147464 | tf_op jit(solution)/shard_map/ppermute | solution.py:291
  72.9 25.5 %collective-permute-start.21 = (bf16[512,1024]{1,0:T(8,128)(2,1)}, bf16[512,1024]{1,0:T(8,128)(2,1)S(1)}, u32[]{:S(2)}, u32[]{:S(2)}) collective-permute-start(bf16[512,1024]{1,0:T(8,128)(2,1)} %get-tuple-element.50.refs_2_), channel_id=1, source_target_pairs={{0,1},{1,0},{2,3},{3,2},{4,5},{5,4},{6,7},{7,6},{8,9},{9,8},{10,11... | collective-permute-start | bytes 3145736 | tf_op jit(solution)/shard_map/ppermute | solution.py:286
  73.5 7.8 %collective-permute-start.15 = (bf16[192,128]{1,0:T(8,128)(2,1)S(1)}, bf16[192,128]{1,0:T(8,128)(2,1)S(1)}, u32[]{:S(2)}, u32[]{:S(2)}) collective-permute-start(bf16[192,128]{1,0:T(8,128)(2,1)S(1)} %get-tuple-element.46), channel_id=1, source_target_pairs={{0,16},{2,18},{4,20},{6,22},{8,24},{10,26},{12,28},{14,30},{16,0},... | collective-permute-start | bytes 147464 | tf_op jit(solution)/shard_map/ppermute | solution.py:291
  75.1 7.4 %collective-permute-start.16 = (bf16[192,128]{1,0:T(8,128)(2,1)S(1)}, bf16[192,128]{1,0:T(8,128)(2,1)S(1)}, u32[]{:S(2)}, u32[]{:S(2)}) collective-permute-start(bf16[192,128]{1,0:T(8,128)(2,1)S(1)} %get-tuple-element.47), channel_id=1, source_target_pairs={{0,20},{2,22},{4,16},{6,18},{8,28},{10,30},{12,24},{14,26},{16,4},... | collective-permute-start | bytes 147464 | tf_op jit(solution)/shard_map/ppermute | solution.py:291
  76.9 6.0 %collective-permute-start.17 = (bf16[192,128]{1,0:T(8,128)(2,1)S(1)}, bf16[192,128]{1,0:T(8,128)(2,1)S(1)}, u32[]{:S(2)}, u32[]{:S(2)}) collective-permute-start(bf16[192,128]{1,0:T(8,128)(2,1)S(1)} %get-tuple-element.48), channel_id=1, source_target_pairs={{0,24},{2,26},{4,28},{6,30},{8,16},{10,18},{12,20},{14,22},{16,8},... | collective-permute-start | bytes 147464 | tf_op jit(solution)/shard_map/ppermute | solution.py:291
  79.0 6.8 %collective-permute-start.18 = (bf16[192,128]{1,0:T(8,128)(2,1)S(1)}, bf16[192,128]{1,0:T(8,128)(2,1)S(1)}, u32[]{:S(2)}, u32[]{:S(2)}) collective-permute-start(bf16[192,128]{1,0:T(8,128)(2,1)S(1)} %get-tuple-element.49), channel_id=1, source_target_pairs={{0,28},{2,30},{4,24},{6,26},{8,20},{10,22},{12,16},{14,18},{16,12}... | collective-permute-start | bytes 147464 | tf_op jit(solution)/shard_map/ppermute | solution.py:291
  85.9 2.3 %collective-permute-start.19 = (bf16[8,192,128]{2,1,0:T(8,128)(2,1)S(1)}, bf16[8,192,128]{2,1,0:T(8,128)(2,1)S(1)}, u32[]{:S(2)}, u32[]{:S(2)}) collective-permute-start(bf16[8,192,128]{2,1,0:T(8,128)(2,1)S(1)} %all-to-all-done.2.refs_1_), channel_id=1, source_target_pairs={{0,2},{2,0},{4,6},{6,4},{8,10},{10,8},{12,14},{14,12},{16,18},{18,... | collective-permute-start | bytes 1179656 | tf_op jit(solution)/shard_map/ppermute | solution.py:294
  93.9 14.6 %all-to-all-start.3 = ((bf16[16,64,128]{2,1,0:T(8,128)(2,1)}), bf16[16,64,128]{2,1,0:T(8,128)(2,1)S(1)}, u32[]{:S(2)}, u32[]{:S(2)}) async-start(bf16[16,64,128]{2,1,0:T(8,128)(2,1)} %bitcast.4), calls=%async_computation.3 | async-start | bytes 524288 | tf_op jit(solution)/shard_map/all_to_all | solution.py:309
  (7 other events, 54.9 us)

commit v4 on v3

--- a/solution.py
+++ b/solution.py
@@ -146,9 +146,15 @@
     )(*operands)
 
 
+def slot_order(count):
+    return [*range(count // 2), *range(count - 1, count // 2 - 1, -1)]
+
+
 def assemble(slots, place):
+    order = slot_order(len(slots))
+
     def kernel(*refs):
-        for slot, ref in enumerate(refs[:-1]):
+        for slot, ref in zip(order, refs):
             refs[-1][place()[0] ^ slot] = ref[...]
 
     return pl.pallas_call(
@@ -158,7 +164,7 @@
         out_shape=pltpu.VMEM((len(slots), *slots[0].shape), slots[0].dtype),
         compiler_params=params(8),
         cost_estimate=pl.CostEstimate(flops=0, bytes_accessed=4 * len(slots) * slots[0].size, transcendentals=0),
-    )(*slots)
+    )(*(slots[slot] for slot in order))
 
 
 def attention_kernel(layer, own_count, start, place, gain_ref, *refs):
@@ -281,16 +287,16 @@
     for layer in range(LAYERS):
         if paired:
             peer = lax.ppermute(residual, "head", swap)
-            before = peer if layer == 0 else before
-            out, _ = lax.optimization_barrier((project_out[layer], before))
+            if layer == 0:
+                out, _ = lax.optimization_barrier((project_out, peer))
+                out = out[0]
             weights_out = [out, lax.ppermute(out, "head", swap)]
             slots = rows_step(peer, (), (layer, input_gain, into), place, True, 20)
-            received = [slots[0]]
-            for slot in range(1, local_heads):
+            received = list(slots)
+            for slot in slot_order(local_heads)[1:]:
                 partners = [(c, c ^ (replicas * slot)) for c in range(shards)]
-                received.append(lax.ppermute(slots[slot], "ctx", partners))
+                received[slot] = lax.ppermute(slots[slot], "ctx", partners)
             own = [to_heads(fields), assemble(received, place)]
-            before = own[1]
             others = [lax.ppermute(chunk, "ctx", neighbours) for chunk in own]
         else:
             weights_out = [lax.all_gather(project_out[layer], "head", axis=0, tiled=True)]
@@ -303,8 +309,8 @@
                     others = [lax.ppermute(own[0], "ctx", neighbours)]
         heads = attention(layer, replicas, output_gain, own, others, first_place, place, split)
         if paired:
-            into, _ = lax.optimization_barrier((project_in, heads))
-            into = into[(layer + 1) % LAYERS]
+            into, out, _ = lax.optimization_barrier((project_in, project_out, heads))
+            into, out = into[(layer + 1) % LAYERS], out[(layer + 1) % LAYERS]
         heads = heads.reshape(split * local_heads, HD, tokens // split)
         mixed = lax.all_to_all(heads, ("ctx", "head"), 0, 0, axis_index_groups=row_groups, tiled=True)
         mixed = (mixed.reshape(split * depth, tokens // split), layer, weights_out, weight_starts)

time: 112 us -> 109 us (0.973)
  waiting for transfers between devices: 35.5 us -> 31.4 us
  starting transfers between devices: 47.1 us -> 49.2 us
    ppermute x14, waiting for transfers between devices: 11.1 us -> 7.72 us  [per_device(): received[slot] = lax.ppermute(slots[slot], 'ctx', partners)]
    all_to_all x2, starting transfers between devices: 8.6 us -> 10.4 us  [per_device(): lax.all_to_all(heads, ('ctx', 'head'), 0, 0, axis_index_groups=row_groups...]
    squeeze x2 -> x3, local copies, waits for them, and re-layouts: 3.67 us -> 3.25 us  [the longest x2 2.21 us: per_device(): into, out = (into[(layer + 1) % LAYERS], out[(layer + 1) % LAYERS])]
where the time goes in v4:
time: 109 us; the launch traced here: 108 us
  starting transfers between devices  49.2 us (45%)
  waiting for transfers between devices  31.4 us (29%)
  Pallas kernels  23.4 us (21%)
  local copies, waits for them, and re-layouts  4.03 us (4%)
    ppermute x14, starting transfers between devices, per_device(): received[slot] = lax.ppermute(slots[slot], 'ctx', partners)  22.5 us
    all_to_all x2, waiting for transfers between devices, per_device(): lax.all_to_all(heads, ('ctx', 'head'), 0, 0, axis_index_groups=row_groups...  18.2 us
    pallas_call x5, Pallas kernels, rows_step(): pl.pallas_call(kernel, in_specs=[HBM if itself else VMEM] * count, out_sp...  11.8 us
    pallas_call x2, Pallas kernels, attention(): pl.pallas_call(kernel, in_specs=[VMEM] * (1 + len(own) + len(others)), ou...  11.6 us
    all_to_all x2, starting transfers between devices, per_device(): lax.all_to_all(heads, ('ctx', 'head'), 0, 0, axis_index_groups=row_groups...  10.4 us
    all_to_all x2, starting transfers between devices, to_heads(): lax.all_to_all(fields, 'ctx', 0, 0, axis_index_groups=shard_groups, tiled...  9.48 us
    ppermute x14, waiting for transfers between devices, per_device(): received[slot] = lax.ppermute(slots[slot], 'ctx', partners)  7.72 us
    ppermute x2, starting transfers between devices, per_device(): peer = lax.ppermute(residual, 'head', swap)  4.02 us
  transfers between devices with their start and end apart: 26, of which 12 were waited for; matrix products, arithmetic and copies ran while one was open for 3% of the time, Pallas kernels for 17%

profile of v4, /device:TPU:0, one launch (start us, length us, event | category | flops | bytes accessed | tf_op | source)
XLA Modules:
  0.0 108.2 jit_solution(7304864570948951767)
XLA Ops:
  0.0 2.9 %collective-permute-start = (bf16[128,1024]{1,0:T(8,128)(2,1)}, bf16[128,1024]{1,0:T(8,128)(2,1)}, u32[]{:S(2)}, u32[]{:S(2)}) collective-permute-start(bf16[128,1024]{1,0:T(8,128)(2,1)} %refs_0_.6), channel_id=1, source_target_pairs={{0,1},{1,0},{2,3},{3,2},{4,5},{5,4},{6,7},{7,6},{8,9},{9,8},{10,11... | collective-permute-start | bytes 786440 | tf_op jit(solution)/shard_map/ppermute | solution.py:289
  2.9 3.3 %shard_map.55 = (bf16[8,192,128]{2,1,0:T(8,128)(2,1)}, bf16[3,1024,512]{2,1,0:T(8,128)(2,1)S(1)}) custom-call(bf16[128,1024]{1,0:T(8,128)(2,1)} %refs_0_.6, f32[2,1024]{1,0:T(2,128)} %refs_1_.5, bf16[2,3,1024,512]{3,2,1,0:T(8,128)(2,1)} %refs_4_.2, bf16[2,3,1024,512]{3,2,1,0:T(8,128)(2,1)} %refs_4_.2, bf16[2,3,1024,512]{3,2,1,0:T(8,128)(2,1)} %refs_4_.2), custom_call_target="tpu_custom_call" | custom-call | flops 402653184 | bytes 3145728 | tf_op jit(solution)/shard_map/pallas_call | solution.py:138
  6.2 5.8 %all-to-all-start = ((bf16[8,192,128]{2,1,0:T(8,128)(2,1)}), bf16[8,192,128]{2,1,0:T(8,128)(2,1)S(1)}, u32[]{:S(2)}, u32[]{:S(2)}) async-start(bf16[8,192,128]{2,1,0:T(8,128)(2,1)} %get-tuple-element.28), calls=%async_computation | async-start | bytes 786432 | tf_op jit(solution)/shard_map/all_to_all | solution.py:283
  12.1 1.8 %shard_map.56 = (bf16[192,128]{1,0:T(8,128)(2,1)S(1)}, bf16[192,128]{1,0:T(8,128)(2,1)S(1)}, bf16[192,128]{1,0:T(8,128)(2,1)S(1)}, bf16[192,128]{1,0:T(8,128)(2,...) custom-call(bf16[128,1024]{1,0:T(8,128)(2,1)} %collective-permute-do, ...), custom_call_target="tpu_custom_call" | custom-call | flops 8053063680 | bytes 3145728 | tf_op jit(solution)/shard_map/pallas_call | solution.py:138
  13.9 2.1 %collective-permute-start.1 = (bf16[192,128]{1,0:T(8,128)(2,1)S(1)}, bf16[192,128]{1,0:T(8,128)(2,1)S(1)}, u32[]{:S(2)}, u32[]{:S(2)}) collective-permute-start(bf16[192,128]{1,0:T(8,128)(2,1)S(1)} %get-tuple-element.31), channel_id=1, source_target_pairs={{0,4},{2,6},{4,0},{6,2},{8,12},{10,14},{12,8},{14,10},{16,20},{18,... | collective-permute-start | bytes 147464 | tf_op jit(solution)/shard_map/ppermute | solution.py:298
  19.2 4.6 %collective-permute-start.4 = (bf16[192,128]{1,0:T(8,128)(2,1)S(1)}, bf16[192,128]{1,0:T(8,128)(2,1)S(1)}, u32[]{:S(2)}, u32[]{:S(2)}) collective-permute-start(bf16[192,128]{1,0:T(8,128)(2,1)S(1)} %get-tuple-element.34), channel_id=1, source_target_pairs={{0,28},{2,30},{4,24},{6,26},{8,20},{10,22},{12,16},{14,18},{16,12}... | collective-permute-start | bytes 147464 | tf_op jit(solution)/shard_map/ppermute | solution.py:298
  27.0 2.7 %collective-permute-done.5.refs_5_ = bf16[192,128]{1,0:T(8,128)(2,1)S(1)} collective-permute-done((bf16[192,128]{1,0:T(8,128)(2,1)S(1)}, bf16[192,128]{1,0:T(8,128)(2,1)S(1)}, u32[]{:S(2)}, u32[]{:S(2)}) %collective-permute-start.5) | collective-permute-done | bytes 49184 | tf_op jit(solution)/shard_map/ppermute | solution.py:298
  29.7 2.0 %collective-permute-done.6.refs_6_ = bf16[192,128]{1,0:T(8,128)(2,1)S(1)} collective-permute-done((bf16[192,128]{1,0:T(8,128)(2,1)S(1)}, bf16[192,128]{1,0:T(8,128)(2,1)S(1)}, u32[]{:S(2)}, u32[]{:S(2)}) %collective-permute-start.6) | collective-permute-done | bytes 49184 | tf_op jit(solution)/shard_map/ppermute | solution.py:298
  34.1 5.8 %shard_map.58 = bf16[2,8,64,128]{3,2,1,0:T(8,128)(2,1)} custom-call(f32[2,512]{1,0:T(2,128)S(1)} %copy-done.3, bf16[8,192,128]{2,1,0:T(8,128)(2,1)S(1)} %all-to-all-done.refs_1_, bf16[8,192,128]{2,1,0:T(8,128)(2,1)S(1)} %shard_map.57.refs_2_, bf16[8,192,128]{2,1,0:T(8,128)(2,1)S(1)} %collective-permute-done.8.refs_3_, ...), custom_call_target="tpu_custom_call" | custom-call | flops 1207959552 | bytes 2097152 | tf_op jit(solution)/shard_map/pallas_call | solution.py:240
  39.9 5.2 %all-to-all-start.1 = ((bf16[16,64,128]{2,1,0:T(8,128)(2,1)}), bf16[16,64,128]{2,1,0:T(8,128)(2,1)}, u32[]{:S(2)}, u32[]{:S(2)}) async-start(bf16[16,64,128]{2,1,0:T(8,128)(2,1)} %bitcast), calls=%async_computation.1 | async-start | bytes 524288 | tf_op jit(solution)/shard_map/all_to_all | solution.py:315
  45.2 2.1 %slice_bitcast_fusion.refs_5_.refs_2_ = bf16[3,1024,512]{2,1,0:T(8,128)(2,1)S(1)} fusion(bf16[2,3,1024,512]{3,2,1,0:T(8,128)(2,1)} %refs_4_.2), kind=kLoop, calls=%fused_computation | loop fusion | bytes 6291456 | tf_op jit(solution)/shard_map/squeeze | solution.py:313
  47.3 8.1 %all-to-all-done.1 = bf16[16,64,128]{2,1,0:T(8,128)(2,1)} async-done(((bf16[16,64,128]{2,1,0:T(8,128)(2,1)}), bf16[16,64,128]{2,1,0:T(8,128)(2,1)}, u32[]{:S(2)}, u32[]{:S(2)}) %all-to-all-start.1) | async-done | bytes 262176 | tf_op jit(solution)/shard_map/all_to_all | solution.py:315
  55.4 2.8 %shard_map.59 = (bf16[128,1024]{1,0:T(8,128)(2,1)}, bf16[8,192,128]{2,1,0:T(8,128)(2,1)S(1)}) custom-call(bf16[128,1024]{1,0:T(8,128)(2,1)S(1)} %copy-done, bf16[1024,128]{1,0:T(8,128)(2,1)} %bitcast.1.refs_1_, bf16[512,1024]{1,0:T(8,128)(2,1)} %slice_bitcast_fusion.2.refs_2_, bf16[512,1024]{1,0:T(8,128)(2,1)} %collective-permute-done.10.refs_3_, ...), custom_call_target="tpu_custom_call" | custom-call | flops 671088640 | bytes 5242880 | tf_op jit(solution)/shard_map/pallas_call | solution.py:138
  60.0 3.6 %all-to-all-start.2 = ((bf16[8,192,128]{2,1,0:T(8,128)(2,1)}), bf16[8,192,128]{2,1,0:T(8,128)(2,1)S(1)}, u32[]{:S(2)}, u32[]{:S(2)}) async-start(bf16[8,192,128]{2,1,0:T(8,128)(2,1)} %copy-done.1), calls=%async_computation.2 | async-start | bytes 786432 | tf_op jit(solution)/shard_map/all_to_all | solution.py:283
  63.7 2.0 %collective-permute-done.11.refs_0_ = bf16[128,1024]{1,0:T(8,128)(2,1)} collective-permute-done((bf16[128,1024]{1,0:T(8,128)(2,1)}, bf16[128,1024]{1,0:T(8,128)(2,1)}, u32[]{:S(2)}, u32[]{:S(2)}) %collective-permute-start.11) | collective-permute-done | bytes 262176 | tf_op jit(solution)/shard_map/ppermute | solution.py:289
  69.0 1.9 %collective-permute-start.14 = (bf16[192,128]{1,0:T(8,128)(2,1)S(1)}, bf16[192,128]{1,0:T(8,128)(2,1)S(1)}, u32[]{:S(2)}, u32[]{:S(2)}) collective-permute-start(bf16[192,128]{1,0:T(8,128)(2,1)S(1)} %get-tuple-element.45), channel_id=1, source_target_pairs={{0,12},{2,14},{4,8},{6,10},{8,4},{10,6},{12,0},{14,2},{16,28},{18,... | collective-permute-start | bytes 147464 | tf_op jit(solution)/shard_map/ppermute | solution.py:298
  72.1 2.5 %collective-permute-start.15 = (bf16[192,128]{1,0:T(8,128)(2,1)S(1)}, bf16[192,128]{1,0:T(8,128)(2,1)S(1)}, u32[]{:S(2)}, u32[]{:S(2)}) collective-permute-start(bf16[192,128]{1,0:T(8,128)(2,1)S(1)} %get-tuple-element.46), channel_id=1, source_target_pairs={{0,28},{2,30},{4,24},{6,26},{8,20},{10,22},{12,16},{14,18},{16,12}... | collective-permute-start | bytes 147464 | tf_op jit(solution)/shard_map/ppermute | solution.py:298
  74.7 1.8 %collective-permute-start.16 = (bf16[192,128]{1,0:T(8,128)(2,1)S(1)}, bf16[192,128]{1,0:T(8,128)(2,1)S(1)}, u32[]{:S(2)}, u32[]{:S(2)}) collective-permute-start(bf16[192,128]{1,0:T(8,128)(2,1)S(1)} %get-tuple-element.47), channel_id=1, source_target_pairs={{0,24},{2,26},{4,28},{6,30},{8,16},{10,18},{12,20},{14,22},{16,8},... | collective-permute-start | bytes 147464 | tf_op jit(solution)/shard_map/ppermute | solution.py:298
  76.6 3.2 %collective-permute-start.18 = (bf16[192,128]{1,0:T(8,128)(2,1)S(1)}, bf16[192,128]{1,0:T(8,128)(2,1)S(1)}, u32[]{:S(2)}, u32[]{:S(2)}) collective-permute-start(bf16[192,128]{1,0:T(8,128)(2,1)S(1)} %get-tuple-element.49), channel_id=1, source_target_pairs={{0,16},{2,18},{4,20},{6,22},{8,24},{10,26},{12,28},{14,30},{16,0},... | collective-permute-start | bytes 147464 | tf_op jit(solution)/shard_map/ppermute | solution.py:298
  80.5 2.0 %collective-permute-done.17.refs_6_ = bf16[192,128]{1,0:T(8,128)(2,1)S(1)} collective-permute-done((bf16[192,128]{1,0:T(8,128)(2,1)S(1)}, bf16[192,128]{1,0:T(8,128)(2,1)S(1)}, u32[]{:S(2)}, u32[]{:S(2)}) %collective-permute-start.17) | collective-permute-done | bytes 49184 | tf_op jit(solution)/shard_map/ppermute | solution.py:298
  85.0 5.8 %shard_map.62 = bf16[2,8,64,128]{3,2,1,0:T(8,128)(2,1)} custom-call(f32[2,512]{1,0:T(2,128)S(1)} %copy-done.3, bf16[8,192,128]{2,1,0:T(8,128)(2,1)S(1)} %all-to-all-done.2.refs_1_, bf16[8,192,128]{2,1,0:T(8,128)(2,1)S(1)} %shard_map.61.refs_2_, bf16[8,192,128]{2,1,0:T(8,128)(2,1)S(1)} %collective-permute-done.19.refs_3_, ...), custom_call_target="tpu_custom_call" | custom-call | flops 1207959552 | bytes 2097152 | tf_op jit(solution)/shard_map/pallas_call | solution.py:240
  90.8 5.2 %all-to-all-start.3 = ((bf16[16,64,128]{2,1,0:T(8,128)(2,1)}), bf16[16,64,128]{2,1,0:T(8,128)(2,1)S(1)}, u32[]{:S(2)}, u32[]{:S(2)}) async-start(bf16[16,64,128]{2,1,0:T(8,128)(2,1)} %bitcast.4), calls=%async_computation.3 | async-start | bytes 524288 | tf_op jit(solution)/shard_map/all_to_all | solution.py:315
  95.9 10.2 %all-to-all-done.3 = bf16[16,64,128]{2,1,0:T(8,128)(2,1)S(1)} async-done(((bf16[16,64,128]{2,1,0:T(8,128)(2,1)}), bf16[16,64,128]{2,1,0:T(8,128)(2,1)S(1)}, u32[]{:S(2)}, u32[]{:S(2)}) %all-to-all-start.3) | async-done | bytes 262176 | tf_op jit(solution)/shard_map/all_to_all | solution.py:315
  106.1 2.1 %shard_map.63 = bf16[128,1024]{1,0:T(8,128)(2,1)} custom-call(bf16[128,1024]{1,0:T(8,128)(2,1)} %get-tuple-element.40.refs_0_, bf16[1024,128]{1,0:T(8,128)(2,1)S(1)} %bitcast.10, bf16[512,1024]{1,0:T(8,128)(2,1)S(1)} %slice_bitcast_fusion.1.refs_2_, bf16[512,1024]{1,0:T(8,128)(2,1)S(1)} %collective-permute-done.21.refs_3_), custom_call_target="tpu_custom_call" | custom-call | flops 268435456 | bytes 2097152 | tf_op jit(solution)/shard_map/pallas_call | solution.py:138
  (52 shorter events, 18.4 us)
Async XLA Ops:
  0.0 12.1 %collective-permute-start = (bf16[128,1024]{1,0:T(8,128)(2,1)}, bf16[128,1024]{1,0:T(8,128)(2,1)}, u32[]{:S(2)}, u32[]{:S(2)}) collective-permute-start(bf16[128,1024]{1,0:T(8,128)(2,1)} %refs_0_.6), channel_id=1, source_target_pairs={{0,1},{1,0},{2,3},{3,2},{4,5},{5,4},{6,7},{7,6},{8,9},{9,8},{10,11... | collective-permute-start | bytes 786440 | tf_op jit(solution)/shard_map/ppermute | solution.py:289
  6.2 25.7 %all-to-all-start = ((bf16[8,192,128]{2,1,0:T(8,128)(2,1)}), bf16[8,192,128]{2,1,0:T(8,128)(2,1)S(1)}, u32[]{:S(2)}, u32[]{:S(2)}) async-start(bf16[8,192,128]{2,1,0:T(8,128)(2,1)} %get-tuple-element.28), calls=%async_computation | async-start | bytes 786432 | tf_op jit(solution)/shard_map/all_to_all | solution.py:283
  13.9 9.9 %collective-permute-start.1 = (bf16[192,128]{1,0:T(8,128)(2,1)S(1)}, bf16[192,128]{1,0:T(8,128)(2,1)S(1)}, u32[]{:S(2)}, u32[]{:S(2)}) collective-permute-start(bf16[192,128]{1,0:T(8,128)(2,1)S(1)} %get-tuple-element.31), channel_id=1, source_target_pairs={{0,4},{2,6},{4,0},{6,2},{8,12},{10,14},{12,8},{14,10},{16,20},{18,... | collective-permute-start | bytes 147464 | tf_op jit(solution)/shard_map/ppermute | solution.py:298
  16.0 8.4 %collective-permute-start.2 = (bf16[192,128]{1,0:T(8,128)(2,1)S(1)}, bf16[192,128]{1,0:T(8,128)(2,1)S(1)}, u32[]{:S(2)}, u32[]{:S(2)}) collective-permute-start(bf16[192,128]{1,0:T(8,128)(2,1)S(1)} %get-tuple-element.32), channel_id=1, source_target_pairs={{0,8},{2,10},{4,12},{6,14},{8,0},{10,2},{12,4},{14,6},{16,24},{18,... | collective-permute-start | bytes 147464 | tf_op jit(solution)/shard_map/ppermute | solution.py:298
  17.5 8.4 %collective-permute-start.3 = (bf16[192,128]{1,0:T(8,128)(2,1)S(1)}, bf16[192,128]{1,0:T(8,128)(2,1)S(1)}, u32[]{:S(2)}, u32[]{:S(2)}) collective-permute-start(bf16[192,128]{1,0:T(8,128)(2,1)S(1)} %get-tuple-element.33), channel_id=1, source_target_pairs={{0,12},{2,14},{4,8},{6,10},{8,4},{10,6},{12,0},{14,2},{16,28},{18,... | collective-permute-start | bytes 147464 | tf_op jit(solution)/shard_map/ppermute | solution.py:298
  18.6 28.7 %collective-permute-start.10 = (bf16[512,1024]{1,0:T(8,128)(2,1)}, bf16[512,1024]{1,0:T(8,128)(2,1)}, u32[]{:S(2)}, u32[]{:S(2)}) collective-permute-start(bf16[512,1024]{1,0:T(8,128)(2,1)} %slice_bitcast_fusion.2.refs_2_), channel_id=1, source_target_pairs={{0,1},{1,0},{2,3},{3,2},{4,5},{5,4},{6,7},{7,6},{8,9},{9,8},{10,11... | collective-permute-start | bytes 3145736 | tf_op jit(solution)/shard_map/ppermute | solution.py:293
  19.2 7.8 %collective-permute-start.4 = (bf16[192,128]{1,0:T(8,128)(2,1)S(1)}, bf16[192,128]{1,0:T(8,128)(2,1)S(1)}, u32[]{:S(2)}, u32[]{:S(2)}) collective-permute-start(bf16[192,128]{1,0:T(8,128)(2,1)S(1)} %get-tuple-element.34), channel_id=1, source_target_pairs={{0,28},{2,30},{4,24},{6,26},{8,20},{10,22},{12,16},{14,18},{16,12}... | collective-permute-start | bytes 147464 | tf_op jit(solution)/shard_map/ppermute | solution.py:298
  23.8 5.9 %collective-permute-start.5 = (bf16[192,128]{1,0:T(8,128)(2,1)S(1)}, bf16[192,128]{1,0:T(8,128)(2,1)S(1)}, u32[]{:S(2)}, u32[]{:S(2)}) collective-permute-start(bf16[192,128]{1,0:T(8,128)(2,1)S(1)} %get-tuple-element.35), channel_id=1, source_target_pairs={{0,24},{2,26},{4,28},{6,30},{8,16},{10,18},{12,20},{14,22},{16,8},... | collective-permute-start | bytes 147464 | tf_op jit(solution)/shard_map/ppermute | solution.py:298
  24.4 7.4 %collective-permute-start.6 = (bf16[192,128]{1,0:T(8,128)(2,1)S(1)}, bf16[192,128]{1,0:T(8,128)(2,1)S(1)}, u32[]{:S(2)}, u32[]{:S(2)}) collective-permute-start(bf16[192,128]{1,0:T(8,128)(2,1)S(1)} %get-tuple-element.36), channel_id=1, source_target_pairs={{0,20},{2,22},{4,16},{6,18},{8,28},{10,30},{12,24},{14,26},{16,4},... | collective-permute-start | bytes 147464 | tf_op jit(solution)/shard_map/ppermute | solution.py:298
  25.9 5.9 %collective-permute-start.7 = (bf16[192,128]{1,0:T(8,128)(2,1)S(1)}, bf16[192,128]{1,0:T(8,128)(2,1)S(1)}, u32[]{:S(2)}, u32[]{:S(2)}) collective-permute-start(bf16[192,128]{1,0:T(8,128)(2,1)S(1)} %get-tuple-element.37), channel_id=1, source_target_pairs={{0,16},{2,18},{4,20},{6,22},{8,24},{10,26},{12,28},{14,30},{16,0},... | collective-permute-start | bytes 147464 | tf_op jit(solution)/shard_map/ppermute | solution.py:298
  31.9 2.3 %collective-permute-start.8 = (bf16[8,192,128]{2,1,0:T(8,128)(2,1)S(1)}, bf16[8,192,128]{2,1,0:T(8,128)(2,1)S(1)}, u32[]{:S(2)}, u32[]{:S(2)}) collective-permute-start(bf16[8,192,128]{2,1,0:T(8,128)(2,1)S(1)} %all-to-all-done.refs_1_), channel_id=1, source_target_pairs={{0,2},{2,0},{4,6},{6,4},{8,10},{10,8},{12,14},{14,12},{16,18},{18,... | collective-permute-start | bytes 1179656 | tf_op jit(solution)/shard_map/ppermute | solution.py:300
  39.9 15.4 %all-to-all-start.1 = ((bf16[16,64,128]{2,1,0:T(8,128)(2,1)}), bf16[16,64,128]{2,1,0:T(8,128)(2,1)}, u32[]{:S(2)}, u32[]{:S(2)}) async-start(bf16[16,64,128]{2,1,0:T(8,128)(2,1)} %bitcast), calls=%async_computation.1 | async-start | bytes 524288 | tf_op jit(solution)/shard_map/all_to_all | solution.py:315
  58.9 6.7 %collective-permute-start.11 = (bf16[128,1024]{1,0:T(8,128)(2,1)}, bf16[128,1024]{1,0:T(8,128)(2,1)}, u32[]{:S(2)}, u32[]{:S(2)}) collective-permute-start(bf16[128,1024]{1,0:T(8,128)(2,1)} %get-tuple-element.40.refs_0_), channel_id=1, source_target_pairs={{0,1},{1,0},{2,3},{3,2},{4,5},{5,4},{6,7},{7,6},{8,9},{9,8},{10,11... | collective-permute-start | bytes 786440 | tf_op jit(solution)/shard_map/ppermute | solution.py:289
  60.0 22.7 %all-to-all-start.2 = ((bf16[8,192,128]{2,1,0:T(8,128)(2,1)}), bf16[8,192,128]{2,1,0:T(8,128)(2,1)S(1)}, u32[]{:S(2)}, u32[]{:S(2)}) async-start(bf16[8,192,128]{2,1,0:T(8,128)(2,1)} %copy-done.1), calls=%async_computation.2 | async-start | bytes 786432 | tf_op jit(solution)/shard_map/all_to_all | solution.py:283
  67.3 7.3 %collective-permute-start.12 = (bf16[192,128]{1,0:T(8,128)(2,1)S(1)}, bf16[192,128]{1,0:T(8,128)(2,1)S(1)}, u32[]{:S(2)}, u32[]{:S(2)}) collective-permute-start(bf16[192,128]{1,0:T(8,128)(2,1)S(1)} %get-tuple-element.43), channel_id=1, source_target_pairs={{0,4},{2,6},{4,0},{6,2},{8,12},{10,14},{12,8},{14,10},{16,20},{18,... | collective-permute-start | bytes 147464 | tf_op jit(solution)/shard_map/ppermute | solution.py:298
  69.0 7.5 %collective-permute-start.13 = (bf16[192,128]{1,0:T(8,128)(2,1)S(1)}, bf16[192,128]{1,0:T(8,128)(2,1)S(1)}, u32[]{:S(2)}, u32[]{:S(2)}) collective-permute-start(bf16[192,128]{1,0:T(8,128)(2,1)S(1)} %get-tuple-element.44), channel_id=1, source_target_pairs={{0,8},{2,10},{4,12},{6,14},{8,0},{10,2},{12,4},{14,6},{16,24},{18,... | collective-permute-start | bytes 147464 | tf_op jit(solution)/shard_map/ppermute | solution.py:298
  69.0 7.6 %collective-permute-start.14 = (bf16[192,128]{1,0:T(8,128)(2,1)S(1)}, bf16[192,128]{1,0:T(8,128)(2,1)S(1)}, u32[]{:S(2)}, u32[]{:S(2)}) collective-permute-start(bf16[192,128]{1,0:T(8,128)(2,1)S(1)} %get-tuple-element.45), channel_id=1, source_target_pairs={{0,12},{2,14},{4,8},{6,10},{8,4},{10,6},{12,0},{14,2},{16,28},{18,... | collective-permute-start | bytes 147464 | tf_op jit(solution)/shard_map/ppermute | solution.py:298
  71.0 25.0 %collective-permute-start.21 = (bf16[512,1024]{1,0:T(8,128)(2,1)S(1)}, bf16[512,1024]{1,0:T(8,128)(2,1)S(1)}, u32[]{:S(2)}, u32[]{:S(2)}) collective-permute-start(bf16[512,1024]{1,0:T(8,128)(2,1)S(1)} %slice_bitcast_fusion.1.refs_2_), channel_id=1, source_target_pairs={{0,1},{1,0},{2,3},{3,2},{4,5},{5,4},{6,7},{7,6},{8,9},{9,8},{10,11... | collective-permute-start | bytes 3145736 | tf_op jit(solution)/shard_map/ppermute | solution.py:293
  72.1 7.7 %collective-permute-start.15 = (bf16[192,128]{1,0:T(8,128)(2,1)S(1)}, bf16[192,128]{1,0:T(8,128)(2,1)S(1)}, u32[]{:S(2)}, u32[]{:S(2)}) collective-permute-start(bf16[192,128]{1,0:T(8,128)(2,1)S(1)} %get-tuple-element.46), channel_id=1, source_target_pairs={{0,28},{2,30},{4,24},{6,26},{8,20},{10,22},{12,16},{14,18},{16,12}... | collective-permute-start | bytes 147464 | tf_op jit(solution)/shard_map/ppermute | solution.py:298
  74.7 5.9 %collective-permute-start.16 = (bf16[192,128]{1,0:T(8,128)(2,1)S(1)}, bf16[192,128]{1,0:T(8,128)(2,1)S(1)}, u32[]{:S(2)}, u32[]{:S(2)}) collective-permute-start(bf16[192,128]{1,0:T(8,128)(2,1)S(1)} %get-tuple-element.47), channel_id=1, source_target_pairs={{0,24},{2,26},{4,28},{6,30},{8,16},{10,18},{12,20},{14,22},{16,8},... | collective-permute-start | bytes 147464 | tf_op jit(solution)/shard_map/ppermute | solution.py:298
  76.4 6.1 %collective-permute-start.17 = (bf16[192,128]{1,0:T(8,128)(2,1)S(1)}, bf16[192,128]{1,0:T(8,128)(2,1)S(1)}, u32[]{:S(2)}, u32[]{:S(2)}) collective-permute-start(bf16[192,128]{1,0:T(8,128)(2,1)S(1)} %get-tuple-element.48), channel_id=1, source_target_pairs={{0,20},{2,22},{4,16},{6,18},{8,28},{10,30},{12,24},{14,26},{16,4},... | collective-permute-start | bytes 147464 | tf_op jit(solution)/shard_map/ppermute | solution.py:298
  76.6 6.0 %collective-permute-start.18 = (bf16[192,128]{1,0:T(8,128)(2,1)S(1)}, bf16[192,128]{1,0:T(8,128)(2,1)S(1)}, u32[]{:S(2)}, u32[]{:S(2)}) collective-permute-start(bf16[192,128]{1,0:T(8,128)(2,1)S(1)} %get-tuple-element.49), channel_id=1, source_target_pairs={{0,16},{2,18},{4,20},{6,22},{8,24},{10,26},{12,28},{14,30},{16,0},... | collective-permute-start | bytes 147464 | tf_op jit(solution)/shard_map/ppermute | solution.py:298
  82.7 2.3 %collective-permute-start.19 = (bf16[8,192,128]{2,1,0:T(8,128)(2,1)S(1)}, bf16[8,192,128]{2,1,0:T(8,128)(2,1)S(1)}, u32[]{:S(2)}, u32[]{:S(2)}) collective-permute-start(bf16[8,192,128]{2,1,0:T(8,128)(2,1)S(1)} %all-to-all-done.2.refs_1_), channel_id=1, source_target_pairs={{0,2},{2,0},{4,6},{6,4},{8,10},{10,8},{12,14},{14,12},{16,18},{18,... | collective-permute-start | bytes 1179656 | tf_op jit(solution)/shard_map/ppermute | solution.py:300
  90.8 15.3 %all-to-all-start.3 = ((bf16[16,64,128]{2,1,0:T(8,128)(2,1)}), bf16[16,64,128]{2,1,0:T(8,128)(2,1)S(1)}, u32[]{:S(2)}, u32[]{:S(2)}) async-start(bf16[16,64,128]{2,1,0:T(8,128)(2,1)} %bitcast.4), calls=%async_computation.3 | async-start | bytes 524288 | tf_op jit(solution)/shard_map/all_to_all | solution.py:315
  (8 other events, 61.4 us)

commit v5 on v4

--- a/solution.py
+++ b/solution.py
@@ -94,7 +94,7 @@
         views += [None] + [(layer, which) for which in range(3)]
         shapes += [(gain.shape, jnp.float32)] + [(project_in.shape[2:], jnp.bfloat16)] * (0 if keep else 3)
         shape, heads = (3 * HD, rows), columns // HD
-        outs += [pltpu.VMEM(shape if slots else (heads, *shape), jnp.bfloat16)] * (heads if slots else 1)
+        outs += [pltpu.VMEM(shape, jnp.bfloat16)] * heads if slots else [pltpu.HBM((heads, *shape), jnp.bfloat16)]
         if keep:
             outs.append(pltpu.VMEM(project_in.shape[1:], jnp.bfloat16))
         flops += 6 * rows * width * columns
@@ -147,7 +147,8 @@
 
 
 def slot_order(count):
-    return [*range(count // 2), *range(count - 1, count // 2 - 1, -1)]
+    half = count // 2
+    return [0, *range(half - 1, 0, -1), *range(count - 1, half - 1, -1)]
 
 
 def assemble(slots, place):

time: 109 us -> 109 us (level)
  waiting for transfers between devices: 31.4 us -> 30.2 us
  starting transfers between devices: 49.2 us -> 50.4 us
    ppermute x14, waiting for transfers between devices: 7.72 us -> 6.49 us  [per_device(): received[slot] = lax.ppermute(slots[slot], 'ctx', partners)]
where the time goes in v5:
time: 109 us; the launch traced here: 108 us
  starting transfers between devices  50.4 us (46%)
  waiting for transfers between devices  30.2 us (28%)
  Pallas kernels  24.2 us (22%)
  local copies, waits for them, and re-layouts  3.27 us (3%)
    ppermute x14, starting transfers between devices, per_device(): received[slot] = lax.ppermute(slots[slot], 'ctx', partners)  23.4 us
    all_to_all x2, waiting for transfers between devices, per_device(): lax.all_to_all(heads, ('ctx', 'head'), 0, 0, axis_index_groups=row_groups...  18.2 us
    pallas_call x5, Pallas kernels, rows_step(): pl.pallas_call(kernel, in_specs=[HBM if itself else VMEM] * count, out_sp...  12.5 us
    pallas_call x2, Pallas kernels, attention(): pl.pallas_call(kernel, in_specs=[VMEM] * (1 + len(own) + len(others)), ou...  11.6 us
    all_to_all x2, starting transfers between devices, per_device(): lax.all_to_all(heads, ('ctx', 'head'), 0, 0, axis_index_groups=row_groups...  10.6 us
    all_to_all x2, starting transfers between devices, to_heads(): lax.all_to_all(fields, 'ctx', 0, 0, axis_index_groups=shard_groups, tiled...  9.48 us
    ppermute x14, waiting for transfers between devices, per_device(): received[slot] = lax.ppermute(slots[slot], 'ctx', partners)  6.49 us
    ppermute x2, starting transfers between devices, per_device(): peer = lax.ppermute(residual, 'head', swap)  4.04 us
  transfers between devices with their start and end apart: 26, of which 12 were waited for; matrix products, arithmetic and copies ran while one was open for 3% of the time, Pallas kernels for 17%

profile of v5, /device:TPU:0, one launch (start us, length us, event | category | flops | bytes accessed | tf_op | source)
XLA Modules:
  0.0 108.2 jit_solution(14077242422429430122)
XLA Ops:
  0.0 2.9 %collective-permute-start = (bf16[128,1024]{1,0:T(8,128)(2,1)}, bf16[128,1024]{1,0:T(8,128)(2,1)}, u32[]{:S(2)}, u32[]{:S(2)}) collective-permute-start(bf16[128,1024]{1,0:T(8,128)(2,1)} %refs_0_.6), channel_id=1, source_target_pairs={{0,1},{1,0},{2,3},{3,2},{4,5},{5,4},{6,7},{7,6},{8,9},{9,8},{10,11... | collective-permute-start | bytes 786440 | tf_op jit(solution)/shard_map/ppermute | solution.py:290
  2.9 3.3 %shard_map.55 = (bf16[8,192,128]{2,1,0:T(8,128)(2,1)}, bf16[3,1024,512]{2,1,0:T(8,128)(2,1)S(1)}) custom-call(bf16[128,1024]{1,0:T(8,128)(2,1)} %refs_0_.6, f32[2,1024]{1,0:T(2,128)} %refs_1_.5, bf16[2,3,1024,512]{3,2,1,0:T(8,128)(2,1)} %refs_4_.2, bf16[2,3,1024,512]{3,2,1,0:T(8,128)(2,1)} %refs_4_.2, bf16[2,3,1024,512]{3,2,1,0:T(8,128)(2,1)} %refs_4_.2), custom_call_target="tpu_custom_call" | custom-call | flops 402653184 | bytes 3145728 | tf_op jit(solution)/shard_map/pallas_call | solution.py:138
  6.2 5.8 %all-to-all-start = ((bf16[8,192,128]{2,1,0:T(8,128)(2,1)}), bf16[8,192,128]{2,1,0:T(8,128)(2,1)S(1)}, u32[]{:S(2)}, u32[]{:S(2)}) async-start(bf16[8,192,128]{2,1,0:T(8,128)(2,1)} %get-tuple-element.28), calls=%async_computation | async-start | bytes 786432 | tf_op jit(solution)/shard_map/all_to_all | solution.py:284
  12.1 1.8 %shard_map.56 = (bf16[192,128]{1,0:T(8,128)(2,1)S(1)}, bf16[192,128]{1,0:T(8,128)(2,1)S(1)}, bf16[192,128]{1,0:T(8,128)(2,1)S(1)}, bf16[192,128]{1,0:T(8,128)(2,...) custom-call(bf16[128,1024]{1,0:T(8,128)(2,1)} %collective-permute-do, ...), custom_call_target="tpu_custom_call" | custom-call | flops 8053063680 | bytes 3145728 | tf_op jit(solution)/shard_map/pallas_call | solution.py:138
  14.0 3.0 %collective-permute-start.1 = (bf16[192,128]{1,0:T(8,128)(2,1)S(1)}, bf16[192,128]{1,0:T(8,128)(2,1)S(1)}, u32[]{:S(2)}, u32[]{:S(2)}) collective-permute-start(bf16[192,128]{1,0:T(8,128)(2,1)S(1)} %get-tuple-element.31), channel_id=1, source_target_pairs={{0,12},{2,14},{4,8},{6,10},{8,4},{10,6},{12,0},{14,2},{16,28},{18,... | collective-permute-start | bytes 147464 | tf_op jit(solution)/shard_map/ppermute | solution.py:299
  19.2 4.6 %collective-permute-start.4 = (bf16[192,128]{1,0:T(8,128)(2,1)S(1)}, bf16[192,128]{1,0:T(8,128)(2,1)S(1)}, u32[]{:S(2)}, u32[]{:S(2)}) collective-permute-start(bf16[192,128]{1,0:T(8,128)(2,1)S(1)} %get-tuple-element.34), channel_id=1, source_target_pairs={{0,28},{2,30},{4,24},{6,26},{8,20},{10,22},{12,16},{14,18},{16,12}... | collective-permute-start | bytes 147464 | tf_op jit(solution)/shard_map/ppermute | solution.py:299
  24.6 1.8 %collective-permute-start.6 = (bf16[192,128]{1,0:T(8,128)(2,1)S(1)}, bf16[192,128]{1,0:T(8,128)(2,1)S(1)}, u32[]{:S(2)}, u32[]{:S(2)}) collective-permute-start(bf16[192,128]{1,0:T(8,128)(2,1)S(1)} %get-tuple-element.36), channel_id=1, source_target_pairs={{0,20},{2,22},{4,16},{6,18},{8,28},{10,30},{12,24},{14,26},{16,4},... | collective-permute-start | bytes 147464 | tf_op jit(solution)/shard_map/ppermute | solution.py:299
  27.8 1.9 %collective-permute-done.5.refs_5_ = bf16[192,128]{1,0:T(8,128)(2,1)S(1)} collective-permute-done((bf16[192,128]{1,0:T(8,128)(2,1)S(1)}, bf16[192,128]{1,0:T(8,128)(2,1)S(1)}, u32[]{:S(2)}, u32[]{:S(2)}) %collective-permute-start.5) | collective-permute-done | bytes 49184 | tf_op jit(solution)/shard_map/ppermute | solution.py:299
  33.9 5.8 %shard_map.58 = bf16[2,8,64,128]{3,2,1,0:T(8,128)(2,1)} custom-call(f32[2,512]{1,0:T(2,128)S(1)} %copy-done.2, bf16[8,192,128]{2,1,0:T(8,128)(2,1)S(1)} %all-to-all-done.refs_1_, bf16[8,192,128]{2,1,0:T(8,128)(2,1)S(1)} %shard_map.57.refs_2_, bf16[8,192,128]{2,1,0:T(8,128)(2,1)S(1)} %collective-permute-done.8.refs_3_, ...), custom_call_target="tpu_custom_call" | custom-call | flops 1207959552 | bytes 2097152 | tf_op jit(solution)/shard_map/pallas_call | solution.py:241
  39.6 5.5 %all-to-all-start.1 = ((bf16[16,64,128]{2,1,0:T(8,128)(2,1)}), bf16[16,64,128]{2,1,0:T(8,128)(2,1)}, u32[]{:S(2)}, u32[]{:S(2)}) async-start(bf16[16,64,128]{2,1,0:T(8,128)(2,1)} %bitcast), calls=%async_computation.1 | async-start | bytes 524288 | tf_op jit(solution)/shard_map/all_to_all | solution.py:316
  45.1 2.1 %slice_bitcast_fusion.refs_5_.refs_2_ = bf16[3,1024,512]{2,1,0:T(8,128)(2,1)S(1)} fusion(bf16[2,3,1024,512]{3,2,1,0:T(8,128)(2,1)} %refs_4_.2), kind=kLoop, calls=%fused_computation | loop fusion | bytes 6291456 | tf_op jit(solution)/shard_map/squeeze | solution.py:314
  47.3 8.1 %all-to-all-done.1 = bf16[16,64,128]{2,1,0:T(8,128)(2,1)} async-done(((bf16[16,64,128]{2,1,0:T(8,128)(2,1)}), bf16[16,64,128]{2,1,0:T(8,128)(2,1)}, u32[]{:S(2)}, u32[]{:S(2)}) %all-to-all-start.1) | async-done | bytes 262176 | tf_op jit(solution)/shard_map/all_to_all | solution.py:316
  55.4 3.6 %shard_map.59 = (bf16[128,1024]{1,0:T(8,128)(2,1)}, bf16[8,192,128]{2,1,0:T(8,128)(2,1)}) custom-call(bf16[128,1024]{1,0:T(8,128)(2,1)S(1)} %copy-done, bf16[1024,128]{1,0:T(8,128)(2,1)} %bitcast.1.refs_1_, bf16[512,1024]{1,0:T(8,128)(2,1)} %slice_bitcast_fusion.2.refs_2_, bf16[512,1024]{1,0:T(8,128)(2,1)} %collective-permute-done.10.refs_3_, ...), custom_call_target="tpu_custom_call" | custom-call | flops 671088640 | bytes 5242880 | tf_op jit(solution)/shard_map/pallas_call | solution.py:138
  60.0 3.6 %all-to-all-start.2 = ((bf16[8,192,128]{2,1,0:T(8,128)(2,1)}), bf16[8,192,128]{2,1,0:T(8,128)(2,1)S(1)}, u32[]{:S(2)}, u32[]{:S(2)}) async-start(bf16[8,192,128]{2,1,0:T(8,128)(2,1)} %get-tuple-element.41), calls=%async_computation.2 | async-start | bytes 786432 | tf_op jit(solution)/shard_map/all_to_all | solution.py:284
  63.7 1.9 %collective-permute-done.11.refs_0_ = bf16[128,1024]{1,0:T(8,128)(2,1)} collective-permute-done((bf16[128,1024]{1,0:T(8,128)(2,1)}, bf16[128,1024]{1,0:T(8,128)(2,1)}, u32[]{:S(2)}, u32[]{:S(2)}) %collective-permute-start.11) | collective-permute-done | bytes 262176 | tf_op jit(solution)/shard_map/ppermute | solution.py:290
  68.4 2.0 %collective-permute-start.13 = (bf16[192,128]{1,0:T(8,128)(2,1)S(1)}, bf16[192,128]{1,0:T(8,128)(2,1)S(1)}, u32[]{:S(2)}, u32[]{:S(2)}) collective-permute-start(bf16[192,128]{1,0:T(8,128)(2,1)S(1)} %get-tuple-element.44), channel_id=1, source_target_pairs={{0,8},{2,10},{4,12},{6,14},{8,0},{10,2},{12,4},{14,6},{16,24},{18,... | collective-permute-start | bytes 147464 | tf_op jit(solution)/shard_map/ppermute | solution.py:299
  72.1 2.5 %collective-permute-start.15 = (bf16[192,128]{1,0:T(8,128)(2,1)S(1)}, bf16[192,128]{1,0:T(8,128)(2,1)S(1)}, u32[]{:S(2)}, u32[]{:S(2)}) collective-permute-start(bf16[192,128]{1,0:T(8,128)(2,1)S(1)} %get-tuple-element.46), channel_id=1, source_target_pairs={{0,28},{2,30},{4,24},{6,26},{8,20},{10,22},{12,16},{14,18},{16,12}... | collective-permute-start | bytes 147464 | tf_op jit(solution)/shard_map/ppermute | solution.py:299
  74.6 1.8 %collective-permute-start.16 = (bf16[192,128]{1,0:T(8,128)(2,1)S(1)}, bf16[192,128]{1,0:T(8,128)(2,1)S(1)}, u32[]{:S(2)}, u32[]{:S(2)}) collective-permute-start(bf16[192,128]{1,0:T(8,128)(2,1)S(1)} %get-tuple-element.47), channel_id=1, source_target_pairs={{0,24},{2,26},{4,28},{6,30},{8,16},{10,18},{12,20},{14,22},{16,8},... | collective-permute-start | bytes 147464 | tf_op jit(solution)/shard_map/ppermute | solution.py:299
  76.6 3.2 %collective-permute-start.18 = (bf16[192,128]{1,0:T(8,128)(2,1)S(1)}, bf16[192,128]{1,0:T(8,128)(2,1)S(1)}, u32[]{:S(2)}, u32[]{:S(2)}) collective-permute-start(bf16[192,128]{1,0:T(8,128)(2,1)S(1)} %get-tuple-element.49), channel_id=1, source_target_pairs={{0,16},{2,18},{4,20},{6,22},{8,24},{10,26},{12,28},{14,30},{16,0},... | collective-permute-start | bytes 147464 | tf_op jit(solution)/shard_map/ppermute | solution.py:299
  80.5 2.1 %collective-permute-done.17.refs_6_ = bf16[192,128]{1,0:T(8,128)(2,1)S(1)} collective-permute-done((bf16[192,128]{1,0:T(8,128)(2,1)S(1)}, bf16[192,128]{1,0:T(8,128)(2,1)S(1)}, u32[]{:S(2)}, u32[]{:S(2)}) %collective-permute-start.17) | collective-permute-done | bytes 49184 | tf_op jit(solution)/shard_map/ppermute | solution.py:299
  85.0 5.8 %shard_map.62 = bf16[2,8,64,128]{3,2,1,0:T(8,128)(2,1)} custom-call(f32[2,512]{1,0:T(2,128)S(1)} %copy-done.2, bf16[8,192,128]{2,1,0:T(8,128)(2,1)S(1)} %all-to-all-done.2.refs_1_, bf16[8,192,128]{2,1,0:T(8,128)(2,1)S(1)} %shard_map.61.refs_2_, bf16[8,192,128]{2,1,0:T(8,128)(2,1)S(1)} %collective-permute-done.19.refs_3_, ...), custom_call_target="tpu_custom_call" | custom-call | flops 1207959552 | bytes 2097152 | tf_op jit(solution)/shard_map/pallas_call | solution.py:241
  90.8 5.1 %all-to-all-start.3 = ((bf16[16,64,128]{2,1,0:T(8,128)(2,1)}), bf16[16,64,128]{2,1,0:T(8,128)(2,1)S(1)}, u32[]{:S(2)}, u32[]{:S(2)}) async-start(bf16[16,64,128]{2,1,0:T(8,128)(2,1)} %bitcast.4), calls=%async_computation.3 | async-start | bytes 524288 | tf_op jit(solution)/shard_map/all_to_all | solution.py:316
  95.9 10.2 %all-to-all-done.3 = bf16[16,64,128]{2,1,0:T(8,128)(2,1)S(1)} async-done(((bf16[16,64,128]{2,1,0:T(8,128)(2,1)}), bf16[16,64,128]{2,1,0:T(8,128)(2,1)S(1)}, u32[]{:S(2)}, u32[]{:S(2)}) %all-to-all-start.3) | async-done | bytes 262176 | tf_op jit(solution)/shard_map/all_to_all | solution.py:316
  106.1 2.1 %shard_map.63 = bf16[128,1024]{1,0:T(8,128)(2,1)} custom-call(bf16[128,1024]{1,0:T(8,128)(2,1)} %get-tuple-element.40.refs_0_, bf16[1024,128]{1,0:T(8,128)(2,1)S(1)} %bitcast.10, bf16[512,1024]{1,0:T(8,128)(2,1)S(1)} %slice_bitcast_fusion.1.refs_2_, bf16[512,1024]{1,0:T(8,128)(2,1)S(1)} %collective-permute-done.21.refs_3_), custom_call_target="tpu_custom_call" | custom-call | flops 268435456 | bytes 2097152 | tf_op jit(solution)/shard_map/pallas_call | solution.py:138
  (50 shorter events, 17.4 us)
Async XLA Ops:
  0.0 12.1 %collective-permute-start = (bf16[128,1024]{1,0:T(8,128)(2,1)}, bf16[128,1024]{1,0:T(8,128)(2,1)}, u32[]{:S(2)}, u32[]{:S(2)}) collective-permute-start(bf16[128,1024]{1,0:T(8,128)(2,1)} %refs_0_.6), channel_id=1, source_target_pairs={{0,1},{1,0},{2,3},{3,2},{4,5},{5,4},{6,7},{7,6},{8,9},{9,8},{10,11... | collective-permute-start | bytes 786440 | tf_op jit(solution)/shard_map/ppermute | solution.py:290
  6.2 25.4 %all-to-all-start = ((bf16[8,192,128]{2,1,0:T(8,128)(2,1)}), bf16[8,192,128]{2,1,0:T(8,128)(2,1)S(1)}, u32[]{:S(2)}, u32[]{:S(2)}) async-start(bf16[8,192,128]{2,1,0:T(8,128)(2,1)} %get-tuple-element.28), calls=%async_computation | async-start | bytes 786432 | tf_op jit(solution)/shard_map/all_to_all | solution.py:284
  14.0 9.9 %collective-permute-start.1 = (bf16[192,128]{1,0:T(8,128)(2,1)S(1)}, bf16[192,128]{1,0:T(8,128)(2,1)S(1)}, u32[]{:S(2)}, u32[]{:S(2)}) collective-permute-start(bf16[192,128]{1,0:T(8,128)(2,1)S(1)} %get-tuple-element.31), channel_id=1, source_target_pairs={{0,12},{2,14},{4,8},{6,10},{8,4},{10,6},{12,0},{14,2},{16,28},{18,... | collective-permute-start | bytes 147464 | tf_op jit(solution)/shard_map/ppermute | solution.py:299
  16.9 7.6 %collective-permute-start.2 = (bf16[192,128]{1,0:T(8,128)(2,1)S(1)}, bf16[192,128]{1,0:T(8,128)(2,1)S(1)}, u32[]{:S(2)}, u32[]{:S(2)}) collective-permute-start(bf16[192,128]{1,0:T(8,128)(2,1)S(1)} %get-tuple-element.32), channel_id=1, source_target_pairs={{0,8},{2,10},{4,12},{6,14},{8,0},{10,2},{12,4},{14,6},{16,24},{18,... | collective-permute-start | bytes 147464 | tf_op jit(solution)/shard_map/ppermute | solution.py:299
  17.5 8.9 %collective-permute-start.3 = (bf16[192,128]{1,0:T(8,128)(2,1)S(1)}, bf16[192,128]{1,0:T(8,128)(2,1)S(1)}, u32[]{:S(2)}, u32[]{:S(2)}) collective-permute-start(bf16[192,128]{1,0:T(8,128)(2,1)S(1)} %get-tuple-element.33), channel_id=1, source_target_pairs={{0,4},{2,6},{4,0},{6,2},{8,12},{10,14},{12,8},{14,10},{16,20},{18,... | collective-permute-start | bytes 147464 | tf_op jit(solution)/shard_map/ppermute | solution.py:299
  18.6 28.7 %collective-permute-start.10 = (bf16[512,1024]{1,0:T(8,128)(2,1)}, bf16[512,1024]{1,0:T(8,128)(2,1)}, u32[]{:S(2)}, u32[]{:S(2)}) collective-permute-start(bf16[512,1024]{1,0:T(8,128)(2,1)} %slice_bitcast_fusion.2.refs_2_), channel_id=1, source_target_pairs={{0,1},{1,0},{2,3},{3,2},{4,5},{5,4},{6,7},{7,6},{8,9},{9,8},{10,11... | collective-permute-start | bytes 3145736 | tf_op jit(solution)/shard_map/ppermute | solution.py:294
  19.2 8.6 %collective-permute-start.4 = (bf16[192,128]{1,0:T(8,128)(2,1)S(1)}, bf16[192,128]{1,0:T(8,128)(2,1)S(1)}, u32[]{:S(2)}, u32[]{:S(2)}) collective-permute-start(bf16[192,128]{1,0:T(8,128)(2,1)S(1)} %get-tuple-element.34), channel_id=1, source_target_pairs={{0,28},{2,30},{4,24},{6,26},{8,20},{10,22},{12,16},{14,18},{16,12}... | collective-permute-start | bytes 147464 | tf_op jit(solution)/shard_map/ppermute | solution.py:299
  23.8 5.9 %collective-permute-start.5 = (bf16[192,128]{1,0:T(8,128)(2,1)S(1)}, bf16[192,128]{1,0:T(8,128)(2,1)S(1)}, u32[]{:S(2)}, u32[]{:S(2)}) collective-permute-start(bf16[192,128]{1,0:T(8,128)(2,1)S(1)} %get-tuple-element.35), channel_id=1, source_target_pairs={{0,24},{2,26},{4,28},{6,30},{8,16},{10,18},{12,20},{14,22},{16,8},... | collective-permute-start | bytes 147464 | tf_op jit(solution)/shard_map/ppermute | solution.py:299
  24.6 6.6 %collective-permute-start.6 = (bf16[192,128]{1,0:T(8,128)(2,1)S(1)}, bf16[192,128]{1,0:T(8,128)(2,1)S(1)}, u32[]{:S(2)}, u32[]{:S(2)}) collective-permute-start(bf16[192,128]{1,0:T(8,128)(2,1)S(1)} %get-tuple-element.36), channel_id=1, source_target_pairs={{0,20},{2,22},{4,16},{6,18},{8,28},{10,30},{12,24},{14,26},{16,4},... | collective-permute-start | bytes 147464 | tf_op jit(solution)/shard_map/ppermute | solution.py:299
  26.4 5.0 %collective-permute-start.7 = (bf16[192,128]{1,0:T(8,128)(2,1)S(1)}, bf16[192,128]{1,0:T(8,128)(2,1)S(1)}, u32[]{:S(2)}, u32[]{:S(2)}) collective-permute-start(bf16[192,128]{1,0:T(8,128)(2,1)S(1)} %get-tuple-element.37), channel_id=1, source_target_pairs={{0,16},{2,18},{4,20},{6,22},{8,24},{10,26},{12,28},{14,30},{16,0},... | collective-permute-start | bytes 147464 | tf_op jit(solution)/shard_map/ppermute | solution.py:299
  31.6 2.3 %collective-permute-start.8 = (bf16[8,192,128]{2,1,0:T(8,128)(2,1)S(1)}, bf16[8,192,128]{2,1,0:T(8,128)(2,1)S(1)}, u32[]{:S(2)}, u32[]{:S(2)}) collective-permute-start(bf16[8,192,128]{2,1,0:T(8,128)(2,1)S(1)} %all-to-all-done.refs_1_), channel_id=1, source_target_pairs={{0,2},{2,0},{4,6},{6,4},{8,10},{10,8},{12,14},{14,12},{16,18},{18,... | collective-permute-start | bytes 1179656 | tf_op jit(solution)/shard_map/ppermute | solution.py:301
  39.6 15.7 %all-to-all-start.1 = ((bf16[16,64,128]{2,1,0:T(8,128)(2,1)}), bf16[16,64,128]{2,1,0:T(8,128)(2,1)}, u32[]{:S(2)}, u32[]{:S(2)}) async-start(bf16[16,64,128]{2,1,0:T(8,128)(2,1)} %bitcast), calls=%async_computation.1 | async-start | bytes 524288 | tf_op jit(solution)/shard_map/all_to_all | solution.py:316
  58.9 6.7 %collective-permute-start.11 = (bf16[128,1024]{1,0:T(8,128)(2,1)}, bf16[128,1024]{1,0:T(8,128)(2,1)}, u32[]{:S(2)}, u32[]{:S(2)}) collective-permute-start(bf16[128,1024]{1,0:T(8,128)(2,1)} %get-tuple-element.40.refs_0_), channel_id=1, source_target_pairs={{0,1},{1,0},{2,3},{3,2},{4,5},{5,4},{6,7},{7,6},{8,9},{9,8},{10,11... | collective-permute-start | bytes 786440 | tf_op jit(solution)/shard_map/ppermute | solution.py:290
  60.0 22.7 %all-to-all-start.2 = ((bf16[8,192,128]{2,1,0:T(8,128)(2,1)}), bf16[8,192,128]{2,1,0:T(8,128)(2,1)S(1)}, u32[]{:S(2)}, u32[]{:S(2)}) async-start(bf16[8,192,128]{2,1,0:T(8,128)(2,1)} %get-tuple-element.41), calls=%async_computation.2 | async-start | bytes 786432 | tf_op jit(solution)/shard_map/all_to_all | solution.py:284
  67.3 7.3 %collective-permute-start.12 = (bf16[192,128]{1,0:T(8,128)(2,1)S(1)}, bf16[192,128]{1,0:T(8,128)(2,1)S(1)}, u32[]{:S(2)}, u32[]{:S(2)}) collective-permute-start(bf16[192,128]{1,0:T(8,128)(2,1)S(1)} %get-tuple-element.43), channel_id=1, source_target_pairs={{0,12},{2,14},{4,8},{6,10},{8,4},{10,6},{12,0},{14,2},{16,28},{18,... | collective-permute-start | bytes 147464 | tf_op jit(solution)/shard_map/ppermute | solution.py:299
  68.4 8.0 %collective-permute-start.13 = (bf16[192,128]{1,0:T(8,128)(2,1)S(1)}, bf16[192,128]{1,0:T(8,128)(2,1)S(1)}, u32[]{:S(2)}, u32[]{:S(2)}) collective-permute-start(bf16[192,128]{1,0:T(8,128)(2,1)S(1)} %get-tuple-element.44), channel_id=1, source_target_pairs={{0,8},{2,10},{4,12},{6,14},{8,0},{10,2},{12,4},{14,6},{16,24},{18,... | collective-permute-start | bytes 147464 | tf_op jit(solution)/shard_map/ppermute | solution.py:299
  70.4 6.2 %collective-permute-start.14 = (bf16[192,128]{1,0:T(8,128)(2,1)S(1)}, bf16[192,128]{1,0:T(8,128)(2,1)S(1)}, u32[]{:S(2)}, u32[]{:S(2)}) collective-permute-start(bf16[192,128]{1,0:T(8,128)(2,1)S(1)} %get-tuple-element.45), channel_id=1, source_target_pairs={{0,4},{2,6},{4,0},{6,2},{8,12},{10,14},{12,8},{14,10},{16,20},{18,... | collective-permute-start | bytes 147464 | tf_op jit(solution)/shard_map/ppermute | solution.py:299
  71.0 25.0 %collective-permute-start.21 = (bf16[512,1024]{1,0:T(8,128)(2,1)S(1)}, bf16[512,1024]{1,0:T(8,128)(2,1)S(1)}, u32[]{:S(2)}, u32[]{:S(2)}) collective-permute-start(bf16[512,1024]{1,0:T(8,128)(2,1)S(1)} %slice_bitcast_fusion.1.refs_2_), channel_id=1, source_target_pairs={{0,1},{1,0},{2,3},{3,2},{4,5},{5,4},{6,7},{7,6},{8,9},{9,8},{10,11... | collective-permute-start | bytes 3145736 | tf_op jit(solution)/shard_map/ppermute | solution.py:294
  72.1 7.7 %collective-permute-start.15 = (bf16[192,128]{1,0:T(8,128)(2,1)S(1)}, bf16[192,128]{1,0:T(8,128)(2,1)S(1)}, u32[]{:S(2)}, u32[]{:S(2)}) collective-permute-start(bf16[192,128]{1,0:T(8,128)(2,1)S(1)} %get-tuple-element.46), channel_id=1, source_target_pairs={{0,28},{2,30},{4,24},{6,26},{8,20},{10,22},{12,16},{14,18},{16,12}... | collective-permute-start | bytes 147464 | tf_op jit(solution)/shard_map/ppermute | solution.py:299
  74.6 5.9 %collective-permute-start.16 = (bf16[192,128]{1,0:T(8,128)(2,1)S(1)}, bf16[192,128]{1,0:T(8,128)(2,1)S(1)}, u32[]{:S(2)}, u32[]{:S(2)}) collective-permute-start(bf16[192,128]{1,0:T(8,128)(2,1)S(1)} %get-tuple-element.47), channel_id=1, source_target_pairs={{0,24},{2,26},{4,28},{6,30},{8,16},{10,18},{12,20},{14,22},{16,8},... | collective-permute-start | bytes 147464 | tf_op jit(solution)/shard_map/ppermute | solution.py:299
  76.4 6.2 %collective-permute-start.17 = (bf16[192,128]{1,0:T(8,128)(2,1)S(1)}, bf16[192,128]{1,0:T(8,128)(2,1)S(1)}, u32[]{:S(2)}, u32[]{:S(2)}) collective-permute-start(bf16[192,128]{1,0:T(8,128)(2,1)S(1)} %get-tuple-element.48), channel_id=1, source_target_pairs={{0,20},{2,22},{4,16},{6,18},{8,28},{10,30},{12,24},{14,26},{16,4},... | collective-permute-start | bytes 147464 | tf_op jit(solution)/shard_map/ppermute | solution.py:299
  76.6 6.0 %collective-permute-start.18 = (bf16[192,128]{1,0:T(8,128)(2,1)S(1)}, bf16[192,128]{1,0:T(8,128)(2,1)S(1)}, u32[]{:S(2)}, u32[]{:S(2)}) collective-permute-start(bf16[192,128]{1,0:T(8,128)(2,1)S(1)} %get-tuple-element.49), channel_id=1, source_target_pairs={{0,16},{2,18},{4,20},{6,22},{8,24},{10,26},{12,28},{14,30},{16,0},... | collective-permute-start | bytes 147464 | tf_op jit(solution)/shard_map/ppermute | solution.py:299
  82.7 2.3 %collective-permute-start.19 = (bf16[8,192,128]{2,1,0:T(8,128)(2,1)S(1)}, bf16[8,192,128]{2,1,0:T(8,128)(2,1)S(1)}, u32[]{:S(2)}, u32[]{:S(2)}) collective-permute-start(bf16[8,192,128]{2,1,0:T(8,128)(2,1)S(1)} %all-to-all-done.2.refs_1_), channel_id=1, source_target_pairs={{0,2},{2,0},{4,6},{6,4},{8,10},{10,8},{12,14},{14,12},{16,18},{18,... | collective-permute-start | bytes 1179656 | tf_op jit(solution)/shard_map/ppermute | solution.py:301
  90.8 15.3 %all-to-all-start.3 = ((bf16[16,64,128]{2,1,0:T(8,128)(2,1)}), bf16[16,64,128]{2,1,0:T(8,128)(2,1)S(1)}, u32[]{:S(2)}, u32[]{:S(2)}) async-start(bf16[16,64,128]{2,1,0:T(8,128)(2,1)} %bitcast.4), calls=%async_computation.3 | async-start | bytes 524288 | tf_op jit(solution)/shard_map/all_to_all | solution.py:316
  (7 other events, 60.4 us)
